TPU v7x, 32 devices: a whole 2x2x4 slice. The times are simulated.
32 devices in a mesh: rep: 16 (over z, y, core), shard: 2 (over x).
Axes of the slice: x: 2, y: 2, z: 4, core: 2. Of those that a mesh axis runs over, the one named last changes fastest.
Arguments:
- tokens: bfloat16 [32, 1024, 960], P(('rep', 'shard')), may hold values from -6 to 6
- segments: int32 [32, 1024], P(('rep', 'shard')), may hold values from 0 to 3, never falling along the last dimension, each value on 1 to 800 neighbouring positions
- gain_attn: bfloat16 [960], P('shard'), may hold values from 0.5 to 1.5
- w_query: bfloat16 [960, 960], P('shard'), may hold values from -0.1875 to 0.1875
- key_weight_matrix: bfloat16 [960, 320], P('shard'), may hold values from -0.1875 to 0.1875
- value_weight_matrix: bfloat16 [960, 320], P('shard'), may hold values from -0.1875 to 0.1875
- w_out: bfloat16 [960, 960], P('shard'), may hold values from -1.5 to 1.5
- gain_mlp: bfloat16 [960], P('shard'), may hold values from 0.5 to 1.5
- w_gate: bfloat16 [960, 2560], P('shard'), may hold values from -0.1875 to 0.1875
- w_up: bfloat16 [960, 2560], P('shard'), may hold values from -0.1875 to 0.1875
- w_down: bfloat16 [2560, 960], P('shard'), may hold values from -0.125 to 0.125
- cotangent: bfloat16 [32, 1024, 960], P(('rep', 'shard')), may hold values from -6 to 6
Outputs:
- mixed: bfloat16 [32, 1024, 960], P(('rep', 'shard'))
- grad_tokens: bfloat16 [32, 1024, 960], P(('rep', 'shard'))
- grad_gain_attn: float32 [960], P('shard')
- grad_query: float32 [960, 960], P('shard')
- grad_key: float32 [960, 320], P('shard')
- grad_value: float32 [960, 320], P('shard')
- grad_out: float32 [960, 960], P('shard')
- grad_gain_mlp: float32 [960], P('shard')
- grad_gate: float32 [960, 2560], P('shard')
- grad_up: float32 [960, 2560], P('shard')
- grad_down: float32 [2560, 960], P('shard')
Inputs may be any that keep to these rules, and one draw needn't show every extreme that they name: `segments`: in each sequence the numbers never fall; each document spans 1 to 800 tokens, and some document spans exactly 800.
All inputs are finite; a program needn't handle non-finite values.
Results may differ from a plain program's by a relative error of at most 0.022.
Values may be sent and summed in bfloat16 or wider, within the bound.
No kernel may reach another device: no remote copies, remote signals or barrier semaphores. Data moves between devices by JAX's collectives and lax.ppermute only.
A program may use at most 320 MiB of HBM per device.

v0:
```python
from functools import partial

import jax
import jax.numpy as jnp
from jax import lax
from jax.sharding import PartitionSpec as P

QUERY_HEADS = 15
KEY_VALUE_HEADS = 5
HEAD_SIZE = 64


EPS = 1e-05
NEGATIVE = -1e30


def angles(documents, head_dim):
    segment_length = documents.shape[0]
    places = jnp.arange(segment_length, dtype=jnp.int32)
    begins = jnp.concatenate([jnp.ones((1,), dtype=jnp.bool_), documents[1:] != documents[:-1]])
    starting = lax.cummax(jnp.where(begins, places, 0), axis=0)
    offsets = (places - starting).astype(jnp.float32)
    rates = 10000.0 ** (-2.0 * jnp.arange(head_dim // 2).astype(jnp.float32) / head_dim)
    phases = offsets[:, None] * rates[None, :]
    return (jnp.cos(phases)[:, None, :], jnp.sin(phases)[:, None, :])


def apply_rotary(value_vectors, cosine_table, sine_table):
    halfway = value_vectors.shape[-1] // 2
    leading = value_vectors[..., :halfway]
    trailing = value_vectors[..., halfway:]
    return jnp.concatenate(
        [
            leading * cosine_table - trailing * sine_table,
            trailing * cosine_table + leading * sine_table,
        ],
        axis=-1,
    )


def invert_rotary(value_vectors, cosine_table, sine_table):
    halfway = value_vectors.shape[-1] // 2
    leading = value_vectors[..., :halfway]
    trailing = value_vectors[..., halfway:]
    return jnp.concatenate(
        [
            leading * cosine_table + trailing * sine_table,
            trailing * cosine_table - leading * sine_table,
        ],
        axis=-1,
    )


def masked_scores(query_block, key_vectors, documents, offset):
    block_count = query_block.shape[0]
    scores = jnp.einsum(
        "qgrd,kgd->grqk", query_block, key_vectors, preferred_element_type=jnp.float32
    ) * key_vectors.shape[-1] ** (-0.5)
    query_rows = offset + jnp.arange(block_count, dtype=jnp.int32)
    key_rows = jnp.arange(key_vectors.shape[0], dtype=jnp.int32)
    query_docs = documents[offset : offset + block_count]
    allowed = (query_docs[:, None] == documents[None, :]) & (
        key_rows[None, :] <= query_rows[:, None]
    )
    return jnp.where(allowed, scores, NEGATIVE)


def attend_forward(pieces):
    query_vectors, key_vectors, value_vectors, documents = pieces
    segment_length = query_vectors.shape[0]
    block_slice = min(512, segment_length)
    outputs = []
    totals = []
    for offset in range(0, segment_length, block_slice):
        scores = masked_scores(
            query_vectors[offset : offset + block_slice], key_vectors, documents, offset
        )
        highest = jnp.max(scores, axis=-1, keepdims=True)
        exponents = jnp.exp(scores - highest)
        summed = jnp.sum(exponents, axis=-1, keepdims=True)
        probs = (exponents / summed).astype(jnp.bfloat16)
        outputs.append(
            jnp.einsum("grqk,kgd->qgrd", probs, value_vectors, preferred_element_type=jnp.float32)
        )
        totals.append(highest[..., 0] + jnp.log(summed[..., 0]))
    return (jnp.concatenate(outputs, axis=0), jnp.concatenate(totals, axis=-1))


def attend_backward(pieces):
    query_vectors, key_vectors, value_vectors, documents, upstream, totals = pieces
    segment_length = query_vectors.shape[0]
    block_slice = min(512, segment_length)
    scaling = key_vectors.shape[-1] ** (-0.5)
    key_grad = jnp.zeros(key_vectors.shape, jnp.float32)
    value_grad = jnp.zeros(value_vectors.shape, jnp.float32)
    query_grads = []
    for offset in range(0, segment_length, block_slice):
        query_block = query_vectors[offset : offset + block_slice]
        upstream_block = upstream[offset : offset + block_slice]
        scores = masked_scores(query_block, key_vectors, documents, offset)
        probs = jnp.exp(scores - totals[..., offset : offset + block_slice, None])
        probs_grad = jnp.einsum(
            "qgrd,kgd->grqk", upstream_block, value_vectors, preferred_element_type=jnp.float32
        )
        inner = jnp.sum(probs * probs_grad, axis=-1, keepdims=True)
        score_grad = (probs * (probs_grad - inner)).astype(jnp.bfloat16)
        query_grads.append(
            jnp.einsum(
                "grqk,kgd->qgrd", score_grad, key_vectors, preferred_element_type=jnp.float32
            )
            * scaling
        )
        key_grad = (
            key_grad
            + jnp.einsum(
                "grqk,qgrd->kgd", score_grad, query_block, preferred_element_type=jnp.float32
            )
            * scaling
        )
        value_grad = value_grad + jnp.einsum(
            "grqk,qgrd->kgd",
            probs.astype(jnp.bfloat16),
            upstream_block,
            preferred_element_type=jnp.float32,
        )
    return (jnp.concatenate(query_grads, axis=0), key_grad, value_grad)


def product(left, right):
    return jnp.dot(left, right, preferred_element_type=jnp.float32)


def norm_backward(grad_in, normed, inverse, gain):
    weighted = grad_in * gain
    return inverse * (weighted - normed * jnp.mean(weighted * normed, axis=-1, keepdims=True))


def per_device(
    tokens,
    segments,
    gain_attn,
    w_query,
    key_weight_matrix,
    value_weight_matrix,
    w_out,
    gain_mlp,
    w_gate,
    w_up,
    w_down,
    cotangent,
):
    packed_sequences, segment_length, width = tokens.shape
    row_total_count = packed_sequences * segment_length
    head_groups = QUERY_HEADS // KEY_VALUE_HEADS
    attn_set = (
        lax.all_gather(gain_attn, "shard", axis=0, tiled=True),
        lax.all_gather(w_query, "shard", axis=0, tiled=True),
        lax.all_gather(key_weight_matrix, "shard", axis=0, tiled=True),
        lax.all_gather(value_weight_matrix, "shard", axis=0, tiled=True),
        lax.all_gather(w_out, "shard", axis=0, tiled=True),
    )
    mlp_set = (
        lax.all_gather(gain_mlp, "shard", axis=0, tiled=True),
        lax.all_gather(w_gate, "shard", axis=0, tiled=True),
        lax.all_gather(w_up, "shard", axis=0, tiled=True),
        lax.all_gather(w_down, "shard", axis=0, tiled=True),
    )
    cosine_table, sine_table = jax.vmap(partial(angles, head_dim=HEAD_SIZE))(segments)
    norm_one = attn_set[0].astype(jnp.float32)
    inputs_flat = tokens.reshape(row_total_count, width).astype(jnp.float32)
    inverse_one = lax.rsqrt(jnp.mean(inputs_flat * inputs_flat, axis=-1, keepdims=True) + EPS)
    normed_one = inputs_flat * inverse_one
    attn_in = (normed_one * norm_one).astype(jnp.bfloat16)
    query_pre = product(attn_in, attn_set[1])
    key_before_rotation = product(attn_in, attn_set[2])
    value_before_heads = product(attn_in, attn_set[3])
    query_vectors = (
        apply_rotary(
            query_pre.reshape(packed_sequences, segment_length, QUERY_HEADS, HEAD_SIZE),
            cosine_table,
            sine_table,
        )
        .astype(jnp.bfloat16)
        .reshape(packed_sequences, segment_length, KEY_VALUE_HEADS, head_groups, HEAD_SIZE)
    )
    key_vectors = apply_rotary(
        key_before_rotation.reshape(packed_sequences, segment_length, KEY_VALUE_HEADS, HEAD_SIZE),
        cosine_table,
        sine_table,
    ).astype(jnp.bfloat16)
    value_vectors = value_before_heads.reshape(
        packed_sequences, segment_length, KEY_VALUE_HEADS, HEAD_SIZE
    ).astype(jnp.bfloat16)
    attended, totals = lax.map(
        attend_forward, (query_vectors, key_vectors, value_vectors, segments)
    )
    heads = attended.reshape(row_total_count, QUERY_HEADS * HEAD_SIZE).astype(jnp.bfloat16)
    middle = inputs_flat + product(heads, attn_set[4])
    norm_two = mlp_set[0].astype(jnp.float32)
    inverse_two = lax.rsqrt(jnp.mean(middle * middle, axis=-1, keepdims=True) + EPS)
    normed_two = middle * inverse_two
    mlp_in = (normed_two * norm_two).astype(jnp.bfloat16)
    gate_pre = product(mlp_in, mlp_set[1])
    up_pre = product(mlp_in, mlp_set[2])
    activated = jax.nn.silu(gate_pre)
    hidden = (activated * up_pre).astype(jnp.bfloat16)
    result = middle + product(hidden, mlp_set[3])
    mixed = result.astype(jnp.bfloat16).reshape(packed_sequences, segment_length, width)
    mlp_back = (
        lax.all_gather(gain_mlp, "shard", axis=0, tiled=True),
        lax.all_gather(w_gate, "shard", axis=0, tiled=True),
        lax.all_gather(w_up, "shard", axis=0, tiled=True),
        lax.all_gather(w_down, "shard", axis=0, tiled=True),
    )
    attn_back = (
        lax.all_gather(gain_attn, "shard", axis=0, tiled=True),
        lax.all_gather(w_query, "shard", axis=0, tiled=True),
        lax.all_gather(key_weight_matrix, "shard", axis=0, tiled=True),
        lax.all_gather(value_weight_matrix, "shard", axis=0, tiled=True),
        lax.all_gather(w_out, "shard", axis=0, tiled=True),
    )
    out_grad = cotangent.reshape(row_total_count, width)
    grad_down = product(hidden.T, out_grad)
    hidden_grad = product(out_grad, mlp_back[3].T)
    sigmoid_gate = jax.nn.sigmoid(gate_pre)
    gate_grad = (
        hidden_grad * up_pre * sigmoid_gate * (1.0 + gate_pre * (1.0 - sigmoid_gate))
    ).astype(jnp.bfloat16)
    up_grad = (hidden_grad * activated).astype(jnp.bfloat16)
    grad_gate = product(mlp_in.T, gate_grad)
    grad_up = product(mlp_in.T, up_grad)
    mlp_in_grad = product(gate_grad, mlp_back[1].T) + product(up_grad, mlp_back[2].T)
    grad_norm_two = jnp.sum(mlp_in_grad * normed_two, axis=0)
    middle_grad = out_grad.astype(jnp.float32) + norm_backward(
        mlp_in_grad, normed_two, inverse_two, mlp_back[0].astype(jnp.float32)
    )
    mlp_grads = (
        lax.psum_scatter(
            grad_norm_two.astype(jnp.bfloat16), "shard", scatter_dimension=0, tiled=True
        ).astype(jnp.float32),
        lax.psum_scatter(
            grad_gate.astype(jnp.bfloat16), "shard", scatter_dimension=0, tiled=True
        ).astype(jnp.float32),
        lax.psum_scatter(
            grad_up.astype(jnp.bfloat16), "shard", scatter_dimension=0, tiled=True
        ).astype(jnp.float32),
        lax.psum_scatter(
            grad_down.astype(jnp.bfloat16), "shard", scatter_dimension=0, tiled=True
        ).astype(jnp.float32),
    )
    mlp_grads = (
        lax.psum(mlp_grads[0].astype(jnp.bfloat16), "rep").astype(jnp.float32),
        lax.psum(mlp_grads[1].astype(jnp.bfloat16), "rep").astype(jnp.float32),
        lax.psum(mlp_grads[2].astype(jnp.bfloat16), "rep").astype(jnp.float32),
        lax.psum(mlp_grads[3].astype(jnp.bfloat16), "rep").astype(jnp.float32),
    )
    branch_grad = middle_grad.astype(jnp.bfloat16)
    grad_out = product(heads.T, branch_grad)
    heads_grad = (
        product(branch_grad, attn_back[4].T)
        .astype(jnp.bfloat16)
        .reshape(packed_sequences, segment_length, KEY_VALUE_HEADS, head_groups, HEAD_SIZE)
    )
    queries_grad, key_vectors_gradient, value_vectors_gradient = lax.map(
        attend_backward, (query_vectors, key_vectors, value_vectors, segments, heads_grad, totals)
    )
    query_back = (
        invert_rotary(
            queries_grad.reshape(packed_sequences, segment_length, QUERY_HEADS, HEAD_SIZE),
            cosine_table,
            sine_table,
        )
        .reshape(row_total_count, QUERY_HEADS * HEAD_SIZE)
        .astype(jnp.bfloat16)
    )
    key_backward_rows = (
        invert_rotary(key_vectors_gradient, cosine_table, sine_table)
        .reshape(row_total_count, KEY_VALUE_HEADS * HEAD_SIZE)
        .astype(jnp.bfloat16)
    )
    value_backward_rows = value_vectors_gradient.reshape(
        row_total_count, KEY_VALUE_HEADS * HEAD_SIZE
    ).astype(jnp.bfloat16)
    grad_query = product(attn_in.T, query_back)
    grad_key = product(attn_in.T, key_backward_rows)
    grad_value = product(attn_in.T, value_backward_rows)
    attn_in_grad = (
        product(query_back, attn_back[1].T)
        + product(key_backward_rows, attn_back[2].T)
        + product(value_backward_rows, attn_back[3].T)
    )
    grad_norm_one = jnp.sum(attn_in_grad * normed_one, axis=0)
    input_grad = middle_grad + norm_backward(
        attn_in_grad, normed_one, inverse_one, attn_back[0].astype(jnp.float32)
    )
    grad_tokens = input_grad.astype(jnp.bfloat16).reshape(packed_sequences, segment_length, width)
    attn_grads = (
        lax.psum_scatter(
            grad_norm_one.astype(jnp.bfloat16), "shard", scatter_dimension=0, tiled=True
        ).astype(jnp.float32),
        lax.psum_scatter(
            grad_query.astype(jnp.bfloat16), "shard", scatter_dimension=0, tiled=True
        ).astype(jnp.float32),
        lax.psum_scatter(
            grad_key.astype(jnp.bfloat16), "shard", scatter_dimension=0, tiled=True
        ).astype(jnp.float32),
        lax.psum_scatter(
            grad_value.astype(jnp.bfloat16), "shard", scatter_dimension=0, tiled=True
        ).astype(jnp.float32),
        lax.psum_scatter(
            grad_out.astype(jnp.bfloat16), "shard", scatter_dimension=0, tiled=True
        ).astype(jnp.float32),
    )
    attn_grads = (
        lax.psum(attn_grads[0].astype(jnp.bfloat16), "rep").astype(jnp.float32),
        lax.psum(attn_grads[1].astype(jnp.bfloat16), "rep").astype(jnp.float32),
        lax.psum(attn_grads[2].astype(jnp.bfloat16), "rep").astype(jnp.float32),
        lax.psum(attn_grads[3].astype(jnp.bfloat16), "rep").astype(jnp.float32),
        lax.psum(attn_grads[4].astype(jnp.bfloat16), "rep").astype(jnp.float32),
    )
    finals = attn_grads + mlp_grads
    return (
        mixed,
        grad_tokens,
        finals[0],
        finals[1],
        finals[2],
        finals[3],
        finals[4],
        finals[5],
        finals[6],
        finals[7],
        finals[8],
    )


def solution(mesh):
    placed = (
        P(("rep", "shard"), None, None),
        P(("rep", "shard"), None),
        P("shard"),
        P("shard", None),
        P("shard", None),
        P("shard", None),
        P("shard", None),
        P("shard"),
        P("shard", None),
        P("shard", None),
        P("shard", None),
        P(("rep", "shard"), None, None),
    )
    return jax.shard_map(
        per_device,
        mesh=mesh,
        in_specs=placed,
        out_specs=(
            P(("rep", "shard"), None, None),
            P(("rep", "shard"), None, None),
            P("shard"),
            P("shard", None),
            P("shard", None),
            P("shard", None),
            P("shard", None),
            P("shard"),
            P("shard", None),
            P("shard", None),
            P("shard", None),
        ),
        check_vma=False,
    )
```

profile of v0, /device:TPU:0, one launch (start us, length us, event | category | flops | bytes accessed | tf_op | source)
XLA Modules:
  0.0 993.5 jit_solution(10147667121517703900)
XLA Ops:
  12.6 5.8 all-reduce.7
  19.7 17.0 %all-gather.1 = bf16[2,480,320]{1,2,0:T(8,128)(2,1)S(1)} all-gather(bf16[1,480,320]{1,2,0:T(8,128)(2,1)S(1)} %bitcast.261), channel_id=1, replica_groups=mesh['rep'=16,'shard'=2] {'shard'}, dimensions={0}, use_global_device_ids=true | all-gather | bytes 921600 | tf_op jit(solution)/shard_map/all_gather | solution.py:158
  38.1 17.9 %all-gather = bf16[2,480,320]{1,2,0:T(8,128)(2,1)S(1)} all-gather(bf16[1,480,320]{1,2,0:T(8,128)(2,1)} %bitcast.262), channel_id=1, replica_groups=mesh['rep'=16,'shard'=2] {'shard'}, dimensions={0}, use_global_device_ids=true | all-gather | bytes 921600 | tf_op jit(solution)/shard_map/all_gather | solution.py:159
  55.9 1.5 copy.43
  57.4 2.8 reshape.470
  60.2 1.8 fusion.86
  65.1 4.0 copy.45
  69.1 3.9 convolution_bitcast_fusion
  74.0 12.7 %fusion.105 = (f32[5,3,512]{2,1,0:T(4,128)S(1)}, f32[5,3,512,1024]{2,3,1,0:T(8,128)}) fusion(bf16[512,5,3,64]{0,3,2,1:T(8,128)(2,1)S(1)} %bitcast.243, bf16[1024,5,32]{0,2,1:T(8,128)(2,1)S(1)} %copy-done.11, bf16[1024,5,32]{0,2,1:T(8,128)(2,1)S(1)} %get-tuple-element.92, pred[512,1024]{0,1:T(8,128)(4,1)S(1)} %get-tuple-element.97), kind=kOutput, calls=%fused_computation.147 | convolution fusion | flops 1031528960 | bytes 33650688 | tf_op jit(solution)/shard_map/while/body/eval_jaxpr/qgrd,kgd->grqk/dot_general | solution.py:56
  86.7 12.9 %fusion.7 = f32[5,3,512]{2,1,0:T(4,128)S(1)} fusion(f32[5,3,512,1024]{2,3,1,0:T(8,128)} %get-tuple-element.103, f32[5,3,512]{2,1,0:T(4,128)S(1)} %get-tuple-element.102), kind=kLoop, calls=%fused_computation.19 | loop fusion | flops 15720960 | bytes 31518720 | tf_op jit(solution)/shard_map/while/body/eval_jaxpr/reduce_sum | solution.py:80
  99.7 15.0 %fusion.82 = bf16[512,5,3,64]{0,3,2,1:T(8,128)(2,1)S(1)} fusion(bf16[1024,5,64,1]{0,2,3,1:T(8,128)(2,1)S(1)} %copy-done.19, f32[5,3,512,1024]{2,3,1,0:T(8,128)} %get-tuple-element.103, f32[5,3,512]{2,1,0:T(4,128)S(1)} %fusion.7, f32[5,3,512]{2,1,0:T(4,128)S(1)} %get-tuple-element.102), kind=kOutput, calls=%fused_computation.109 | convolution fusion | flops 1030717440 | bytes 33157120 | tf_op jit(solution)/shard_map/while/body/eval_jaxpr/grqk,kgd->qgrd/dot_general | solution.py:83
  114.6 12.7 %fusion.106 = (f32[5,3,512]{2,1,0:T(4,128)S(1)}, f32[5,3,512,1024]{2,3,1,0:T(8,128)}) fusion(bf16[512,5,3,64]{0,3,2,1:T(8,128)(2,1)S(1)} %bitcast.241, bf16[1024,5,32]{0,2,1:T(8,128)(2,1)S(1)} %copy-done.11, bf16[1024,5,32]{0,2,1:T(8,128)(2,1)S(1)} %get-tuple-element.92, pred[512,1024]{0,1:T(8,128)(4,1)S(1)} %get-tuple-element.96), kind=kOutput, calls=%fused_computation.148 | convolution fusion | flops 1031528960 | bytes 33650688 | tf_op jit(solution)/shard_map/while/body/eval_jaxpr/qgrd,kgd->grqk/dot_general | solution.py:56
  127.3 12.8 %fusion.6 = f32[5,3,512]{2,1,0:T(4,128)S(1)} fusion(f32[5,3,512,1024]{2,3,1,0:T(8,128)} %get-tuple-element.105, f32[5,3,512]{2,1,0:T(4,128)S(1)} %get-tuple-element.104), kind=kLoop, calls=%fused_computation.18 | loop fusion | flops 15720960 | bytes 31518720 | tf_op jit(solution)/shard_map/while/body/eval_jaxpr/reduce_sum | solution.py:80
  140.1 12.9 %fusion.81 = bf16[512,5,3,64]{0,3,2,1:T(8,128)(2,1)S(1)} fusion(bf16[1024,5,64,1]{0,2,3,1:T(8,128)(2,1)S(1)} %copy-done.19, f32[5,3,512,1024]{2,3,1,0:T(8,128)} %get-tuple-element.105, f32[5,3,512]{2,1,0:T(4,128)S(1)} %fusion.6, f32[5,3,512]{2,1,0:T(4,128)S(1)} %get-tuple-element.104), kind=kOutput, calls=%fused_computation.108 | convolution fusion | flops 1030717440 | bytes 33157120 | tf_op jit(solution)/shard_map/while/body/eval_jaxpr/grqk,kgd->qgrd/dot_general | solution.py:83
  153.0 1.5 pad_maximum_fusion.1
  154.5 4.6 multiply_reduce_fusion.2
  159.1 1.9 copy-done.1
  161.0 1.7 multiply_convert_fusion.3
  162.7 10.9 %fusion.108 = f32[1024,2560]{1,0:T(8,128)} fusion(bf16[1024,960]{0,1:T(8,128)(2,1)} %multiply_convert_fusion.3, bf16[960,2560]{1,0:T(8,128)(2,1)} %all-gather.14.cloned.1.call-done), kind=kOutput, calls=%fused_computation.150 | convolution fusion | flops 5033164800 | bytes 17367040 | tf_op jit(solution)/shard_map/dot_general | solution.py:130
  173.6 50.4 %all-gather.12.cloned.1.call-done = bf16[960,2560]{1,0:T(8,128)(2,1)} async-done(((bf16[480,2560]{1,0:T(8,128)(2,1)}), bf16[960,2560]{1,0:T(8,128)(2,1)}) %all-gather.12.cloned.1.call-update) | async-done | bytes 4915216 | tf_op jit(solution)/shard_map/all_gather | solution.py:164
  223.9 10.8 %fusion.107 = f32[1024,2560]{1,0:T(8,128)} fusion(bf16[1024,960]{0,1:T(8,128)(2,1)} %multiply_convert_fusion.3, bf16[960,2560]{1,0:T(8,128)(2,1)} %all-gather.12.cloned.1.call-done), kind=kOutput, calls=%fused_computation.149 | convolution fusion | flops 5033164800 | bytes 17367040 | tf_op jit(solution)/shard_map/dot_general | solution.py:130
  234.7 55.5 %all-gather.16.cloned.1.call-done = bf16[2560,960]{0,1:T(8,128)(2,1)} async-done(((bf16[1280,960]{0,1:T(8,128)(2,1)}), bf16[2560,960]{0,1:T(8,128)(2,1)}) %all-gather.16.cloned.1.call-update) | async-done | bytes 4915216 | tf_op jit(solution)/shard_map/all_gather | solution.py:166
  290.2 20.2 %multiply_convert_fusion = (bf16[1024,2560]{1,0:T(8,128)(2,1)}, bf16[1024,2560]{1,0:T(8,128)(2,1)}, bf16[1024,2560]{1,0:T(8,128)(2,1)}) fusion(f32[1024,2560]{1,0:T(8,128)} %fusion.107, f32[1024,2560]{1,0:T(8,128)} %fusion.108, bf16[2560,960]{0,1:T(8,128)(2,1)} %all-gather.16.cloned.1.call-done, bf16[1,1024,960]{1,2,0:T(8,128)(2,1)} %param.23), kind=kOutput, calls=%fused_computation.28 | convolution fusion | flops 5072486400 | bytes 43581440 | tf_op jit(solution)/shard_map/dot_general | solution.py:130
  310.5 9.3 fusion.109
  319.8 8.9 multiply_reduce_fusion
  330.3 2.2 convolution_convert_fusion.3
  332.6 13.6 %fusion.57 = f32[5,64,1024]{2,1,0:T(8,128)} fusion(bf16[512,5,3,64]{0,3,2,1:T(8,128)(2,1)S(1)} %bitcast.245, f32[5,3,512,1024]{2,3,1,0:T(8,128)} %get-tuple-element.105, f32[5,3,512]{2,1,0:T(4,128)S(1)} %log_add_fusion.1), kind=kOutput, calls=%fused_computation.98 | convolution fusion | flops 1022361600 | bytes 33781760 | tf_op jit(solution)/shard_map/while/body/eval_jaxpr/grqk,qgrd->kgd/dot_general | solution.py:120
  346.2 23.8 %fusion.3 = (f32[5,3,512]{2,1,0:T(4,128)S(1)}, f32[5,1024,512,3]{2,1,3,0:T(8,128)}) fusion(f32[5,3,512,1024]{2,3,1,0:T(8,128)} %get-tuple-element.105, f32[5,3,512]{2,1,0:T(4,128)S(1)} %log_add_fusion.1, bf16[1024,5,64,1]{0,2,3,1:T(8,128)(2,1)} %fusion.86, bf16[512,5,3,64]{0,3,2,1:T(8,128)(2,1)S(1)} %bitcast.246), kind=kOutput, calls=%fused_computation.7 | convolution fusion | flops 1030218240 | bytes 64614400 | tf_op jit(solution)/shard_map/while/body/eval_jaxpr/qgrd,kgd->grqk/dot_general | solution.py:102
  370.1 23.8 %fusion = (f32[5,3,512]{2,1,0:T(4,128)S(1)}, f32[5,1024,512,3]{2,1,3,0:T(8,128)}) fusion(f32[5,3,512,1024]{2,3,1,0:T(8,128)} %get-tuple-element.103, f32[5,3,512]{2,1,0:T(4,128)S(1)} %log_add_fusion, bf16[1024,5,64,1]{0,2,3,1:T(8,128)(2,1)S(1)} %copy-done.20, bf16[512,5,3,64]{0,3,2,1:T(8,128)(2,1)S(1)} %bitcast.247), kind=kOutput, calls=%fused_computation.2 | convolution fusion | flops 1030218240 | bytes 64614400 | tf_op jit(solution)/shard_map/while/body/eval_jaxpr/qgrd,kgd->grqk/dot_general | solution.py:102
  393.9 13.6 %fusion.69 = bf16[5,64,1024]{2,1,0:T(8,128)(2,1)} fusion(f32[5,64,1024]{2,1,0:T(8,128)S(1)} %copy-done.13, bf16[512,5,3,64]{0,3,2,1:T(8,128)(2,1)S(1)} %bitcast.248, f32[5,3,512,1024]{2,3,1,0:T(8,128)} %get-tuple-element.103, f32[5,3,512]{2,1,0:T(4,128)S(1)} %log_add_fusion), kind=kOutput, calls=%fused_computation.104 | convolution fusion | flops 1023016960 | bytes 34437120 | tf_op jit(solution)/shard_map/while/body/eval_jaxpr/grqk,qgrd->kgd/dot_general | solution.py:120
  407.4 2.0 fusion.72
  410.7 26.8 %fusion.2 = bf16[5,3,512,1024]{2,3,1,0:T(8,128)(2,1)} fusion(f32[5,1024,512,3]{2,1,3,0:T(8,128)} %get-tuple-element.110, f32[5,3,512,1024]{2,3,1,0:T(8,128)} %get-tuple-element.103, f32[5,3,512]{2,1,0:T(4,128)S(1)} %get-tuple-element.109, f32[5,3,512]{2,1,0:T(4,128)S(1)} %log_add_fusion), kind=kLoop, calls=%fused_computation.4 | loop fusion | flops 31457280 | bytes 78704640 | tf_op jit(solution)/shard_map/while/body/eval_jaxpr/convert_element_type | solution.py:106
  437.6 10.3 %convolution_bitcast_fusion.1 = f32[5,64,1024]{2,1,0:T(8,128)S(1)} fusion(bf16[512,5,3,64]{0,3,2,1:T(8,128)(2,1)S(1)} %bitcast.244, bf16[5,3,512,1024]{2,3,1,0:T(8,128)(2,1)} %fusion.2), kind=kOutput, calls=%fused_computation.101 | convolution fusion | flops 1006632960 | bytes 18022400 | tf_op jit(solution)/shard_map/while/body/eval_jaxpr/grqk,qgrd->kgd/dot_general | solution.py:115
  447.9 26.7 %fusion.5 = bf16[5,3,512,1024]{2,3,1,0:T(8,128)(2,1)} fusion(f32[5,1024,512,3]{2,1,3,0:T(8,128)} %get-tuple-element.112, f32[5,3,512,1024]{2,3,1,0:T(8,128)} %get-tuple-element.105, f32[5,3,512]{2,1,0:T(4,128)S(1)} %get-tuple-element.111, f32[5,3,512]{2,1,0:T(4,128)S(1)} %log_add_fusion.1), kind=kLoop, calls=%fused_computation.9 | loop fusion | flops 31457280 | bytes 78704640 | tf_op jit(solution)/shard_map/while/body/eval_jaxpr/convert_element_type | solution.py:106
  474.5 11.4 %fusion.85 = f32[1,1024,5,64]{1,3,2,0:T(8,128)} fusion(f32[5,64,1024]{2,1,0:T(8,128)S(1)} %convolution_bitcast_fusion.1, bf16[512,5,3,64]{0,3,2,1:T(8,128)(2,1)S(1)} %bitcast.242, bf16[5,3,512,1024]{2,3,1,0:T(8,128)(2,1)} %fusion.5), kind=kOutput, calls=%fused_computation.112 | convolution fusion | flops 1007288320 | bytes 19333120 | tf_op jit(solution)/shard_map/while/body/eval_jaxpr/grqk,qgrd->kgd/dot_general | solution.py:115
  486.0 1.5 multiply_add_fusion.2
  489.7 6.3 convolution_convert_fusion.4
  496.3 8.3 multiply_bitcast_fusion
  504.6 8.3 multiply_bitcast_fusion.1
  514.2 1.3 copy-done.31
  515.5 3.5 fusion.52
  519.1 9.7 convolution_convert_fusion.2
  528.8 9.7 convolution_convert_fusion.1
  538.7 9.8 convolution_convert_fusion
  548.8 2.0 copy.71
  550.7 1.9 copy.69
  552.6 20.8 %reduce-scatter.12.cloned.1.call-done = bf16[480,960]{1,0:T(8,128)(2,1)} async-done(((bf16[960,960]{1,0:T(8,128)(2,1)}), bf16[480,960]{1,0:T(8,128)(2,1)}) %reduce-scatter.12.cloned.1.call-update) | async-done | bytes 921616 | tf_op jit(solution)/shard_map/reduce_scatter | solution.py:301
  573.4 64.9 %reduce-scatter.16.cloned.1.call-done = bf16[480,2560]{1,0:T(8,128)(2,1)} async-done(((bf16[960,2560]{1,0:T(8,128)(2,1)}), bf16[480,2560]{1,0:T(8,128)(2,1)}) %reduce-scatter.16.cloned.1.call-update) | async-done | bytes 2457616 | tf_op jit(solution)/shard_map/reduce_scatter | solution.py:241
  638.3 65.0 %reduce-scatter.18.cloned.1.call-done = bf16[480,2560]{1,0:T(8,128)(2,1)} async-done(((bf16[960,2560]{1,0:T(8,128)(2,1)}), bf16[480,2560]{1,0:T(8,128)(2,1)}) %reduce-scatter.18.cloned.1.call-update) | async-done | bytes 2457616 | tf_op jit(solution)/shard_map/reduce_scatter | solution.py:244
  703.3 64.9 %reduce-scatter.20.cloned.1.call-done = bf16[1280,960]{0,1:T(8,128)(2,1)} async-done(((bf16[2560,960]{0,1:T(8,128)(2,1)}), bf16[1280,960]{0,1:T(8,128)(2,1)}) %reduce-scatter.20.cloned.1.call-update) | async-done | bytes 2457616 | tf_op jit(solution)/shard_map/reduce_scatter | solution.py:247
  771.5 2.2 fusion.111
  773.7 3.9 fusion.30
  777.7 4.9 all-reduce.6
  782.7 34.3 %all-reduce.4 = (bf16[480]{0:T(512)(128)(2,1)S(1)}, bf16[480]{0:T(512)(128)(2,1)S(1)}) all-reduce(bf16[480]{0:T(512)(128)(2,1)S(1)} %dynamic-slice.4, bf16[480]{0:T(512)(128)(2,1)S(1)} %dynamic-slice.6), channel_id=1, replica_groups=mesh['rep'=16,'shard'=2] {'rep'}, use_global_device_ids=true, to_apply=%region_14.15 | all-reduce | flops 960 | bytes 3840 | tf_op jit(solution)/shard_map/psum | solution.py:315
  818.2 5.8 fusion.37
  824.0 9.8 fusion.36
  833.8 136.2 %all-reduce.10.cloned.1.call-done = (bf16[480,960]{1,0:T(8,128)(2,1)}, bf16[480,320]{0,1:T(8,128)(2,1)}, bf16[480,320]{0,1:T(8,128)(2,1)}, bf16[480,960]{1,0:T(8...) async-done(((bf16[480,960]{1,0:T(8,128)(2,1)}, bf16[480,320]{0,1:T(8,128)(2,1)}, bf16[480,320]{0,1:T(8,128)(2,1)}, ...) | async-done | bytes 9830416 | tf_op jit(solution)/shard_map/psum | solution.py:316
  970.0 2.0 convert_element_type.280
  972.0 1.9 convert_element_type.282
  973.9 2.7 convert_element_type.278
  976.6 1.5 convert_element_type.284
  978.1 2.9 convert_element_type.288
  981.0 2.9 convert_element_type.290
  983.9 2.6 convert_element_type.292
  (170 shorter events, 22.4 us)
Async XLA Ops:
  7.2 58.0 %all-gather.8.cloned.1.call-start = ((), (), s32[]{:S(2)}) async-start(), calls=%async_computation.7 | async-start | bytes 2949120 | tf_op jit(solution)/shard_map/all_gather | solution.py:157
  7.9 146.6 %all-gather.10.cloned.1.call-start = ((), (), s32[]{:S(2)}) async-start(), calls=%async_computation.8 | async-start | bytes 2949120 | tf_op jit(solution)/shard_map/all_gather | solution.py:160
  8.7 2.0 copy-start.35
  8.7 2.2 copy-start.40
  8.7 3.4 copy-start.42
  8.7 3.6 copy-start.43
  8.7 10.5 %copy-start = (bf16[1,1024,960]{1,2,0:T(8,128)(2,1)S(1)}, bf16[1,1024,960]{1,2,0:T(8,128)(2,1)}, u32[]{:S(2)}) copy-start(bf16[1,1024,960]{1,2,0:T(8,128)(2,1)} %param.12) | copy-start | bytes 5898244
  8.7 154.0 %all-gather.14.cloned.1.call-start = ((), (), s32[]{:S(2)}) async-start(), calls=%async_computation.10 | async-start | bytes 7372800 | tf_op jit(solution)/shard_map/all_gather | solution.py:165
  9.4 10.3 %copy-start.34 = (bf16[480,320]{0,1:T(8,128)(2,1)S(1)}, bf16[480,320]{0,1:T(8,128)(2,1)}, u32[]{:S(2)}) copy-start(bf16[480,320]{0,1:T(8,128)(2,1)} %param.16) | copy-start | bytes 921604
  9.5 214.5 %all-gather.12.cloned.1.call-start = ((), (), s32[]{:S(2)}) async-start(), calls=%async_computation.9 | async-start | bytes 7372800 | tf_op jit(solution)/shard_map/all_gather | solution.py:164
  10.0 280.2 %all-gather.16.cloned.1.call-start = ((), (), s32[]{:S(2)}) async-start(), calls=%async_computation.11 | async-start | bytes 7372800 | tf_op jit(solution)/shard_map/all_gather | solution.py:166
  10.6 538.2 %reduce-scatter.24.cloned.1.call-start = ((), (), s32[]{:S(2)}) async-start(), calls=%async_computation.18 | async-start | bytes 1105920
  18.4 50.7 %copy-start.36 = (f32[960]{0:T(1024)}, f32[960]{0:T(1024)S(1)}, u32[]{:S(2)}) copy-start(f32[960]{0:T(1024)S(1)} %convert_element_type.245) | copy-start | bytes 11524
  19.7 49.4 %copy-start.38 = (f32[1024]{0:T(1024)}, f32[1024]{0:T(1024)S(1)}, u32[]{:S(2)}) copy-start(f32[1024]{0:T(1024)S(1)} %add_rsqrt_fusion.1) | copy-start | bytes 12292
  38.1 23.9 %copy-start.23 = (bf16[960,320]{0,1:T(8,128)(2,1)}, bf16[960,320]{0,1:T(8,128)(2,1)S(1)}, u32[]{:S(2)}) copy-start(bf16[960,320]{0,1:T(8,128)(2,1)S(1)} %reshape.472) | copy-start | bytes 1843204
  60.2 1.8 copy-start.21
  63.5 0.9 copy-start.16
  63.5 9.5 copy-start.14
  64.4 50.2 %copy-start.9 = (bf16[1024,5,32]{0,2,1:T(8,128)(2,1)}, bf16[1024,5,32]{0,2,1:T(8,128)(2,1)S(1)}, u32[]{:S(2)}) copy-start(bf16[1024,5,32]{0,2,1:T(8,128)(2,1)S(1)} %get-tuple-element.92) | copy-start | bytes 983044
  69.1 3.9 copy-start.17
  73.0 1.0 copy-start.11
  73.9 12.8 %copy-start.7 = (bf16[1,512,15,64]{1,3,2,0:T(8,128)(2,1)}, bf16[1,512,15,64]{1,3,2,0:T(8,128)(2,1)S(1)}, u32[]{:S(2)}) copy-start(bf16[1,512,15,64]{1,3,2,0:T(8,128)(2,1)S(1)} %get-tuple-element.89) | copy-start | bytes 2949124
  73.9 40.7 %copy-start.5 = (bf16[1,512,15,64]{1,3,2,0:T(8,128)(2,1)}, bf16[1,512,15,64]{1,3,2,0:T(8,128)(2,1)S(1)}, u32[]{:S(2)}) copy-start(bf16[1,512,15,64]{1,3,2,0:T(8,128)(2,1)S(1)} %get-tuple-element.88) | copy-start | bytes 2949124
  86.7 12.9 %copy-start.19 = (bf16[1024,5,64,1]{0,2,3,1:T(8,128)(2,1)S(1)}, bf16[1024,5,64,1]{0,2,3,1:T(8,128)(2,1)}, u32[]{:S(2)}) copy-start(bf16[1024,5,64,1]{0,2,3,1:T(8,128)(2,1)} %fusion.86) | copy-start | bytes 1966084
  159.1 2.0 copy-start.1
  310.5 9.3 copy-start.2
  310.5 9.3 copy-start.45
  319.8 9.0 copy-start.29
  328.7 1.5 copy-start.44
  330.3 2.2 copy-start.4
  346.2 23.9 %copy-start.20 = (bf16[1024,5,64,1]{0,2,3,1:T(8,128)(2,1)S(1)}, bf16[1024,5,64,1]{0,2,3,1:T(8,128)(2,1)}, u32[]{:S(2)}) copy-start(bf16[1024,5,64,1]{0,2,3,1:T(8,128)(2,1)} %fusion.86) | copy-start | bytes 1966084
  370.0 23.8 %copy-start.13 = (f32[5,64,1024]{2,1,0:T(8,128)S(1)}, f32[5,64,1024]{2,1,0:T(8,128)}, u32[]{:S(2)}) copy-start(f32[5,64,1024]{2,1,0:T(8,128)} %fusion.57) | copy-start | bytes 3932164
  393.8 13.6 %copy-start.37 = (f32[960]{0:T(1024)S(1)}, f32[960]{0:T(1024)}, u32[]{:S(2)}) copy-start(f32[960]{0:T(1024)} %copy-done.36) | copy-start | bytes 11524
  393.8 13.6 %copy-start.39 = (f32[1024]{0:T(1024)S(1)}, f32[1024]{0:T(1024)}, u32[]{:S(2)}) copy-start(f32[1024]{0:T(1024)} %copy-done.38) | copy-start | bytes 12292
  410.7 140.1 %reduce-scatter.22.cloned.1.call-start = ((), (), s32[]{:S(2)}) async-start(), calls=%async_computation.17 | async-start | bytes 1105920
  410.7 26.8 %copy-start.8 = (bf16[1,512,15,64]{1,3,2,0:T(8,128)(2,1)S(1)}, bf16[1,512,15,64]{1,3,2,0:T(8,128)(2,1)}, u32[]{:S(2)}) copy-start(bf16[1,512,15,64]{1,3,2,0:T(8,128)(2,1)} %copy-done.7) | copy-start | bytes 2949124
  447.8 26.7 %copy-start.6 = (bf16[1,512,15,64]{1,3,2,0:T(8,128)(2,1)S(1)}, bf16[1,512,15,64]{1,3,2,0:T(8,128)(2,1)}, u32[]{:S(2)}) copy-start(bf16[1,512,15,64]{1,3,2,0:T(8,128)(2,1)} %copy-done.5) | copy-start | bytes 2949124
  474.5 11.4 %copy-start.15 = (f32[1024,32]{0,1:T(8,128)S(1)}, f32[1024,32]{0,1:T(8,128)}, u32[]{:S(2)}) copy-start(f32[1024,32]{0,1:T(8,128)} %copy-done.14) | copy-start | bytes 393220
  474.5 11.4 %copy-start.18 = (f32[1024,32]{0,1:T(8,128)S(1)}, f32[1024,32]{0,1:T(8,128)}, u32[]{:S(2)}) copy-start(f32[1024,32]{0,1:T(8,128)} %copy-done.16) | copy-start | bytes 393220
  489.7 6.6 copy-start.10
  489.7 6.6 copy-start.12
  489.7 62.9 %reduce-scatter.14.cloned.1.call-start = ((), (), s32[]{:S(2)}) async-start(), calls=%async_computation.13 | async-start | bytes 2949120 | tf_op jit(solution)/shard_map/reduce_scatter | solution.py:310
  496.0 77.4 %reduce-scatter.12.cloned.1.call-start = ((), (), s32[]{:S(2)}) async-start(), calls=%async_computation.12 | async-start | bytes 2949120 | tf_op jit(solution)/shard_map/reduce_scatter | solution.py:301
  514.2 1.3 copy-start.31
  519.0 119.2 %reduce-scatter.16.cloned.1.call-start = ((), (), s32[]{:S(2)}) async-start(), calls=%async_computation.14 | async-start | bytes 7372800 | tf_op jit(solution)/shard_map/reduce_scatter | solution.py:241
  528.8 174.5 %reduce-scatter.18.cloned.1.call-start = ((), (), s32[]{:S(2)}) async-start(), calls=%async_computation.15 | async-start | bytes 7372800 | tf_op jit(solution)/shard_map/reduce_scatter | solution.py:244
  538.6 229.6 %reduce-scatter.20.cloned.1.call-start = ((), (), s32[]{:S(2)}) async-start(), calls=%async_computation.16 | async-start | bytes 7372800 | tf_op jit(solution)/shard_map/reduce_scatter | solution.py:247
  548.5 421.5 %all-reduce.10.cloned.1.call-start = ((), (), s32[]{:S(2)}) async-start(), calls=%async_computation.19 | async-start | bytes 19988480 | tf_op jit(solution)/shard_map/psum | solution.py:316
  768.3 1.1 copy-start.24
  769.4 1.5 copy-start.30
  769.4 2.1 copy-start.32
  771.5 2.2 copy-start.22
  771.5 2.2 copy-start.25
  773.7 3.9 copy-start.41
  818.2 5.8 copy-start.3
  970.0 6.6 copy-start.33
  970.0 8.1 copy-start.28
  978.1 2.9 copy-start.27
  981.0 2.9 copy-start.26
Sparse Core Ops, SparseCore 0:
  9.6 47.7 all-gather.7
  58.9 32.2 all-gather.9
  92.7 64.8 all-gather.13
  159.0 64.8 all-gather.11
  225.3 64.8 all-gather.15
  410.8 16.8 reduce-scatter.23
  489.8 16.9 reduce-scatter.21
  509.6 30.4 reduce-scatter.13
  543.0 30.3 reduce-scatter.11
  576.1 62.1 reduce-scatter.15
  641.2 62.0 reduce-scatter.17
  706.1 62.1 reduce-scatter.19
  773.6 196.3 all-reduce.9
where the time goes:
time: 998 us; the launch traced here: 993 us
  waiting for transfers between devices  461 us (46%)
  matrix products  299 us (30%)
  other arithmetic  114 us (11%)
  blocking collectives  80 us (8%)
  local copies, waits for them, and re-layouts  22.6 us (2%)
  between operations  16.4 us (2%)
    psum x1, waiting for transfers between devices, per_device(): lax.psum(attn_grads[1].astype(jnp.bfloat16), 'rep').astype(jnp.float32)  136 us
    dot_general x21, matrix products, product(): return jnp.dot(left, right, preferred_element_type=jnp.float32)  133 us
    reduce_scatter x1, waiting for transfers between devices, per_device(): lax.psum_scatter(grad_up.astype(jnp.bfloat16), 'shard', scatter_dimension...  65 us
    reduce_scatter x1, waiting for transfers between devices, per_device(): lax.psum_scatter(grad_down.astype(jnp.bfloat16), 'shard', scatter_dimensi...  64.9 us
    reduce_scatter x1, waiting for transfers between devices, per_device(): lax.psum_scatter(grad_gate.astype(jnp.bfloat16), 'shard', scatter_dimensi...  64.9 us
    all_gather x1, waiting for transfers between devices, per_device(): lax.all_gather(w_down, 'shard', axis=0, tiled=True)  55.5 us
    convert_element_type x2, other arithmetic, attend_backward(): score_grad = (probs * (probs_grad - inner)).astype(jnp.bfloat16)  53.5 us
    all_gather x1, waiting for transfers between devices, per_device(): lax.all_gather(w_gate, 'shard', axis=0, tiled=True)  50.4 us
  transfers between devices with their start and end apart: 13, of which 7 were waited for; matrix products, arithmetic and copies ran while one was open for 30% of the time, Pallas kernels for 0%

commit v1 on v0

--- a/solution.py
+++ b/solution.py
@@ -133,6 +133,105 @@
 def norm_backward(grad_in, normed, inverse, gain):
     weighted = grad_in * gain
     return inverse * (weighted - normed * jnp.mean(weighted * normed, axis=-1, keepdims=True))
+
+
+def bit_swap(count, bit):
+    return [(i, i ^ bit) for i in range(count)]
+
+
+def swap_rep(value, bit):
+    return lax.ppermute(value, "rep", bit_swap(lax.axis_size("rep"), bit))
+
+
+def swap_shard(value, bit):
+    return lax.ppermute(value, "shard", bit_swap(lax.axis_size("shard"), bit))
+
+
+def rep_bit(bit):
+    return (lax.axis_index("rep") // bit) % 2
+
+
+def place_pair(mine, other, bit, axis):
+    low = jnp.concatenate([mine, other], axis=axis)
+    high = jnp.concatenate([other, mine], axis=axis)
+    return jnp.where(bit == 0, low, high)
+
+
+def gather_rows(piece):
+    shards = lax.axis_size("shard")
+    rows, columns = piece.shape
+    quarter = rows // 4
+    core, side = rep_bit(1), rep_bit(2)
+    part = lax.dynamic_slice_in_dim(piece, (core * 2 + side) * quarter, quarter, 0)
+    held = part[None]
+    bit = 1
+    while bit < shards:
+        held = jnp.concatenate([held, swap_shard(held, bit)], axis=0)
+        bit *= 2
+    others = held[1:]
+    others = place_pair(others, swap_rep(others, 2), side, 1)
+    others = place_pair(others, swap_rep(others, 1), core, 1)
+    me = lax.axis_index("shard")
+    if shards == 2:
+        return place_pair(piece, others[0], me, 0)
+    whole = jnp.zeros((shards, rows, columns), piece.dtype)
+    whole = lax.dynamic_update_slice_in_dim(whole, piece[None], me, 0)
+    for j in range(1, shards):
+        whole = lax.dynamic_update_slice_in_dim(whole, others[j - 1][None], me ^ j, 0)
+    return whole.reshape(shards * rows, columns)
+
+
+def add_up(left, right):
+    return (left.astype(jnp.float32) + right.astype(jnp.float32)).astype(jnp.bfloat16)
+
+
+def halve(value, bit, axis, swap):
+    half = value.shape[axis] // 2
+    mine = lax.dynamic_slice_in_dim(value, bit * half, half, axis)
+    theirs = lax.dynamic_slice_in_dim(value, (1 - bit) * half, half, axis)
+    return add_up(mine, swap(theirs))
+
+
+def halve_shard(value):
+    bit = lax.axis_size("shard") // 2
+    while bit:
+        value = halve(
+            value, (lax.axis_index("shard") // bit) % 2, 0, partial(swap_shard, bit=bit)
+        )
+        bit //= 2
+    return value
+
+
+def reduce_rows(grad, order, axes):
+    shards = lax.axis_size("shard")
+    rows, columns = grad.shape
+    value = grad.astype(jnp.bfloat16).reshape(shards, rows // shards, columns)
+    value = halve(value, rep_bit(1), axes[1], partial(swap_rep, bit=1))
+    for step in order:
+        if step == 0:
+            value = halve_shard(value)
+        else:
+            value = halve(value, rep_bit(step), axes[step], partial(swap_rep, bit=step))
+    bit = 8
+    while bit < lax.axis_size("rep"):
+        value = add_up(value, swap_rep(value, bit))
+        bit *= 2
+    for step in [s for s in reversed(order) if s] + [1]:
+        value = place_pair(value, swap_rep(value, step), rep_bit(step), axes[step])
+    return value[0].astype(jnp.float32)
+
+
+def reduce_gains(grads):
+    bit = 1
+    while bit < lax.axis_size("rep"):
+        grads = grads + swap_rep(grads, bit)
+        bit *= 2
+    bit = 1
+    while bit < lax.axis_size("shard"):
+        grads = grads + swap_shard(grads, bit)
+        bit *= 2
+    own = grads.shape[1] // lax.axis_size("shard")
+    return lax.dynamic_slice_in_dim(grads, lax.axis_index("shard") * own, own, 1)
 
 
 def per_device(
@@ -152,18 +251,27 @@
     packed_sequences, segment_length, width = tokens.shape
     row_total_count = packed_sequences * segment_length
     head_groups = QUERY_HEADS // KEY_VALUE_HEADS
+    columns = QUERY_HEADS * HEAD_SIZE
+    key_columns = KEY_VALUE_HEADS * HEAD_SIZE
+    gains = jnp.stack([gain_attn, gain_mlp], axis=1)
+    gains = jnp.pad(gains, ((0, 0), (0, 62)))
+    first = gather_rows(
+        jnp.concatenate([w_query, key_weight_matrix, value_weight_matrix, gains], axis=1)
+    )
+    end_key = columns + key_columns
+    end_value = end_key + key_columns
     attn_set = (
-        lax.all_gather(gain_attn, "shard", axis=0, tiled=True),
-        lax.all_gather(w_query, "shard", axis=0, tiled=True),
-        lax.all_gather(key_weight_matrix, "shard", axis=0, tiled=True),
-        lax.all_gather(value_weight_matrix, "shard", axis=0, tiled=True),
-        lax.all_gather(w_out, "shard", axis=0, tiled=True),
+        first[:, end_value],
+        first[:, :columns],
+        first[:, columns:end_key],
+        first[:, end_key:end_value],
+        gather_rows(w_out),
     )
     mlp_set = (
-        lax.all_gather(gain_mlp, "shard", axis=0, tiled=True),
-        lax.all_gather(w_gate, "shard", axis=0, tiled=True),
-        lax.all_gather(w_up, "shard", axis=0, tiled=True),
-        lax.all_gather(w_down, "shard", axis=0, tiled=True),
+        first[:, end_value + 1],
+        gather_rows(w_gate),
+        gather_rows(w_up),
+        gather_rows(w_down),
     )
     cosine_table, sine_table = jax.vmap(partial(angles, head_dim=HEAD_SIZE))(segments)
     norm_one = attn_set[0].astype(jnp.float32)
@@ -206,19 +314,8 @@
     hidden = (activated * up_pre).astype(jnp.bfloat16)
     result = middle + product(hidden, mlp_set[3])
     mixed = result.astype(jnp.bfloat16).reshape(packed_sequences, segment_length, width)
-    mlp_back = (
-        lax.all_gather(gain_mlp, "shard", axis=0, tiled=True),
-        lax.all_gather(w_gate, "shard", axis=0, tiled=True),
-        lax.all_gather(w_up, "shard", axis=0, tiled=True),
-        lax.all_gather(w_down, "shard", axis=0, tiled=True),
-    )
-    attn_back = (
-        lax.all_gather(gain_attn, "shard", axis=0, tiled=True),
-        lax.all_gather(w_query, "shard", axis=0, tiled=True),
-        lax.all_gather(key_weight_matrix, "shard", axis=0, tiled=True),
-        lax.all_gather(value_weight_matrix, "shard", axis=0, tiled=True),
-        lax.all_gather(w_out, "shard", axis=0, tiled=True),
-    )
+    mlp_back = mlp_set
+    attn_back = attn_set
     out_grad = cotangent.reshape(row_total_count, width)
     grad_down = product(hidden.T, out_grad)
     hidden_grad = product(out_grad, mlp_back[3].T)
@@ -234,26 +331,11 @@
     middle_grad = out_grad.astype(jnp.float32) + norm_backward(
         mlp_in_grad, normed_two, inverse_two, mlp_back[0].astype(jnp.float32)
     )
-    mlp_grads = (
-        lax.psum_scatter(
-            grad_norm_two.astype(jnp.bfloat16), "shard", scatter_dimension=0, tiled=True
-        ).astype(jnp.float32),
-        lax.psum_scatter(
-            grad_gate.astype(jnp.bfloat16), "shard", scatter_dimension=0, tiled=True
-        ).astype(jnp.float32),
-        lax.psum_scatter(
-            grad_up.astype(jnp.bfloat16), "shard", scatter_dimension=0, tiled=True
-        ).astype(jnp.float32),
-        lax.psum_scatter(
-            grad_down.astype(jnp.bfloat16), "shard", scatter_dimension=0, tiled=True
-        ).astype(jnp.float32),
-    )
-    mlp_grads = (
-        lax.psum(mlp_grads[0].astype(jnp.bfloat16), "rep").astype(jnp.float32),
-        lax.psum(mlp_grads[1].astype(jnp.bfloat16), "rep").astype(jnp.float32),
-        lax.psum(mlp_grads[2].astype(jnp.bfloat16), "rep").astype(jnp.float32),
-        lax.psum(mlp_grads[3].astype(jnp.bfloat16), "rep").astype(jnp.float32),
-    )
+    wide = {1: 2, 2: 2, 4: 1}
+    tall = {1: 1, 2: 1, 4: 1}
+    sum_gate = reduce_rows(grad_gate, (0, 2, 4), wide)
+    sum_up = reduce_rows(grad_up, (4, 2, 0), wide)
+    sum_down = reduce_rows(grad_down, (2, 0, 4), tall)
     branch_grad = middle_grad.astype(jnp.bfloat16)
     grad_out = product(heads.T, branch_grad)
     heads_grad = (
@@ -294,43 +376,22 @@
         attn_in_grad, normed_one, inverse_one, attn_back[0].astype(jnp.float32)
     )
     grad_tokens = input_grad.astype(jnp.bfloat16).reshape(packed_sequences, segment_length, width)
-    attn_grads = (
-        lax.psum_scatter(
-            grad_norm_one.astype(jnp.bfloat16), "shard", scatter_dimension=0, tiled=True
-        ).astype(jnp.float32),
-        lax.psum_scatter(
-            grad_query.astype(jnp.bfloat16), "shard", scatter_dimension=0, tiled=True
-        ).astype(jnp.float32),
-        lax.psum_scatter(
-            grad_key.astype(jnp.bfloat16), "shard", scatter_dimension=0, tiled=True
-        ).astype(jnp.float32),
-        lax.psum_scatter(
-            grad_value.astype(jnp.bfloat16), "shard", scatter_dimension=0, tiled=True
-        ).astype(jnp.float32),
-        lax.psum_scatter(
-            grad_out.astype(jnp.bfloat16), "shard", scatter_dimension=0, tiled=True
-        ).astype(jnp.float32),
-    )
-    attn_grads = (
-        lax.psum(attn_grads[0].astype(jnp.bfloat16), "rep").astype(jnp.float32),
-        lax.psum(attn_grads[1].astype(jnp.bfloat16), "rep").astype(jnp.float32),
-        lax.psum(attn_grads[2].astype(jnp.bfloat16), "rep").astype(jnp.float32),
-        lax.psum(attn_grads[3].astype(jnp.bfloat16), "rep").astype(jnp.float32),
-        lax.psum(attn_grads[4].astype(jnp.bfloat16), "rep").astype(jnp.float32),
-    )
-    finals = attn_grads + mlp_grads
+    attn_sums = reduce_rows(
+        jnp.concatenate([grad_query, grad_key, grad_value, grad_out], axis=1), (0, 4, 2), wide
+    )
+    gain_sums = reduce_gains(jnp.stack([grad_norm_one, grad_norm_two]))
     return (
         mixed,
         grad_tokens,
-        finals[0],
-        finals[1],
-        finals[2],
-        finals[3],
-        finals[4],
-        finals[5],
-        finals[6],
-        finals[7],
-        finals[8],
+        gain_sums[0],
+        attn_sums[:, :columns],
+        attn_sums[:, columns:end_key],
+        attn_sums[:, end_key:end_value],
+        attn_sums[:, end_value:],
+        gain_sums[1],
+        sum_gate,
+        sum_up,
+        sum_down,
     )
 
 

time: 998 us -> 839 us (0.84)
  waiting for transfers between devices: 461 us -> 192 us
  local copies, waits for them, and re-layouts: 22.6 us -> 114 us
  blocking collectives: 80 us -> 0 us
  other arithmetic: 114 us -> 180 us
  starting transfers between devices: 0.98 us -> 41.6 us
  between operations: 16.4 us -> 2.67 us
    reduce_scatter x5 -> x0, waiting for transfers between devices: 216 us -> none  [the longest x1 65 us: per_device(): lax.psum_scatter(grad_up.astype(jnp.bfloat16), 'shard', scatter_dimension...]
    ppermute x0 -> x52, waiting for transfers between devices: none -> 192 us  [the longest x42 138 us: swap_rep(): return lax.ppermute(value, 'rep', bit_swap(lax.axis_size('rep'), bit))]
    psum x1 -> x0, waiting for transfers between devices: 136 us -> none  [per_device(): lax.psum(attn_grads[1].astype(jnp.bfloat16), 'rep').astype(jnp.float32)]
    all_gather x5 -> x0, waiting for transfers between devices: 106 us -> none  [the longest x1 55.5 us: per_device(): lax.all_gather(w_down, 'shard', axis=0, tiled=True)]
    select_n x0 -> x31, other arithmetic: none -> 53 us  [place_pair(): return jnp.where(bit == 0, low, high)]
    ppermute x0 -> x52, starting transfers between devices: none -> 41.6 us  [the longest x42 29.1 us: swap_rep(): return lax.ppermute(value, 'rep', bit_swap(lax.axis_size('rep'), bit))]
    all_gather x2 -> x0, blocking collectives: 34.9 us -> none  [the longest x1 17.9 us: per_device(): lax.all_gather(value_weight_matrix, 'shard', axis=0, tiled=True)]
    psum x1 -> x0, blocking collectives: 34.3 us -> none  [per_device(): lax.psum(attn_grads[0].astype(jnp.bfloat16), 'rep').astype(jnp.float32)]
  transfers between devices with their start and end apart: 13 -> 52, of which waited for: 7 -> 23; matrix products, arithmetic and copies ran while one was open for 30% -> 41% of each run, Pallas kernels for 0% -> 0%
where the time goes in v1:
time: 839 us; the launch traced here: 828 us
  matrix products  298 us (36%)
  waiting for transfers between devices  192 us (23%)
  other arithmetic  180 us (21%)
  local copies, waits for them, and re-layouts  114 us (14%)
  starting transfers between devices  41.6 us (5%)
    ppermute x42, waiting for transfers between devices, swap_rep(): return lax.ppermute(value, 'rep', bit_swap(lax.axis_size('rep'), bit))  138 us
    dot_general x21, matrix products, product(): return jnp.dot(left, right, preferred_element_type=jnp.float32)  130 us
    ppermute x10, waiting for transfers between devices, swap_shard(): return lax.ppermute(value, 'shard', bit_swap(lax.axis_size('shard'), bit))  54.5 us
    convert_element_type x2, other arithmetic, attend_backward(): score_grad = (probs * (probs_grad - inner)).astype(jnp.bfloat16)  53.6 us
    select_n x31, other arithmetic, place_pair(): return jnp.where(bit == 0, low, high)  53 us
    dot_general x2, matrix products, attend_backward(): jnp.einsum('qgrd,kgd->grqk', upstream_block, value_vectors, preferred_ele...  47.6 us
    unnamed x191, local copies, waits for them, and re-layouts  29.7 us
    ppermute x42, starting transfers between devices, swap_rep(): return lax.ppermute(value, 'rep', bit_swap(lax.axis_size('rep'), bit))  29.1 us
  transfers between devices with their start and end apart: 52, of which 23 were waited for; matrix products, arithmetic and copies ran while one was open for 41% of the time, Pallas kernels for 0%

profile of v1, /device:TPU:0, one launch (start us, length us, event | category | flops | bytes accessed | tf_op | source)
XLA Modules:
  0.0 828.2 jit_solution(9702455206621400531)
XLA Ops:
  14.7 3.8 concatenate.737
  26.6 4.4 copy.130
  31.0 29.5 %collective-permute-done = bf16[1,120,1664]{2,1,0:T(8,128)(2,1)} collective-permute-done((bf16[1,120,1664]{2,1,0:T(8,128)(2,1)}, bf16[1,120,1664]{2,1,0:T(8,128)(2,1)}, u32[]{:S(2)}, u32[]{:S(2)}) %collective-permute-start) | collective-permute-done | bytes 399392 | tf_op jit(solution)/shard_map/ppermute | solution.py:147
  67.2 5.7 collective-permute-done.1
  78.7 7.3 collective-permute-done.10
  88.9 10.3 %collective-permute-done.7 = bf16[1,120,2560]{2,1,0:T(8,128)(2,1)S(1)} collective-permute-done((bf16[1,120,2560]{2,1,0:T(8,128)(2,1)}, bf16[1,120,2560]{2,1,0:T(8,128)(2,1)S(1)}, u32[]{:S(2)}, u32[]{:S(2)}) %collective-permute-start.7) | collective-permute-done | bytes 614432 | tf_op jit(solution)/shard_map/ppermute | solution.py:143
  102.0 9.5 %collective-permute-done.13 = bf16[1,320,960]{2,1,0:T(8,128)(2,1)S(1)} collective-permute-done((bf16[1,320,960]{2,1,0:T(8,128)(2,1)}, bf16[1,320,960]{2,1,0:T(8,128)(2,1)S(1)}, u32[]{:S(2)}, u32[]{:S(2)}) %collective-permute-start.13) | collective-permute-done | bytes 614432 | tf_op jit(solution)/shard_map/ppermute | solution.py:143
  117.7 3.6 maximum_select_fusion.13
  126.3 4.8 maximum_select_fusion.3
  144.0 3.8 copy.124
  147.8 4.4 convolution_bitcast_fusion
  153.4 12.7 %fusion.117 = (f32[5,3,512]{2,1,0:T(4,128)S(1)}, f32[5,3,512,1024]{2,3,1,0:T(8,128)}) fusion(bf16[512,5,3,64]{0,3,2,1:T(8,128)(2,1)S(1)} %bitcast.300, bf16[1024,5,32]{0,2,1:T(8,128)(2,1)S(1)} %get-tuple-element.145, bf16[1024,5,32]{0,2,1:T(8,128)(2,1)S(1)} %get-tuple-element.144, pred[512,1024]{0,1:T(8,128)(4,1)S(1)} %get-tuple-element.151), kind=kOutput, calls=%fused_computation.262 | convolution fusion | flops 1031528960 | bytes 33650688 | tf_op jit(solution)/shard_map/while/body/eval_jaxpr/qgrd,kgd->grqk/dot_general | solution.py:56
  166.1 12.8 %fusion.7 = f32[5,3,512]{2,1,0:T(4,128)S(1)} fusion(f32[5,3,512,1024]{2,3,1,0:T(8,128)} %get-tuple-element.155, f32[5,3,512]{2,1,0:T(4,128)S(1)} %get-tuple-element.154), kind=kLoop, calls=%fused_computation.19 | loop fusion | flops 15720960 | bytes 31518720 | tf_op jit(solution)/shard_map/while/body/eval_jaxpr/reduce_sum | solution.py:80
  178.9 13.0 %fusion.82 = bf16[512,5,3,64]{0,3,2,1:T(8,128)(2,1)S(1)} fusion(bf16[1024,5,64,1]{0,2,3,1:T(8,128)(2,1)S(1)} %copy-done.36, f32[5,3,512,1024]{2,3,1,0:T(8,128)} %get-tuple-element.155, f32[5,3,512]{2,1,0:T(4,128)S(1)} %fusion.7, f32[5,3,512]{2,1,0:T(4,128)S(1)} %get-tuple-element.154), kind=kOutput, calls=%fused_computation.137 | convolution fusion | flops 1030717440 | bytes 33157120 | tf_op jit(solution)/shard_map/while/body/eval_jaxpr/grqk,kgd->qgrd/dot_general | solution.py:83
  192.0 12.6 %fusion.118 = (f32[5,3,512]{2,1,0:T(4,128)S(1)}, f32[5,3,512,1024]{2,3,1,0:T(8,128)}) fusion(bf16[512,5,3,64]{0,3,2,1:T(8,128)(2,1)S(1)} %bitcast.298, bf16[1024,5,32]{0,2,1:T(8,128)(2,1)S(1)} %get-tuple-element.145, bf16[1024,5,32]{0,2,1:T(8,128)(2,1)S(1)} %get-tuple-element.144, pred[512,1024]{0,1:T(8,128)(4,1)S(1)} %get-tuple-element.150), kind=kOutput, calls=%fused_computation.263 | convolution fusion | flops 1031528960 | bytes 33650688 | tf_op jit(solution)/shard_map/while/body/eval_jaxpr/qgrd,kgd->grqk/dot_general | solution.py:56
  204.6 12.8 %fusion.6 = f32[5,3,512]{2,1,0:T(4,128)S(1)} fusion(f32[5,3,512,1024]{2,3,1,0:T(8,128)} %get-tuple-element.157, f32[5,3,512]{2,1,0:T(4,128)S(1)} %get-tuple-element.156), kind=kLoop, calls=%fused_computation.18 | loop fusion | flops 15720960 | bytes 31518720 | tf_op jit(solution)/shard_map/while/body/eval_jaxpr/reduce_sum | solution.py:80
  217.4 12.9 %fusion.81 = bf16[512,5,3,64]{0,3,2,1:T(8,128)(2,1)S(1)} fusion(bf16[1024,5,64,1]{0,2,3,1:T(8,128)(2,1)S(1)} %copy-done.36, f32[5,3,512,1024]{2,3,1,0:T(8,128)} %get-tuple-element.157, f32[5,3,512]{2,1,0:T(4,128)S(1)} %fusion.6, f32[5,3,512]{2,1,0:T(4,128)S(1)} %get-tuple-element.156), kind=kOutput, calls=%fused_computation.136 | convolution fusion | flops 1030717440 | bytes 33157120 | tf_op jit(solution)/shard_map/while/body/eval_jaxpr/grqk,kgd->qgrd/dot_general | solution.py:83
  240.1 8.6 %fusion.93 = f32[1024,2560]{1,0:T(8,128)} fusion(bf16[1024,960]{0,1:T(8,128)(2,1)S(1)} %multiply_convert_fusion.1, bf16[480,2560]{1,0:T(8,128)(2,1)S(1)} %maximum_select_fusion.7, bf16[480,2560]{1,0:T(8,128)(2,1)S(1)} %copy-done.69, pred[]{:T(512)S(6)} %eq.140), kind=kOutput, calls=%fused_computation.167 | convolution fusion | flops 5055283200 | bytes 17367040 | tf_op jit(solution)/shard_map/dot_general | solution.py:130
  251.1 8.3 %fusion.94 = f32[1024,2560]{1,0:T(8,128)} fusion(bf16[1024,960]{0,1:T(8,128)(2,1)S(1)} %multiply_convert_fusion.1, bf16[480,2560]{1,0:T(8,128)(2,1)S(1)} %maximum_select_fusion.6, bf16[480,2560]{1,0:T(8,128)(2,1)S(1)} %copy-done.71, pred[]{:T(512)S(6)} %eq.140), kind=kOutput, calls=%fused_computation.168 | convolution fusion | flops 5055283200 | bytes 17367040 | tf_op jit(solution)/shard_map/dot_general | solution.py:130
  263.5 21.0 %fusion.20 = (bf16[1024,2560]{1,0:T(8,128)(2,1)}, bf16[1024,2560]{1,0:T(8,128)(2,1)}, bf16[1024,2560]{1,0:T(8,128)(2,1)}) fusion(f32[1024,2560]{1,0:T(8,128)} %fusion.93, f32[1024,2560]{1,0:T(8,128)} %fusion.94, bf16[1,1024,960]{1,2,0:T(8,128)(2,1)S(1)} %copy-done.54, bf16[1280,960]{1,0:T(8,128)(2,1)S(1)} %maximum_select_fusion.4, ...), kind=kOutput, calls=%fused_computation.32 | convolution fusion | flops 5094604800 | bytes 43581440 | tf_op jit(solution)/shard_map/dot_general | solution.py:130
  284.6 10.0 %fusion.92 = f32[1024,960]{0,1:T(8,128)} fusion(bf16[1024,2560]{1,0:T(8,128)(2,1)} %get-tuple-element.124, bf16[480,2560]{1,0:T(8,128)(2,1)S(1)} %copy-done.47, bf16[480,2560]{1,0:T(8,128)(2,1)S(1)} %copy-done.70, pred[]{:T(512)S(6)} %eq.140), kind=kOutput, calls=%fused_computation.166 | convolution fusion | flops 5055283200 | bytes 14090241 | tf_op jit(solution)/shard_map/dot_general | solution.py:130
  294.6 6.9 convolution_convert_fusion.1
  301.5 9.6 %fusion.44 = bf16[1,1024,960]{1,2,0:T(8,128)(2,1)} fusion(f32[1024,960]{0,1:T(8,128)S(1)} %copy-done.7, bf16[1024,2560]{1,0:T(8,128)(2,1)} %get-tuple-element.125, bf16[1280,960]{1,0:T(8,128)(2,1)S(1)} %copy-done.39, bf16[1280,960]{1,0:T(8,128)(2,1)S(1)} %copy-done.37, pred[]{:T(512)S(6)} %eq.140), kind=kOutput, calls=%fused_computation.94 | convolution fusion | flops 5057249280 | bytes 16056321 | tf_op jit(solution)/shard_map/dot_general | solution.py:130
  311.1 9.8 %convolution_convert_fusion = bf16[2560,960]{0,1:T(8,128)(2,1)} fusion(bf16[1024,2560]{1,0:T(8,128)(2,1)} %get-tuple-element.125, bf16[1,1024,960]{1,2,0:T(8,128)(2,1)} %param.23), kind=kOutput, calls=%fused_computation.37 | convolution fusion | flops 5035622400 | bytes 12124160 | tf_op jit(solution)/shard_map/dot_general | solution.py:130
  320.9 9.7 %convolution_convert_fusion.2 = bf16[960,2560]{1,0:T(8,128)(2,1)} fusion(bf16[1024,960]{0,1:T(8,128)(2,1)S(1)} %copy-done.60, bf16[1024,2560]{1,0:T(8,128)(2,1)} %get-tuple-element.123), kind=kOutput, calls=%fused_computation.39 | convolution fusion | flops 5035622400 | bytes 12124160 | tf_op jit(solution)/shard_map/dot_general | solution.py:130
  330.6 11.6 %multiply_reduce_fusion = (f32[960]{0:T(1024)}, f32[1024]{0:T(1024)S(1)}, f32[1024,960]{0,1:T(8,128)S(1)}) fusion(f32[1024,960]{0,1:T(8,128)S(1)} %copy-done.7, f32[1024]{0:T(1024)S(1)} %add_rsqrt_fusion, f32[960]{0:T(1024)S(1)} %get-tuple-element.121, f32[1024,960]{0,1:T(8,128)} %fusion.92, bf16[1024,2560]{1,0:T(8,128)(2,1)} %get-tuple-element.123, ...), kind=kOutput, calls=%fused_computation.66 | convolution fusion | flops 5062162432 | bytes 21970432 | tf_op jit(solution)/shard_map/dot_general | solution.py:130
  347.4 24.0 %fusion = (f32[5,3,512]{2,1,0:T(4,128)S(1)}, f32[5,1024,512,3]{2,1,3,0:T(8,128)}) fusion(f32[5,3,512,1024]{2,3,1,0:T(8,128)} %get-tuple-element.155, f32[5,3,512]{2,1,0:T(4,128)S(1)} %log_add_fusion, bf16[1024,5,64,1]{0,2,3,1:T(8,128)(2,1)S(1)} %copy-done.36, bf16[512,5,3,64]{0,3,2,1:T(8,128)(2,1)S(1)} %bitcast.304), kind=kOutput, calls=%fused_computation.2 | convolution fusion | flops 1030218240 | bytes 64614400 | tf_op jit(solution)/shard_map/while/body/eval_jaxpr/qgrd,kgd->grqk/dot_general | solution.py:102
  371.4 26.8 %fusion.2 = bf16[5,3,512,1024]{2,3,1,0:T(8,128)(2,1)} fusion(f32[5,1024,512,3]{2,1,3,0:T(8,128)} %get-tuple-element.162, f32[5,3,512,1024]{2,3,1,0:T(8,128)} %get-tuple-element.155, f32[5,3,512]{2,1,0:T(4,128)S(1)} %get-tuple-element.161, f32[5,3,512]{2,1,0:T(4,128)S(1)} %log_add_fusion), kind=kLoop, calls=%fused_computation.4 | loop fusion | flops 31457280 | bytes 78704640 | tf_op jit(solution)/shard_map/while/body/eval_jaxpr/convert_element_type | solution.py:106
  398.1 11.4 %convolution_bitcast_fusion.1 = f32[5,64,1024]{2,1,0:T(8,128)} fusion(bf16[512,5,3,64]{0,3,2,1:T(8,128)(2,1)S(1)} %bitcast.301, bf16[5,3,512,1024]{2,3,1,0:T(8,128)(2,1)} %fusion.2), kind=kOutput, calls=%fused_computation.129 | convolution fusion | flops 1006632960 | bytes 18022400 | tf_op jit(solution)/shard_map/while/body/eval_jaxpr/grqk,qgrd->kgd/dot_general | solution.py:115
  409.6 9.6 %multiply_bitcast_fusion = f32[512,5,3,64]{0,3,2,1:T(8,128)} fusion(bf16[5,3,512,1024]{2,3,1,0:T(8,128)(2,1)} %fusion.2, bf16[1024,5,32]{0,2,1:T(8,128)(2,1)S(1)} %copy-done.21, bf16[1024,5,32]{0,2,1:T(8,128)(2,1)S(1)} %copy-done.18), kind=kOutput, calls=%fused_computation.112 | convolution fusion | flops 1008435200 | bytes 18350080 | tf_op jit(solution)/shard_map/while/body/eval_jaxpr/grqk,kgd->qgrd/dot_general | solution.py:108
  419.2 13.5 %fusion.63 = f32[5,64,1024]{2,1,0:T(8,128)} fusion(bf16[512,5,3,64]{0,3,2,1:T(8,128)(2,1)S(1)} %bitcast.302, f32[5,3,512,1024]{2,3,1,0:T(8,128)} %get-tuple-element.157, f32[5,3,512]{2,1,0:T(4,128)S(1)} %copy-done.64), kind=kOutput, calls=%fused_computation.126 | convolution fusion | flops 1022361600 | bytes 33781760 | tf_op jit(solution)/shard_map/while/body/eval_jaxpr/grqk,qgrd->kgd/dot_general | solution.py:120
  432.7 23.6 %fusion.3 = (f32[5,3,512]{2,1,0:T(4,128)S(1)}, f32[5,1024,512,3]{2,1,3,0:T(8,128)}) fusion(f32[5,3,512,1024]{2,3,1,0:T(8,128)} %get-tuple-element.157, f32[5,3,512]{2,1,0:T(4,128)S(1)} %copy-done.64, bf16[1024,5,64,1]{0,2,3,1:T(8,128)(2,1)S(1)} %copy-done.36, bf16[512,5,3,64]{0,3,2,1:T(8,128)(2,1)S(1)} %bitcast.303), kind=kOutput, calls=%fused_computation.7 | convolution fusion | flops 1030218240 | bytes 64614400 | tf_op jit(solution)/shard_map/while/body/eval_jaxpr/qgrd,kgd->grqk/dot_general | solution.py:102
  456.3 10.9 %reshape.1718 = bf16[2,1280,960]{1,0,2:T(2,128)(2,1)} reshape(bf16[2560,960]{0,1:T(8,128)(2,1)} %convolution_convert_fusion) | data formatting | bytes 9830400 | tf_op jit(solution)/shard_map/reshape | solution.py:208
  467.2 6.3 fusion.56
  473.6 14.3 %fusion.75 = bf16[5,64,1024]{2,1,0:T(8,128)(2,1)} fusion(f32[5,64,1024]{2,1,0:T(8,128)} %fusion.63, bf16[512,5,3,64]{0,3,2,1:T(8,128)(2,1)} %bitcast.305, f32[5,3,512,1024]{2,3,1,0:T(8,128)} %get-tuple-element.155, f32[5,3,512]{2,1,0:T(4,128)S(1)} %log_add_fusion), kind=kOutput, calls=%fused_computation.132 | convolution fusion | flops 1023016960 | bytes 34437120 | tf_op jit(solution)/shard_map/while/body/eval_jaxpr/grqk,qgrd->kgd/dot_general | solution.py:120
  488.0 4.9 constant_dynamic-slice_fusion.5
  500.5 26.9 %fusion.5 = bf16[5,3,512,1024]{2,3,1,0:T(8,128)(2,1)} fusion(f32[5,1024,512,3]{2,1,3,0:T(8,128)} %get-tuple-element.164, f32[5,3,512,1024]{2,3,1,0:T(8,128)} %get-tuple-element.157, f32[5,3,512]{2,1,0:T(4,128)S(1)} %get-tuple-element.163, f32[5,3,512]{2,1,0:T(4,128)S(1)} %copy-done.64), kind=kLoop, calls=%fused_computation.9 | loop fusion | flops 31457280 | bytes 78704640 | tf_op jit(solution)/shard_map/while/body/eval_jaxpr/convert_element_type | solution.py:106
  527.5 8.4 %multiply_bitcast_fusion.1 = f32[512,5,3,64]{0,3,2,1:T(8,128)S(1)} fusion(bf16[5,3,512,1024]{2,3,1,0:T(8,128)(2,1)} %fusion.5, bf16[1024,5,32]{0,2,1:T(8,128)(2,1)S(1)} %copy-done.22, bf16[1024,5,32]{0,2,1:T(8,128)(2,1)S(1)} %copy-done.19), kind=kOutput, calls=%fused_computation.113 | convolution fusion | flops 1008435200 | bytes 18350080 | tf_op jit(solution)/shard_map/while/body/eval_jaxpr/grqk,kgd->qgrd/dot_general | solution.py:108
  535.9 11.4 %fusion.85 = f32[1,1024,5,64]{1,3,2,0:T(8,128)} fusion(f32[5,64,1024]{2,1,0:T(8,128)S(1)} %copy-done.25, bf16[512,5,3,64]{0,3,2,1:T(8,128)(2,1)S(1)} %bitcast.299, bf16[5,3,512,1024]{2,3,1,0:T(8,128)(2,1)} %fusion.5), kind=kOutput, calls=%fused_computation.140 | convolution fusion | flops 1007288320 | bytes 19333120 | tf_op jit(solution)/shard_map/while/body/eval_jaxpr/grqk,qgrd->kgd/dot_general | solution.py:115
  556.2 3.6 fusion.34
  559.9 3.5 convolution_convert_fusion.4
  573.0 8.7 %concatenate.803 = bf16[2,480,2560]{2,1,0:T(8,128)(2,1)} concatenate(bf16[2,480,960]{2,1,0:T(8,128)(2,1)} %convolution_convert_fusion.4, bf16[2,480,320]{2,1,0:T(8,128)(2,1)S(1)} %copy.139, bf16[2,480,320]{2,1,0:T(8,128)(2,1)S(1)} %copy.140, bf16[2,480,960]{2,1,0:T(8,128)(2,1)} %fusion.56), dimensions={2} | concatenate | bytes 9830400 | tf_op jit(solution)/shard_map/concatenate | solution.py:380
  592.8 4.4 fusion.45
  597.2 5.9 copy.164
  613.1 4.4 copy.143
  625.2 11.3 %collective-permute-done.37 = bf16[2,240,1280]{2,1,0:T(8,128)(2,1)} collective-permute-done((bf16[2,240,1280]{2,1,0:T(8,128)(2,1)}, bf16[2,240,1280]{2,1,0:T(8,128)(2,1)}, u32[]{:S(2)}, u32[]{:S(2)}) %collective-permute-start.37) | collective-permute-done | bytes 1228832 | tf_op jit(solution)/shard_map/ppermute | solution.py:143
  638.7 4.0 collective-permute-done.29
  645.0 7.6 collective-permute-done.45
  654.6 14.3 %collective-permute-done.21 = bf16[1,480,1280]{2,1,0:T(8,128)(2,1)S(1)} collective-permute-done((bf16[1,480,1280]{2,1,0:T(8,128)(2,1)S(1)}, bf16[1,480,1280]{2,1,0:T(8,128)(2,1)S(1)}, u32[]{:S(2)}, u32[]{:S(2)}) %collective-permute-start.21) | collective-permute-done | bytes 1228832 | tf_op jit(solution)/shard_map/ppermute | solution.py:147
  671.5 5.2 collective-permute-done.30
  678.2 4.7 collective-permute-done.46
  690.1 6.7 collective-permute-done.31
  697.0 5.1 collective-permute-done.47
  705.4 20.0 %collective-permute-done.40 = bf16[1,240,640]{2,1,0:T(8,128)(2,1)S(1)} collective-permute-done((bf16[1,240,640]{2,1,0:T(8,128)(2,1)S(1)}, bf16[1,240,640]{2,1,0:T(8,128)(2,1)S(1)}, u32[]{:S(2)}, u32[]{:S(2)}) %collective-permute-start.40) | collective-permute-done | bytes 307232 | tf_op jit(solution)/shard_map/ppermute | solution.py:143
  726.0 6.1 collective-permute-done.32
  732.3 6.9 collective-permute-done.48
  744.0 5.2 collective-permute-done.33
  750.7 5.5 collective-permute-done.49
  758.8 10.6 %collective-permute-done.42 = bf16[1,240,1280]{2,1,0:T(8,128)(2,1)S(1)} collective-permute-done((bf16[1,240,1280]{2,1,0:T(8,128)(2,1)S(1)}, bf16[1,240,1280]{2,1,0:T(8,128)(2,1)S(1)}, u32[]{:S(2)}, u32[]{:S(2)}) %collective-permute-start.42) | collective-permute-done | bytes 614432 | tf_op jit(solution)/shard_map/ppermute | solution.py:143
  770.9 9.3 %collective-permute-done.50 = bf16[1,320,960]{2,1,0:T(8,128)(2,1)S(1)} collective-permute-done((bf16[1,320,960]{2,1,0:T(8,128)(2,1)S(1)}, bf16[1,320,960]{2,1,0:T(8,128)(2,1)S(1)}, u32[]{:S(2)}, u32[]{:S(2)}) %collective-permute-start.50) | collective-permute-done | bytes 614432 | tf_op jit(solution)/shard_map/ppermute | solution.py:143
  803.6 5.8 copy.148
  813.2 4.9 fusion.112
  818.1 4.8 fusion.41
  822.9 4.8 fusion.40
  (413 shorter events, 200.7 us)
Async XLA Ops:
  2.4 22.0 %collective-permute-start.3 = (bf16[1,120,960]{2,1,0:T(8,128)(2,1)}, bf16[1,120,960]{2,1,0:T(8,128)(2,1)S(1)}, u32[]{:S(2)}, u32[]{:S(2)}) collective-permute-start(bf16[1,120,960]{2,1,0:T(8,128)(2,1)} %dynamic-slice_bitcast_fusion.3), channel_id=1, source_target_pairs={{0,1},{1,0},{2,3},{3,2},{4,5},{5,4},{6,7},{7,6},{8,9},{9,8},{10,11... | collective-permute-start | bytes 691208 | tf_op jit(solution)/shard_map/ppermute | solution.py:147
  7.2 57.6 %collective-permute-start.9 = (bf16[1,120,2560]{2,1,0:T(8,128)(2,1)}, bf16[1,120,2560]{2,1,0:T(8,128)(2,1)}, u32[]{:S(2)}, u32[]{:S(2)}) collective-permute-start(bf16[1,120,2560]{2,1,0:T(8,128)(2,1)} %dynamic-slice_bitcast_fusion), channel_id=1, source_target_pairs={{0,1},{1,0},{2,3},{3,2},{4,5},{5,4},{6,7},{7,6},{8,9},{9,8},{10,11... | collective-permute-start | bytes 1843208 | tf_op jit(solution)/shard_map/ppermute | solution.py:147
  9.3 55.9 %collective-permute-start.6 = (bf16[1,120,2560]{2,1,0:T(8,128)(2,1)}, bf16[1,120,2560]{2,1,0:T(8,128)(2,1)}, u32[]{:S(2)}, u32[]{:S(2)}) collective-permute-start(bf16[1,120,2560]{2,1,0:T(8,128)(2,1)} %dynamic-slice_bitcast_fusion.1), channel_id=1, source_target_pairs={{0,1},{1,0},{2,3},{3,2},{4,5},{5,4},{6,7},{7,6},{8,9},{9,8},{10,11... | collective-permute-start | bytes 1843208 | tf_op jit(solution)/shard_map/ppermute | solution.py:147
  13.8 53.1 %collective-permute-start.12 = (bf16[1,320,960]{2,1,0:T(8,128)(2,1)}, bf16[1,320,960]{2,1,0:T(8,128)(2,1)}, u32[]{:S(2)}, u32[]{:S(2)}) collective-permute-start(bf16[1,320,960]{2,1,0:T(8,128)(2,1)} %bitcast.48), channel_id=1, source_target_pairs={{0,1},{1,0},{2,3},{3,2},{4,5},{5,4},{6,7},{7,6},{8,9},{9,8},{10,11... | collective-permute-start | bytes 1843208 | tf_op jit(solution)/shard_map/ppermute | solution.py:147
  20.3 40.2 %collective-permute-start = (bf16[1,120,1664]{2,1,0:T(8,128)(2,1)}, bf16[1,120,1664]{2,1,0:T(8,128)(2,1)}, u32[]{:S(2)}, u32[]{:S(2)}) collective-permute-start(bf16[1,120,1664]{2,1,0:T(8,128)(2,1)} %dynamic-slice_bitcast_fusion.2), channel_id=1, source_target_pairs={{0,1},{1,0},{2,3},{3,2},{4,5},{5,4},{6,7},{7,6},{8,9},{9,8},{10,11... | collective-permute-start | bytes 1198088 | tf_op jit(solution)/shard_map/ppermute | solution.py:147
  24.4 37.9 %collective-permute-start.4 = (bf16[1,120,960]{2,1,0:T(8,128)(2,1)S(1)}, bf16[1,120,960]{2,1,0:T(8,128)(2,1)}, u32[]{:S(2)}, u32[]{:S(2)}) collective-permute-start(bf16[1,120,960]{2,1,0:T(8,128)(2,1)S(1)} %collective-permute-done.3), channel_id=1, source_target_pairs={{0,4},{2,6},{4,0},{6,2},{8,12},{10,14},{12,8},{14,10},{16,20},{18,... | collective-permute-start | bytes 691208 | tf_op jit(solution)/shard_map/ppermute | solution.py:143
  26.5 126.0 %copy-start.31 = (f32[1024,32]{0,1:T(8,128)}, f32[1024,32]{0,1:T(8,128)S(1)}, u32[]{:S(2)}) copy-start(f32[1024,32]{0,1:T(8,128)S(1)} %get-tuple-element.146) | copy-start | bytes 393220
  26.5 126.0 %copy-start.33 = (f32[1024,32]{0,1:T(8,128)}, f32[1024,32]{0,1:T(8,128)S(1)}, u32[]{:S(2)}) copy-start(f32[1024,32]{0,1:T(8,128)S(1)} %get-tuple-element.147) | copy-start | bytes 393220
  60.5 12.4 %collective-permute-start.1 = (bf16[1,120,1664]{2,1,0:T(8,128)(2,1)}, bf16[1,120,1664]{2,1,0:T(8,128)(2,1)S(1)}, u32[]{:S(2)}, u32[]{:S(2)}) collective-permute-start(bf16[1,120,1664]{2,1,0:T(8,128)(2,1)} %collective-permute-done), channel_id=1, source_target_pairs={{0,4},{2,6},{4,0},{6,2},{8,12},{10,14},{12,8},{14,10},{16,20},{18,... | collective-permute-start | bytes 1198088 | tf_op jit(solution)/shard_map/ppermute | solution.py:143
  62.3 77.0 %copy-start.75 = (f32[1024]{0:T(1024)}, f32[1024]{0:T(1024)S(1)}, u32[]{:S(2)}) copy-start(f32[1024]{0:T(1024)S(1)} %add_rsqrt_fusion.1) | copy-start | bytes 12292
  63.5 13.8 %collective-permute-start.5 = (bf16[1,240,960]{2,1,0:T(8,128)(2,1)S(1)}, bf16[1,240,960]{2,1,0:T(8,128)(2,1)S(1)}, u32[]{:S(2)}, u32[]{:S(2)}) collective-permute-start(bf16[1,240,960]{2,1,0:T(8,128)(2,1)S(1)} %maximum_select_fusion.45), channel_id=1, source_target_pairs={{0,2},{2,0},{4,6},{6,4},{8,10},{10,8},{12,14},{14,12},{16,18},{18,... | collective-permute-start | bytes 1382408 | tf_op jit(solution)/shard_map/ppermute | solution.py:143
  64.8 21.2 %collective-permute-start.10 = (bf16[1,120,2560]{2,1,0:T(8,128)(2,1)}, bf16[1,120,2560]{2,1,0:T(8,128)(2,1)S(1)}, u32[]{:S(2)}, u32[]{:S(2)}) collective-permute-start(bf16[1,120,2560]{2,1,0:T(8,128)(2,1)} %collective-permute-done.9), channel_id=1, source_target_pairs={{0,4},{2,6},{4,0},{6,2},{8,12},{10,14},{12,8},{14,10},{16,20},{18,... | collective-permute-start | bytes 1843208 | tf_op jit(solution)/shard_map/ppermute | solution.py:143
  65.2 34.1 %collective-permute-start.7 = (bf16[1,120,2560]{2,1,0:T(8,128)(2,1)}, bf16[1,120,2560]{2,1,0:T(8,128)(2,1)S(1)}, u32[]{:S(2)}, u32[]{:S(2)}) collective-permute-start(bf16[1,120,2560]{2,1,0:T(8,128)(2,1)} %collective-permute-done.6), channel_id=1, source_target_pairs={{0,4},{2,6},{4,0},{6,2},{8,12},{10,14},{12,8},{14,10},{16,20},{18,... | collective-permute-start | bytes 1843208 | tf_op jit(solution)/shard_map/ppermute | solution.py:143
  66.9 44.6 %collective-permute-start.13 = (bf16[1,320,960]{2,1,0:T(8,128)(2,1)}, bf16[1,320,960]{2,1,0:T(8,128)(2,1)S(1)}, u32[]{:S(2)}, u32[]{:S(2)}) collective-permute-start(bf16[1,320,960]{2,1,0:T(8,128)(2,1)} %collective-permute-done.12), channel_id=1, source_target_pairs={{0,4},{2,6},{4,0},{6,2},{8,12},{10,14},{12,8},{14,10},{16,20},{18,... | collective-permute-start | bytes 1843208 | tf_op jit(solution)/shard_map/ppermute | solution.py:143
  75.1 49.3 %collective-permute-start.2 = (bf16[1,240,1664]{2,1,0:T(8,128)(2,1)}, bf16[1,240,1664]{2,1,0:T(8,128)(2,1)}, u32[]{:S(2)}, u32[]{:S(2)}) collective-permute-start(bf16[1,240,1664]{2,1,0:T(8,128)(2,1)} %maximum_select_fusion.35), channel_id=1, source_target_pairs={{0,2},{2,0},{4,6},{6,4},{8,10},{10,8},{12,14},{14,12},{16,18},{18,... | collective-permute-start | bytes 2396168 | tf_op jit(solution)/shard_map/ppermute | solution.py:143
  88.9 148.1 %collective-permute-start.11 = (bf16[1,240,2560]{2,1,0:T(8,128)(2,1)}, bf16[1,240,2560]{2,1,0:T(8,128)(2,1)}, u32[]{:S(2)}, u32[]{:S(2)}) collective-permute-start(bf16[1,240,2560]{2,1,0:T(8,128)(2,1)} %maximum_select_fusion.20), channel_id=1, source_target_pairs={{0,2},{2,0},{4,6},{6,4},{8,10},{10,8},{12,14},{14,12},{16,18},{18,... | collective-permute-start | bytes 3686408 | tf_op jit(solution)/shard_map/ppermute | solution.py:143
  102.0 146.7 %collective-permute-start.8 = (bf16[1,240,2560]{2,1,0:T(8,128)(2,1)}, bf16[1,240,2560]{2,1,0:T(8,128)(2,1)}, u32[]{:S(2)}, u32[]{:S(2)}) collective-permute-start(bf16[1,240,2560]{2,1,0:T(8,128)(2,1)} %maximum_select_fusion.18), channel_id=1, source_target_pairs={{0,2},{2,0},{4,6},{6,4},{8,10},{10,8},{12,14},{14,12},{16,18},{18,... | collective-permute-start | bytes 3686408 | tf_op jit(solution)/shard_map/ppermute | solution.py:143
  117.6 141.8 %collective-permute-start.14 = (bf16[1,640,960]{1,2,0:T(8,128)(2,1)}, bf16[1,640,960]{1,2,0:T(8,128)(2,1)}, u32[]{:S(2)}, u32[]{:S(2)}) collective-permute-start(bf16[1,640,960]{1,2,0:T(8,128)(2,1)} %copy.128), channel_id=1, source_target_pairs={{0,2},{2,0},{4,6},{6,4},{8,10},{10,8},{12,14},{14,12},{16,18},{18,... | collective-permute-start | bytes 3686408 | tf_op jit(solution)/shard_map/ppermute | solution.py:143
  152.5 39.5 %copy-start.17 = (bf16[1024,5,32]{0,2,1:T(8,128)(2,1)}, bf16[1024,5,32]{0,2,1:T(8,128)(2,1)S(1)}, u32[]{:S(2)}) copy-start(bf16[1024,5,32]{0,2,1:T(8,128)(2,1)S(1)} %get-tuple-element.144) | copy-start | bytes 983044
  152.5 39.5 %copy-start.20 = (bf16[1024,5,32]{0,2,1:T(8,128)(2,1)}, bf16[1024,5,32]{0,2,1:T(8,128)(2,1)S(1)}, u32[]{:S(2)}) copy-start(bf16[1024,5,32]{0,2,1:T(8,128)(2,1)S(1)} %get-tuple-element.145) | copy-start | bytes 983044
  153.4 38.6 %copy-start.8 = (bf16[1,512,15,64]{1,3,2,0:T(8,128)(2,1)}, bf16[1,512,15,64]{1,3,2,0:T(8,128)(2,1)S(1)}, u32[]{:S(2)}) copy-start(bf16[1,512,15,64]{1,3,2,0:T(8,128)(2,1)S(1)} %get-tuple-element.140) | copy-start | bytes 2949124
  263.5 21.0 %copy-start.47 = (bf16[480,2560]{1,0:T(8,128)(2,1)S(1)}, bf16[480,2560]{1,0:T(8,128)(2,1)}, u32[]{:S(2)}) copy-start(bf16[480,2560]{1,0:T(8,128)(2,1)} %copy-done.46) | copy-start | bytes 7372804
  263.5 21.1 %copy-start.70 = (bf16[480,2560]{1,0:T(8,128)(2,1)S(1)}, bf16[480,2560]{1,0:T(8,128)(2,1)}, u32[]{:S(2)}) copy-start(bf16[480,2560]{1,0:T(8,128)(2,1)} %param.21) | copy-start | bytes 7372804
  347.4 24.0 %copy-start.16 = (bf16[512,960]{0,1:T(8,128)(2,1)}, bf16[512,960]{0,1:T(8,128)(2,1)S(1)}, u32[]{:S(2)}) copy-start(bf16[512,960]{0,1:T(8,128)(2,1)S(1)} %get-tuple-element.139) | copy-start | bytes 2949124
  371.4 26.8 %copy-start.11 = (bf16[1,512,15,64]{1,3,2,0:T(8,128)(2,1)S(1)}, bf16[1,512,15,64]{1,3,2,0:T(8,128)(2,1)}, u32[]{:S(2)}) copy-start(bf16[1,512,15,64]{1,3,2,0:T(8,128)(2,1)} %copy-done.10) | copy-start | bytes 2949124
  499.5 104.3 %collective-permute-start.36 = (bf16[2,480,1280]{2,1,0:T(8,128)(2,1)}, bf16[2,480,1280]{2,1,0:T(8,128)(2,1)}, u32[]{:S(2)}, u32[]{:S(2)}) collective-permute-start(bf16[2,480,1280]{2,1,0:T(8,128)(2,1)} %constant_dynamic-slice_fusion.9), channel_id=1, source_target_pairs={{0,2},{2,0},{4,6},{6,4},{8,10},{10,8},{12,14},{14,12},{16,18},{18,... | collective-permute-start | bytes 7372808 | tf_op jit(solution)/shard_map/ppermute | solution.py:143
  500.0 108.9 %collective-permute-start.28 = (bf16[2,480,1280]{2,1,0:T(8,128)(2,1)}, bf16[2,480,1280]{2,1,0:T(8,128)(2,1)}, u32[]{:S(2)}, u32[]{:S(2)}) collective-permute-start(bf16[2,480,1280]{2,1,0:T(8,128)(2,1)} %constant_dynamic-slice_fusion.13), channel_id=1, source_target_pairs={{0,2},{2,0},{4,6},{6,4},{8,10},{10,8},{12,14},{14,12},{16,18},{18,... | collective-permute-start | bytes 7372808 | tf_op jit(solution)/shard_map/ppermute | solution.py:143
  500.0 113.0 %collective-permute-start.44 = (bf16[2,640,960]{1,2,0:T(8,128)(2,1)}, bf16[2,640,960]{1,2,0:T(8,128)(2,1)}, u32[]{:S(2)}, u32[]{:S(2)}) collective-permute-start(bf16[2,640,960]{1,2,0:T(8,128)(2,1)} %copy.165), channel_id=1, source_target_pairs={{0,2},{2,0},{4,6},{6,4},{8,10},{10,8},{12,14},{14,12},{16,18},{18,... | collective-permute-start | bytes 7372808 | tf_op jit(solution)/shard_map/ppermute | solution.py:143
  500.5 26.9 %copy-start.19 = (bf16[1024,5,32]{0,2,1:T(8,128)(2,1)S(1)}, bf16[1024,5,32]{0,2,1:T(8,128)(2,1)}, u32[]{:S(2)}) copy-start(bf16[1024,5,32]{0,2,1:T(8,128)(2,1)} %copy-done.17) | copy-start | bytes 983044
  500.5 26.9 %copy-start.22 = (bf16[1024,5,32]{0,2,1:T(8,128)(2,1)S(1)}, bf16[1024,5,32]{0,2,1:T(8,128)(2,1)}, u32[]{:S(2)}) copy-start(bf16[1024,5,32]{0,2,1:T(8,128)(2,1)} %copy-done.20) | copy-start | bytes 983044
  559.8 7.0 collective-permute-start.15
  566.8 14.9 %collective-permute-start.16 = (f32[2,960]{1,0:T(2,128)S(1)}, f32[2,960]{1,0:T(2,128)S(1)}, u32[]{:S(2)}, u32[]{:S(2)}) collective-permute-start(f32[2,960]{1,0:T(2,128)S(1)} %fusion.111), channel_id=1, source_target_pairs={{0,4},{2,6},{4,0},{6,2},{8,12},{10,14},{12,8},{14,10},{16,20},{18,... | collective-permute-start | bytes 23048 | tf_op jit(solution)/shard_map/ppermute | solution.py:143
  581.7 4.9 collective-permute-start.17
  586.7 34.7 %collective-permute-start.20 = (bf16[2,480,1280]{2,1,0:T(8,128)(2,1)}, bf16[2,480,1280]{2,1,0:T(8,128)(2,1)}, u32[]{:S(2)}, u32[]{:S(2)}) collective-permute-start(bf16[2,480,1280]{2,1,0:T(8,128)(2,1)} %constant_dynamic-slice_fusion.17), channel_id=1, source_target_pairs={{0,2},{2,0},{4,6},{6,4},{8,10},{10,8},{12,14},{14,12},{16,18},{18,... | collective-permute-start | bytes 7372808 | tf_op jit(solution)/shard_map/ppermute | solution.py:143
  586.7 4.6 collective-permute-start.18
  591.3 11.8 %collective-permute-start.19 = (f32[2,960]{1,0:T(2,128)S(1)}, f32[2,960]{1,0:T(2,128)S(1)}, u32[]{:S(2)}, u32[]{:S(2)}) collective-permute-start(f32[2,960]{1,0:T(2,128)S(1)} %add.340), channel_id=1, source_target_pairs={{0,1},{1,0},{2,3},{3,2},{4,5},{5,4},{6,7},{7,6},{8,9},{9,8},{10,11... | collective-permute-start | bytes 23048 | tf_op jit(solution)/shard_map/ppermute | solution.py:147
  608.2 28.3 %collective-permute-start.37 = (bf16[2,240,1280]{2,1,0:T(8,128)(2,1)}, bf16[2,240,1280]{2,1,0:T(8,128)(2,1)}, u32[]{:S(2)}, u32[]{:S(2)}) collective-permute-start(bf16[2,240,1280]{2,1,0:T(8,128)(2,1)} %constant_dynamic-slice_fusion.8), channel_id=1, source_target_pairs={{0,8},{2,10},{4,12},{6,14},{8,0},{10,2},{12,4},{14,6},{16,24},{18,... | collective-permute-start | bytes 3686408 | tf_op jit(solution)/shard_map/ppermute | solution.py:143
  612.4 30.3 %collective-permute-start.29 = (bf16[1,480,1280]{2,1,0:T(8,128)(2,1)}, bf16[1,480,1280]{2,1,0:T(8,128)(2,1)}, u32[]{:S(2)}, u32[]{:S(2)}) collective-permute-start(bf16[1,480,1280]{2,1,0:T(8,128)(2,1)} %constant_dynamic-slice_fusion.12), channel_id=1, source_target_pairs={{0,1},{1,0},{2,3},{3,2},{4,5},{5,4},{6,7},{7,6},{8,9},{9,8},{10,11... | collective-permute-start | bytes 3686408 | tf_op jit(solution)/shard_map/ppermute | solution.py:147
  620.7 31.8 %collective-permute-start.45 = (bf16[2,320,960]{2,1,0:T(8,128)(2,1)S(1)}, bf16[2,320,960]{2,1,0:T(8,128)(2,1)S(1)}, u32[]{:S(2)}, u32[]{:S(2)}) collective-permute-start(bf16[2,320,960]{2,1,0:T(8,128)(2,1)S(1)} %constant_dynamic-slice_fusion.3), channel_id=1, source_target_pairs={{0,4},{2,6},{4,0},{6,2},{8,12},{10,14},{12,8},{14,10},{16,20},{18,... | collective-permute-start | bytes 3686408 | tf_op jit(solution)/shard_map/ppermute | solution.py:143
  623.8 45.2 %collective-permute-start.21 = (bf16[1,480,1280]{2,1,0:T(8,128)(2,1)S(1)}, bf16[1,480,1280]{2,1,0:T(8,128)(2,1)S(1)}, u32[]{:S(2)}, u32[]{:S(2)}) collective-permute-start(bf16[1,480,1280]{2,1,0:T(8,128)(2,1)S(1)} %constant_dynamic-slice_fusion.16), channel_id=1, source_target_pairs={{0,1},{1,0},{2,3},{3,2},{4,5},{5,4},{6,7},{7,6},{8,9},{9,8},{10,11... | collective-permute-start | bytes 3686408 | tf_op jit(solution)/shard_map/ppermute | solution.py:147
  638.2 32.5 %collective-permute-start.38 = (bf16[2,240,640]{2,1,0:T(8,128)(2,1)S(1)}, bf16[2,240,640]{2,1,0:T(8,128)(2,1)S(1)}, u32[]{:S(2)}, u32[]{:S(2)}) collective-permute-start(bf16[2,240,640]{2,1,0:T(8,128)(2,1)S(1)} %constant_dynamic-slice_fusion.7), channel_id=1, source_target_pairs={{0,4},{2,6},{4,0},{6,2},{8,12},{10,14},{12,8},{14,10},{16,20},{18,... | collective-permute-start | bytes 1843208 | tf_op jit(solution)/shard_map/ppermute | solution.py:143
  644.4 32.3 %collective-permute-start.30 = (bf16[1,480,640]{2,1,0:T(8,128)(2,1)S(1)}, bf16[1,480,640]{2,1,0:T(8,128)(2,1)S(1)}, u32[]{:S(2)}, u32[]{:S(2)}) collective-permute-start(bf16[1,480,640]{2,1,0:T(8,128)(2,1)S(1)} %constant_dynamic-slice_fusion.11), channel_id=1, source_target_pairs={{0,4},{2,6},{4,0},{6,2},{8,12},{10,14},{12,8},{14,10},{16,20},{18,... | collective-permute-start | bytes 1843208 | tf_op jit(solution)/shard_map/ppermute | solution.py:143
  653.1 29.8 %collective-permute-start.46 = (bf16[1,320,960]{2,1,0:T(8,128)(2,1)S(1)}, bf16[1,320,960]{2,1,0:T(8,128)(2,1)S(1)}, u32[]{:S(2)}, u32[]{:S(2)}) collective-permute-start(bf16[1,320,960]{2,1,0:T(8,128)(2,1)S(1)} %constant_dynamic-slice_fusion.2), channel_id=1, source_target_pairs={{0,1},{1,0},{2,3},{3,2},{4,5},{5,4},{6,7},{7,6},{8,9},{9,8},{10,11... | collective-permute-start | bytes 1843208 | tf_op jit(solution)/shard_map/ppermute | solution.py:147
  669.3 15.3 %collective-permute-start.22 = (bf16[1,240,1280]{2,1,0:T(8,128)(2,1)S(1)}, bf16[1,240,1280]{2,1,0:T(8,128)(2,1)S(1)}, u32[]{:S(2)}, u32[]{:S(2)}) collective-permute-start(bf16[1,240,1280]{2,1,0:T(8,128)(2,1)S(1)} %constant_dynamic-slice_fusion.15), channel_id=1, source_target_pairs={{0,8},{2,10},{4,12},{6,14},{8,0},{10,2},{12,4},{14,6},{16,24},{18,... | collective-permute-start | bytes 1843208 | tf_op jit(solution)/shard_map/ppermute | solution.py:143
  670.9 16.5 %collective-permute-start.39 = (bf16[1,240,640]{2,1,0:T(8,128)(2,1)S(1)}, bf16[1,240,640]{2,1,0:T(8,128)(2,1)S(1)}, u32[]{:S(2)}, u32[]{:S(2)}) collective-permute-start(bf16[1,240,640]{2,1,0:T(8,128)(2,1)S(1)} %constant_dynamic-slice_fusion.6), channel_id=1, source_target_pairs={{0,1},{1,0},{2,3},{3,2},{4,5},{5,4},{6,7},{7,6},{8,9},{9,8},{10,11... | collective-permute-start | bytes 921608 | tf_op jit(solution)/shard_map/ppermute | solution.py:147
  676.9 20.0 %collective-permute-start.31 = (bf16[1,240,640]{2,1,0:T(8,128)(2,1)S(1)}, bf16[1,240,640]{2,1,0:T(8,128)(2,1)S(1)}, u32[]{:S(2)}, u32[]{:S(2)}) collective-permute-start(bf16[1,240,640]{2,1,0:T(8,128)(2,1)S(1)} %constant_dynamic-slice_fusion.10), channel_id=1, source_target_pairs={{0,8},{2,10},{4,12},{6,14},{8,0},{10,2},{12,4},{14,6},{16,24},{18,... | collective-permute-start | bytes 921608 | tf_op jit(solution)/shard_map/ppermute | solution.py:143
  683.3 18.9 %collective-permute-start.47 = (bf16[1,160,960]{2,1,0:T(8,128)(2,1)S(1)}, bf16[1,160,960]{2,1,0:T(8,128)(2,1)S(1)}, u32[]{:S(2)}, u32[]{:S(2)}) collective-permute-start(bf16[1,160,960]{2,1,0:T(8,128)(2,1)S(1)} %constant_dynamic-slice_fusion.1), channel_id=1, source_target_pairs={{0,8},{2,10},{4,12},{6,14},{8,0},{10,2},{12,4},{14,6},{16,24},{18,... | collective-permute-start | bytes 921608 | tf_op jit(solution)/shard_map/ppermute | solution.py:143
  684.8 17.5 %collective-permute-start.23 = (bf16[1,240,640]{2,1,0:T(8,128)(2,1)S(1)}, bf16[1,240,640]{2,1,0:T(8,128)(2,1)S(1)}, u32[]{:S(2)}, u32[]{:S(2)}) collective-permute-start(bf16[1,240,640]{2,1,0:T(8,128)(2,1)S(1)} %constant_dynamic-slice_fusion.14), channel_id=1, source_target_pairs={{0,4},{2,6},{4,0},{6,2},{8,12},{10,14},{12,8},{14,10},{16,20},{18,... | collective-permute-start | bytes 921608 | tf_op jit(solution)/shard_map/ppermute | solution.py:143
  687.5 38.0 %collective-permute-start.40 = (bf16[1,240,640]{2,1,0:T(8,128)(2,1)S(1)}, bf16[1,240,640]{2,1,0:T(8,128)(2,1)S(1)}, u32[]{:S(2)}, u32[]{:S(2)}) collective-permute-start(bf16[1,240,640]{2,1,0:T(8,128)(2,1)S(1)} %add_convert_fusion.18), channel_id=1, source_target_pairs={{0,16},{2,18},{4,20},{6,22},{8,24},{10,26},{12,28},{14,30},{16,0},... | collective-permute-start | bytes 921608 | tf_op jit(solution)/shard_map/ppermute | solution.py:143
  696.9 35.2 %collective-permute-start.32 = (bf16[1,240,640]{2,1,0:T(8,128)(2,1)S(1)}, bf16[1,240,640]{2,1,0:T(8,128)(2,1)S(1)}, u32[]{:S(2)}, u32[]{:S(2)}) collective-permute-start(bf16[1,240,640]{2,1,0:T(8,128)(2,1)S(1)} %add_convert_fusion.20), channel_id=1, source_target_pairs={{0,16},{2,18},{4,20},{6,22},{8,24},{10,26},{12,28},{14,30},{16,0},... | collective-permute-start | bytes 921608 | tf_op jit(solution)/shard_map/ppermute | solution.py:143
  702.2 36.9 %collective-permute-start.48 = (bf16[1,160,960]{2,1,0:T(8,128)(2,1)S(1)}, bf16[1,160,960]{2,1,0:T(8,128)(2,1)S(1)}, u32[]{:S(2)}, u32[]{:S(2)}) collective-permute-start(bf16[1,160,960]{2,1,0:T(8,128)(2,1)S(1)} %add_convert_fusion.15), channel_id=1, source_target_pairs={{0,16},{2,18},{4,20},{6,22},{8,24},{10,26},{12,28},{14,30},{16,0},... | collective-permute-start | bytes 921608 | tf_op jit(solution)/shard_map/ppermute | solution.py:143
  702.4 40.2 %collective-permute-start.24 = (bf16[1,240,640]{2,1,0:T(8,128)(2,1)S(1)}, bf16[1,240,640]{2,1,0:T(8,128)(2,1)S(1)}, u32[]{:S(2)}, u32[]{:S(2)}) collective-permute-start(bf16[1,240,640]{2,1,0:T(8,128)(2,1)S(1)} %add_convert_fusion.22), channel_id=1, source_target_pairs={{0,16},{2,18},{4,20},{6,22},{8,24},{10,26},{12,28},{14,30},{16,0},... | collective-permute-start | bytes 921608 | tf_op jit(solution)/shard_map/ppermute | solution.py:143
  725.5 17.8 %collective-permute-start.41 = (bf16[1,240,640]{2,1,0:T(8,128)(2,1)S(1)}, bf16[1,240,640]{2,1,0:T(8,128)(2,1)S(1)}, u32[]{:S(2)}, u32[]{:S(2)}) collective-permute-start(bf16[1,240,640]{2,1,0:T(8,128)(2,1)S(1)} %add_convert_fusion.17), channel_id=1, source_target_pairs={{0,4},{2,6},{4,0},{6,2},{8,12},{10,14},{12,8},{14,10},{16,20},{18,... | collective-permute-start | bytes 921608 | tf_op jit(solution)/shard_map/ppermute | solution.py:143
  732.2 17.0 %collective-permute-start.33 = (bf16[1,240,640]{2,1,0:T(8,128)(2,1)S(1)}, bf16[1,240,640]{2,1,0:T(8,128)(2,1)S(1)}, u32[]{:S(2)}, u32[]{:S(2)}) collective-permute-start(bf16[1,240,640]{2,1,0:T(8,128)(2,1)S(1)} %add_convert_fusion.19), channel_id=1, source_target_pairs={{0,8},{2,10},{4,12},{6,14},{8,0},{10,2},{12,4},{14,6},{16,24},{18,... | collective-permute-start | bytes 921608 | tf_op jit(solution)/shard_map/ppermute | solution.py:143
  739.2 17.0 %collective-permute-start.49 = (bf16[1,160,960]{2,1,0:T(8,128)(2,1)S(1)}, bf16[1,160,960]{2,1,0:T(8,128)(2,1)S(1)}, u32[]{:S(2)}, u32[]{:S(2)}) collective-permute-start(bf16[1,160,960]{2,1,0:T(8,128)(2,1)S(1)} %add_convert_fusion.14), channel_id=1, source_target_pairs={{0,8},{2,10},{4,12},{6,14},{8,0},{10,2},{12,4},{14,6},{16,24},{18,... | collective-permute-start | bytes 921608 | tf_op jit(solution)/shard_map/ppermute | solution.py:143
  742.7 14.3 %collective-permute-start.25 = (bf16[1,240,640]{2,1,0:T(8,128)(2,1)S(1)}, bf16[1,240,640]{2,1,0:T(8,128)(2,1)S(1)}, u32[]{:S(2)}, u32[]{:S(2)}) collective-permute-start(bf16[1,240,640]{2,1,0:T(8,128)(2,1)S(1)} %add_convert_fusion.21), channel_id=1, source_target_pairs={{0,4},{2,6},{4,0},{6,2},{8,12},{10,14},{12,8},{14,10},{16,20},{18,... | collective-permute-start | bytes 921608 | tf_op jit(solution)/shard_map/ppermute | solution.py:143
  743.5 25.9 %collective-permute-start.42 = (bf16[1,240,1280]{2,1,0:T(8,128)(2,1)S(1)}, bf16[1,240,1280]{2,1,0:T(8,128)(2,1)S(1)}, u32[]{:S(2)}, u32[]{:S(2)}) collective-permute-start(bf16[1,240,1280]{2,1,0:T(8,128)(2,1)S(1)} %maximum_select_fusion.43), channel_id=1, source_target_pairs={{0,8},{2,10},{4,12},{6,14},{8,0},{10,2},{12,4},{14,6},{16,24},{18,... | collective-permute-start | bytes 1843208 | tf_op jit(solution)/shard_map/ppermute | solution.py:143
  750.2 38.1 %collective-permute-start.34 = (bf16[1,480,640]{2,1,0:T(8,128)(2,1)}, bf16[1,480,640]{2,1,0:T(8,128)(2,1)}, u32[]{:S(2)}, u32[]{:S(2)}) collective-permute-start(bf16[1,480,640]{2,1,0:T(8,128)(2,1)} %maximum_select_fusion.41), channel_id=1, source_target_pairs={{0,4},{2,6},{4,0},{6,2},{8,12},{10,14},{12,8},{14,10},{16,20},{18,... | collective-permute-start | bytes 1843208 | tf_op jit(solution)/shard_map/ppermute | solution.py:143
  756.4 23.8 %collective-permute-start.50 = (bf16[1,320,960]{2,1,0:T(8,128)(2,1)S(1)}, bf16[1,320,960]{2,1,0:T(8,128)(2,1)S(1)}, u32[]{:S(2)}, u32[]{:S(2)}) collective-permute-start(bf16[1,320,960]{2,1,0:T(8,128)(2,1)S(1)} %maximum_select_fusion.37), channel_id=1, source_target_pairs={{0,4},{2,6},{4,0},{6,2},{8,12},{10,14},{12,8},{14,10},{16,20},{18,... | collective-permute-start | bytes 1843208 | tf_op jit(solution)/shard_map/ppermute | solution.py:143
  758.0 26.6 %collective-permute-start.26 = (bf16[1,240,1280]{2,1,0:T(8,128)(2,1)}, bf16[1,240,1280]{2,1,0:T(8,128)(2,1)}, u32[]{:S(2)}, u32[]{:S(2)}) collective-permute-start(bf16[1,240,1280]{2,1,0:T(8,128)(2,1)} %maximum_select_fusion.39), channel_id=1, source_target_pairs={{0,8},{2,10},{4,12},{6,14},{8,0},{10,2},{12,4},{14,6},{16,24},{18,... | collective-permute-start | bytes 1843208 | tf_op jit(solution)/shard_map/ppermute | solution.py:143
  770.9 47.2 %collective-permute-start.43 = (bf16[1,480,1280]{2,1,0:T(8,128)(2,1)}, bf16[1,480,1280]{2,1,0:T(8,128)(2,1)}, u32[]{:S(2)}, u32[]{:S(2)}) collective-permute-start(bf16[1,480,1280]{2,1,0:T(8,128)(2,1)} %maximum_select_fusion.26), channel_id=1, source_target_pairs={{0,2},{2,0},{4,6},{6,4},{8,10},{10,8},{12,14},{14,12},{16,18},{18,... | collective-permute-start | bytes 3686408 | tf_op jit(solution)/shard_map/ppermute | solution.py:143
  784.5 14.4 %collective-permute-start.51 = (bf16[1,640,960]{1,2,0:T(8,128)(2,1)}, bf16[1,640,960]{1,2,0:T(8,128)(2,1)}, u32[]{:S(2)}, u32[]{:S(2)}) collective-permute-start(bf16[1,640,960]{1,2,0:T(8,128)(2,1)} %copy.144), channel_id=1, source_target_pairs={{0,2},{2,0},{4,6},{6,4},{8,10},{10,8},{12,14},{14,12},{16,18},{18,... | collective-permute-start | bytes 3686408 | tf_op jit(solution)/shard_map/ppermute | solution.py:143
  786.2 9.7 %collective-permute-start.27 = (bf16[1,480,1280]{2,1,0:T(8,128)(2,1)S(1)}, bf16[1,480,1280]{2,1,0:T(8,128)(2,1)S(1)}, u32[]{:S(2)}, u32[]{:S(2)}) collective-permute-start(bf16[1,480,1280]{2,1,0:T(8,128)(2,1)S(1)} %maximum_select_fusion.22), channel_id=1, source_target_pairs={{0,2},{2,0},{4,6},{6,4},{8,10},{10,8},{12,14},{14,12},{16,18},{18,... | collective-permute-start | bytes 3686408 | tf_op jit(solution)/shard_map/ppermute | solution.py:143
  791.0 31.9 %collective-permute-start.35 = (bf16[1,480,1280]{2,1,0:T(8,128)(2,1)}, bf16[1,480,1280]{2,1,0:T(8,128)(2,1)}, u32[]{:S(2)}, u32[]{:S(2)}) collective-permute-start(bf16[1,480,1280]{2,1,0:T(8,128)(2,1)} %maximum_select_fusion.24), channel_id=1, source_target_pairs={{0,2},{2,0},{4,6},{6,4},{8,10},{10,8},{12,14},{14,12},{16,18},{18,... | collective-permute-start | bytes 3686408 | tf_op jit(solution)/shard_map/ppermute | solution.py:143
  (79 other events, 530.2 us)

commit v2 on v1

v2 whole, which is shorter than its diff:
```python
from functools import partial

import jax
import jax.numpy as jnp
from jax import lax
from jax.experimental import pallas as pl
from jax.experimental.pallas import tpu as pltpu
from jax.sharding import PartitionSpec as P

QUERY_HEADS = 15
KEY_VALUE_HEADS = 5
HEAD_SIZE = 64


EPS = 1e-05
NEGATIVE = -1e30


def angles(documents, head_dim):
    segment_length = documents.shape[0]
    places = jnp.arange(segment_length, dtype=jnp.int32)
    begins = jnp.concatenate([jnp.ones((1,), dtype=jnp.bool_), documents[1:] != documents[:-1]])
    starting = lax.cummax(jnp.where(begins, places, 0), axis=0)
    offsets = (places - starting).astype(jnp.float32)
    rates = 10000.0 ** (-2.0 * jnp.arange(head_dim // 2).astype(jnp.float32) / head_dim)
    phases = offsets[:, None] * rates[None, :]
    return (jnp.cos(phases)[:, None, :], jnp.sin(phases)[:, None, :])


def bit_swap(count, bit):
    return [(i, i ^ bit) for i in range(count)]


def swap_rep(value, bit):
    return lax.ppermute(value, "rep", bit_swap(lax.axis_size("rep"), bit))


def swap_shard(value, bit):
    return lax.ppermute(value, "shard", bit_swap(lax.axis_size("shard"), bit))


def rep_bit(bit):
    return (lax.axis_index("rep") // bit) % 2


def place_pair(mine, other, bit, axis):
    low = jnp.concatenate([mine, other], axis=axis)
    high = jnp.concatenate([other, mine], axis=axis)
    return jnp.where(bit == 0, low, high)


def gather_rows(piece):
    shards = lax.axis_size("shard")
    rows, columns = piece.shape
    quarter = rows // 4
    core, side = rep_bit(1), rep_bit(2)
    part = lax.dynamic_slice_in_dim(piece, (core * 2 + side) * quarter, quarter, 0)
    held = part[None]
    bit = 1
    while bit < shards:
        held = jnp.concatenate([held, swap_shard(held, bit)], axis=0)
        bit *= 2
    others = held[1:]
    others = place_pair(others, swap_rep(others, 2), side, 1)
    others = place_pair(others, swap_rep(others, 1), core, 1)
    me = lax.axis_index("shard")
    if shards == 2:
        return place_pair(piece, others[0], me, 0)
    whole = jnp.zeros((shards, rows, columns), piece.dtype)
    whole = lax.dynamic_update_slice_in_dim(whole, piece[None], me, 0)
    for j in range(1, shards):
        whole = lax.dynamic_update_slice_in_dim(whole, others[j - 1][None], me ^ j, 0)
    return whole.reshape(shards * rows, columns)


def add_up(left, right):
    return (left.astype(jnp.float32) + right.astype(jnp.float32)).astype(jnp.bfloat16)


def halve(value, bit, axis, swap):
    half = value.shape[axis] // 2
    mine = lax.dynamic_slice_in_dim(value, bit * half, half, axis)
    theirs = lax.dynamic_slice_in_dim(value, (1 - bit) * half, half, axis)
    return add_up(mine, swap(theirs))


def halve_shard(value):
    bit = lax.axis_size("shard") // 2
    while bit:
        value = halve(
            value, (lax.axis_index("shard") // bit) % 2, 0, partial(swap_shard, bit=bit)
        )
        bit //= 2
    return value


def reduce_rows(grad, order, axes):
    shards = lax.axis_size("shard")
    rows, columns = grad.shape
    value = grad.astype(jnp.bfloat16).reshape(shards, rows // shards, columns)
    value = halve(value, rep_bit(1), axes[1], partial(swap_rep, bit=1))
    for step in order:
        if step == 0:
            value = halve_shard(value)
        else:
            value = halve(value, rep_bit(step), axes[step], partial(swap_rep, bit=step))
    bit = 8
    while bit < lax.axis_size("rep"):
        value = add_up(value, swap_rep(value, bit))
        bit *= 2
    for step in [s for s in reversed(order) if s] + [1]:
        value = place_pair(value, swap_rep(value, step), rep_bit(step), axes[step])
    return value[0].astype(jnp.float32)


def reduce_gains(grads):
    bit = 1
    while bit < lax.axis_size("rep"):
        grads = grads + swap_rep(grads, bit)
        bit *= 2
    bit = 1
    while bit < lax.axis_size("shard"):
        grads = grads + swap_shard(grads, bit)
        bit *= 2
    own = grads.shape[1] // lax.axis_size("shard")
    return lax.dynamic_slice_in_dim(grads, lax.axis_index("shard") * own, own, 1)


LANES = 128
BLOCK = 256
GROUP = QUERY_HEADS // KEY_VALUE_HEADS
SPAN = (GROUP + 2) * HEAD_SIZE
WIDE = -(-SPAN // LANES) * LANES
SCALE = HEAD_SIZE**-0.5
ROOM = 56 * 1024 * 1024


def dot(left, right):
    return jnp.dot(left, right, preferred_element_type=jnp.float32)


def dot_nt(left, right):
    return lax.dot_general(left, right, (((1,), (1,)), ((), ())), preferred_element_type=jnp.float32)


def dot_tn(left, right):
    return lax.dot_general(left, right, (((0,), (0,)), ((), ())), preferred_element_type=jnp.float32)


def lanes_of(shape):
    return lax.broadcasted_iota(jnp.int32, shape, len(shape) - 1)


def turn(pair, cosine, sine):
    lane = lanes_of(pair.shape) % HEAD_SIZE
    half = HEAD_SIZE // 2
    partner = jnp.where(
        lane < half, pltpu.roll(pair, LANES - half, 1), pltpu.roll(pair, half, 1)
    )
    return pair * cosine + partner * sine


def three_parts(column):
    high = column.astype(jnp.bfloat16)
    rest = column - high.astype(jnp.float32)
    middle = rest.astype(jnp.bfloat16)
    low = (rest - middle.astype(jnp.float32)).astype(jnp.bfloat16)
    return high, middle, low


def put_parts(base, column, first):
    lane = lanes_of(base.shape)
    for k, part in enumerate(three_parts(column)):
        base = jnp.where(lane == first + k, part.astype(jnp.float32), base)
    return base


def call(kernel, grid, in_specs, out_specs, out_shape, scratch=(), flops=0, prefetch=0, move=0):
    return pl.pallas_call(
        kernel,
        grid_spec=pltpu.PrefetchScalarGridSpec(
            num_scalar_prefetch=prefetch,
            grid=grid,
            in_specs=in_specs,
            out_specs=out_specs,
            scratch_shapes=list(scratch),
        ),
        out_shape=out_shape,
        compiler_params=pltpu.CompilerParams(
            dimension_semantics=("arbitrary",) * len(grid), vmem_limit_bytes=ROOM
        ),
        cost_estimate=pl.CostEstimate(flops=flops, bytes_accessed=move, transcendentals=0),
    )


def struct(shape, dtype):
    return jax.ShapeDtypeStruct(shape, dtype)


def whole(shape):
    return pl.BlockSpec(shape, lambda *_: (0,) * len(shape))


def window(at_ref, core, side, rows):
    half = rows // 2
    return core * half + side * (half - rows * 4 // 15)


def fill_rows(at_ref, whole_ref, own_ref, parts):
    rows, tall = own_ref.shape[0], parts[0].shape[0]
    x, side, core = at_ref[0], at_ref[1], at_ref[2]
    whole_ref[pl.ds(pl.multiple_of(x * rows, 16), rows), :] = own_ref[...]
    for k, part in enumerate(parts):
        c, y = core ^ (k // 2), side ^ (k % 2)
        start = (1 - x) * rows + window(at_ref, c, y, rows)
        whole_ref[pl.ds(pl.multiple_of(start, 16), tall), :] = part[...]


def project_kernel(
    at_ref, x_ref, doc_ref, cos_ref, sin_ref, gain_ref, own_ref, p0, p1, p2, p3,
    flip_ref, q_ref, k_ref, v_ref, in_ref, w_ref,
):
    step = pl.program_id(0)

    @pl.when(step == 0)
    def _():
        fill_rows(at_ref, w_ref, own_ref, (p0, p1, p2, p3))
        x = x_ref[...].astype(jnp.float32)
        inverse = lax.rsqrt(jnp.mean(x * x, axis=0, keepdims=True) + EPS)
        flip = (x * inverse * gain_ref[...]).astype(jnp.bfloat16)
        flip_ref[...] = flip
        in_ref[...] = flip.T

    y = dot(in_ref[...], w_ref[:, pl.ds(pl.multiple_of(step * WIDE, LANES), WIDE)])
    cosine, sine = cos_ref[...], sin_ref[...]
    first = turn(y[:, :LANES], cosine, sine)
    second = turn(y[:, LANES : 2 * LANES], cosine, sine)
    lane = lanes_of(first.shape)
    inner = lane < HEAD_SIZE
    doc = doc_ref[...]
    same = ((lane - HEAD_SIZE) == doc).astype(jnp.float32)
    q_ref[0] = jnp.where(inner, first * SCALE, same).astype(jnp.bfloat16)
    q_ref[1] = jnp.where(inner, pltpu.roll(first, HEAD_SIZE, 1) * SCALE, same).astype(jnp.bfloat16)
    q_ref[2] = jnp.where(inner, second * SCALE, same).astype(jnp.bfloat16)
    away = jnp.where(
        lane < HEAD_SIZE + 4,
        jnp.where((lane - HEAD_SIZE) == doc, 0.0, NEGATIVE),
        jnp.where(lane < HEAD_SIZE + 7, 1.0, 0.0),
    )
    k_ref[0] = jnp.where(inner, pltpu.roll(second, HEAD_SIZE, 1), away).astype(jnp.bfloat16)
    ones = jnp.where(lane < HEAD_SIZE + 3, 1.0, 0.0)
    v_ref[0] = jnp.where(inner, y[:, 2 * LANES :], ones).astype(jnp.bfloat16)


def project(at, x, documents, cosine, sine, gain, own, parts):
    width, rows = x.shape
    table = whole((rows, LANES))
    across = own.shape[1]
    return call(
        project_kernel,
        (KEY_VALUE_HEADS,),
        [whole((width, rows)), whole((rows, 1)), table, table, whole((width, 1)), whole(own.shape)]
        + [whole(parts[0].shape)] * 4,
        [
            whole((width, rows)),
            pl.BlockSpec((GROUP, rows, LANES), lambda g, a: (g, 0, 0)),
            pl.BlockSpec((1, rows, LANES), lambda g, a: (g, 0, 0)),
            pl.BlockSpec((1, rows, LANES), lambda g, a: (g, 0, 0)),
        ],
        [
            struct((width, rows), jnp.bfloat16),
            struct((QUERY_HEADS, rows, LANES), jnp.bfloat16),
            struct((KEY_VALUE_HEADS, rows, LANES), jnp.bfloat16),
            struct((KEY_VALUE_HEADS, rows, LANES), jnp.bfloat16),
        ],
        scratch=[pltpu.VMEM((rows, width), jnp.bfloat16), pltpu.VMEM((width, across), jnp.bfloat16)],
        flops=2 * rows * width * WIDE * KEY_VALUE_HEADS,
        prefetch=1,
        move=20_000_000,
    )(at, x, documents, cosine, sine, gain, own, *parts)


def attend_kernel(q_ref, k_ref, v_ref, o_ref, qb_ref):
    rows = q_ref.shape[1]
    deep = GROUP * BLOCK
    row = lax.broadcasted_iota(jnp.int32, (GROUP, BLOCK, BLOCK), 1).reshape(deep, BLOCK)
    below = lanes_of((deep, BLOCK)) <= row
    for i in range(rows // BLOCK):
        here = pl.ds(i * BLOCK, BLOCK)
        q = q_ref[:, here, :].reshape(deep, LANES)
        near = jnp.where(below, dot_nt(q, k_ref[0, here, :]), NEGATIVE)
        top = jnp.max(near, axis=-1, keepdims=True)
        if i:
            past = pl.ds(0, i * BLOCK)
            far = dot_nt(q, k_ref[0, past, :])
            top = jnp.maximum(top, jnp.max(far, axis=-1, keepdims=True))
            total = dot(jnp.exp(far - top).astype(jnp.bfloat16), v_ref[0, past, :])
            total += dot(jnp.exp(near - top).astype(jnp.bfloat16), v_ref[0, here, :])
        else:
            total = dot(jnp.exp(near - top).astype(jnp.bfloat16), v_ref[0, here, :])
        summed = total[:, HEAD_SIZE : HEAD_SIZE + 1]
        out = (total / summed).reshape(GROUP, BLOCK, LANES)
        o_ref[0, here, :] = jnp.concatenate(
            [out[h][:, :HEAD_SIZE] for h in range(GROUP)], axis=1
        ).astype(jnp.bfloat16)
        back = put_parts(q.astype(jnp.float32), -(top + jnp.log(summed)), HEAD_SIZE + 4)
        qb_ref[:, here, :] = back.astype(jnp.bfloat16).reshape(GROUP, BLOCK, LANES)


def attend(q, k, v, first, groups):
    rows = q.shape[1]
    one = pl.BlockSpec((1, rows, LANES), lambda g: (g + first, 0, 0))
    three = pl.BlockSpec((GROUP, rows, LANES), lambda g: (g + first, 0, 0))
    return call(
        attend_kernel,
        (groups,),
        [three, one, one],
        [
            pl.BlockSpec((1, rows, GROUP * HEAD_SIZE), lambda g: (g, 0, 0)),
            pl.BlockSpec((GROUP, rows, LANES), lambda g: (g, 0, 0)),
        ],
        [
            struct((groups, rows, GROUP * HEAD_SIZE), jnp.bfloat16),
            struct((groups * GROUP, rows, LANES), jnp.bfloat16),
        ],
        flops=2 * 4 * rows * rows * LANES * GROUP * groups,
        move=3_000_000 * groups,
    )(q, k, v)


def blend_kernel(
    at_ref, x_ref, dy_ref, o0_ref, o1_ref, gain_ref, own_ref, p0, p1, p2, p3,
    mid_ref, in_ref, flip_ref, back_ref, w_ref,
):
    @pl.when(pl.program_id(0) == 0)
    def _():
        fill_rows(at_ref, w_ref, own_ref, (p0, p1, p2, p3))

    total = x_ref[...].astype(jnp.float32).T
    deep = GROUP * HEAD_SIZE
    early = o0_ref.shape[0]
    for g in range(KEY_VALUE_HEADS):
        heads = o0_ref[g] if g < early else o1_ref[g - early]
        total += dot(heads, w_ref[pl.ds(g * deep, deep), :])
    mid_ref[...] = total
    inverse = lax.rsqrt(jnp.mean(total * total, axis=-1, keepdims=True) + EPS)
    entry = (total * inverse * gain_ref[...]).astype(jnp.bfloat16)
    in_ref[...] = entry
    flip_ref[...] = entry.T
    back_ref[...] = dy_ref[...].T


def head_specs(heads):
    deep = GROUP * HEAD_SIZE
    return [pl.BlockSpec((h.shape[0], BLOCK, deep), lambda i, a: (0, i, 0)) for h in heads]


def blend(at, x, dy, heads, gain, own, parts):
    width, rows = x.shape
    band = pl.BlockSpec((BLOCK, width), lambda i, a: (i, 0))
    side = pl.BlockSpec((width, BLOCK), lambda i, a: (0, i))
    return call(
        blend_kernel,
        (rows // BLOCK,),
        [side, side]
        + head_specs(heads)
        + [whole((1, width)), whole(own.shape)]
        + [whole(parts[0].shape)] * 4,
        [band, band, side, band],
        [
            struct((rows, width), jnp.float32),
            struct((rows, width), jnp.bfloat16),
            struct((width, rows), jnp.bfloat16),
            struct((rows, width), jnp.bfloat16),
        ],
        scratch=[pltpu.VMEM((2 * own.shape[0], width), jnp.bfloat16)],
        flops=2 * rows * width * width,
        prefetch=1,
        move=18_000_000,
    )(at, x, dy, *heads, gain, own, *parts)


def mix_kernel(
    at_ref, in_ref, flip_ref, dy_ref, back_ref, gate_own, g0, g1, up_own, u0, u1, down_own, d0, d1,
    y_ref, din_ref, gg_ref, gu_ref, gd_ref, gate_ref, up_ref, down_ref,
):
    step = pl.program_id(0)
    x, side = at_ref[0], at_ref[1]
    rows = gate_own.shape[0]
    mine = pl.ds(pl.multiple_of(x * rows, 16), rows)
    theirs = pl.ds(pl.multiple_of((1 - x) * rows, 16), rows)
    gate_ref[mine, :] = gate_own[...]
    up_ref[mine, :] = up_own[...]

    @pl.when(step == side)
    def _():
        gate_ref[theirs, :] = g0[...]
        up_ref[theirs, :] = u0[...]

    @pl.when(step != side)
    def _():
        gate_ref[theirs, :] = g1[...]
        up_ref[theirs, :] = u1[...]

    @pl.when(step == x)
    def _():
        down_ref[...] = down_own[...]

    @pl.when(step != x)
    def _():
        down_ref[pl.ds(pl.multiple_of(side * rows, 16), rows), :] = d0[...]
        down_ref[pl.ds(pl.multiple_of((1 - side) * rows, 16), rows), :] = d1[...]

    entry, dy = in_ref[...], dy_ref[...]
    w_gate, w_up, w_down = gate_ref[...], up_ref[...], down_ref[...]
    gate = dot(entry, w_gate)
    up = dot(entry, w_up)
    sigmoid = jax.nn.sigmoid(gate)
    active = gate * sigmoid
    hidden = (active * up).astype(jnp.bfloat16)
    hidden_grad = dot(dy, w_down)
    gate_grad = (hidden_grad * up * sigmoid * (1.0 + gate * (1.0 - sigmoid))).astype(jnp.bfloat16)
    up_grad = (hidden_grad * active).astype(jnp.bfloat16)
    gd_ref[0] = dot(back_ref[...], hidden).astype(jnp.bfloat16)
    gg_ref[...] = dot(flip_ref[...], gate_grad).astype(jnp.bfloat16)
    gu_ref[...] = dot(flip_ref[...], up_grad).astype(jnp.bfloat16)
    y = dot_nt(hidden, w_down)
    din = dot_nt(gate_grad, w_gate) + dot_nt(up_grad, w_up)

    @pl.when(step == 0)
    def _():
        y_ref[...] = y
        din_ref[...] = din

    @pl.when(step > 0)
    def _():
        y_ref[...] += y
        din_ref[...] += din


def mix(at, entry, flip, dy, back, gate, up, down):
    rows, width = entry.shape
    cut = gate[1].shape[1]
    full, turned = whole((rows, width)), whole((width, rows))
    side = pl.BlockSpec((width // 2, cut), lambda i, a: (0, 2 * i + a[3]))
    piece = whole((width // 2, cut))
    grad = pl.BlockSpec((width, cut), lambda i, a: (0, i))
    return call(
        mix_kernel,
        (2,),
        [full, turned, full, turned, side, piece, piece, side, piece, piece]
        + [pl.BlockSpec((width, cut), lambda i, a: (0, a[3])), piece, piece],
        [full, full, grad, grad, pl.BlockSpec((1, width, cut), lambda i, a: (i, 0, 0))],
        [
            struct((rows, width), jnp.float32),
            struct((rows, width), jnp.float32),
            struct((width, 2 * cut), jnp.bfloat16),
            struct((width, 2 * cut), jnp.bfloat16),
            struct((2, width, cut), jnp.bfloat16),
        ],
        scratch=[pltpu.VMEM((width, cut), jnp.bfloat16)] * 3,
        flops=2 * 9 * rows * width * cut * 2,
        prefetch=1,
        move=30_000_000,
    )(at, entry, flip, dy, back, *gate, *up, *down)


def middle_kernel(
    at_ref, mid_ref, y0_ref, y1_ref, d0_ref, d1_ref, dy_ref, o0_ref, o1_ref, gain_ref,
    own_ref, p0, p1, p2, p3, mixed_ref, grad_ref, do_ref, gain_out, w_out, w_total, w_ref,
):
    step = pl.program_id(0)

    @pl.when(step == 0)
    def _():
        fill_rows(at_ref, w_ref, own_ref, (p0, p1, p2, p3))

    middle = mid_ref[...]
    mixed_ref[...] = (middle + y0_ref[...] + y1_ref[...]).T.astype(jnp.bfloat16)
    inverse = lax.rsqrt(jnp.mean(middle * middle, axis=-1, keepdims=True) + EPS)
    normed = middle * inverse
    back = d0_ref[...] + d1_ref[...]
    product = back * normed
    weighted = product * gain_ref[...]
    mean = jnp.mean(weighted, axis=-1, keepdims=True)
    grad = dy_ref[...].astype(jnp.float32) + inverse * (back * gain_ref[...] - normed * mean)
    grad_ref[...] = grad
    branch = grad.astype(jnp.bfloat16)
    deep = GROUP * HEAD_SIZE
    partial_gain = jnp.sum(product, axis=0, keepdims=True)

    @pl.when(step == 0)
    def _():
        gain_out[...] = partial_gain

    @pl.when(step > 0)
    def _():
        gain_out[...] += partial_gain

    lane = lanes_of((BLOCK, LANES))
    for g in range(KEY_VALUE_HEADS):
        span = pl.ds(g * deep, deep)
        heads = o0_ref[g] if g < o0_ref.shape[0] else o1_ref[g - o0_ref.shape[0]]
        part = dot_tn(heads, branch)

        @pl.when(step == 0)
        def _(part=part, span=span):
            w_total[span, :] = part

        @pl.when(step > 0)
        def _(part=part, span=span):
            w_total[span, :] += part

        upstream = dot_nt(branch, w_ref[span, :]).astype(jnp.bfloat16).astype(jnp.float32)
        inner = upstream * heads.astype(jnp.float32)
        for h in range(GROUP):
            at = h * HEAD_SIZE
            delta = jnp.sum(inner[:, at : at + HEAD_SIZE], axis=-1, keepdims=True)
            own = upstream[:, at : at + HEAD_SIZE]
            wide = jnp.concatenate([own, jnp.zeros_like(own)], axis=1)
            do_ref[g * GROUP + h] = put_parts(wide, -delta, HEAD_SIZE).astype(jnp.bfloat16)

    @pl.when(step == pl.num_programs(0) - 1)
    def _():
        w_out[...] = w_total[...].astype(jnp.bfloat16)


def middle_back(at, middle, y0, y1, d0, d1, dy, heads, gain, own, parts):
    rows, width = middle.shape
    band = pl.BlockSpec((BLOCK, width), lambda i, a: (i, 0))
    square = (2 * own.shape[0], width)
    return call(
        middle_kernel,
        (rows // BLOCK,),
        [band] * 6
        + head_specs(heads)
        + [whole((1, width)), whole(own.shape)]
        + [whole(parts[0].shape)] * 4,
        [
            pl.BlockSpec((width, BLOCK), lambda i, a: (0, i)),
            band,
            pl.BlockSpec((QUERY_HEADS, BLOCK, LANES), lambda i, a: (0, i, 0)),
            whole((1, width)),
            whole(square),
        ],
        [
            struct((width, rows), jnp.bfloat16),
            struct((rows, width), jnp.float32),
            struct((QUERY_HEADS, rows, LANES), jnp.bfloat16),
            struct((1, width), jnp.float32),
            struct(square, jnp.bfloat16),
        ],
        scratch=[pltpu.VMEM(square, jnp.float32), pltpu.VMEM(square, jnp.bfloat16)],
        flops=2 * 2 * rows * width * width,
        prefetch=1,
        move=40_000_000,
    )(at, middle, y0, y1, d0, d1, dy, *heads, gain, own, *parts)


def attend_back_kernel(q_ref, k_ref, v_ref, do_ref, cos_ref, sin_ref, out_ref, dq_ref):
    rows = q_ref.shape[1]
    count = rows // BLOCK
    after = lax.broadcasted_iota(jnp.int32, (BLOCK, BLOCK), 0) <= lanes_of((BLOCK, BLOCK))
    key_grads, value_grads = [], []
    for j in range(count):
        here = pl.ds(j * BLOCK, BLOCK)
        k, v = k_ref[0, here, :], v_ref[0, here, :]
        dk = jnp.zeros((BLOCK, LANES), jnp.float32)
        dv = jnp.zeros((BLOCK, LANES), jnp.float32)
        for h in range(GROUP):
            for start, size in ((j * BLOCK, BLOCK), ((j + 1) * BLOCK, rows - (j + 1) * BLOCK)):
                if not size:
                    continue
                span = pl.ds(start, size)
                q, do = q_ref[h, span, :], do_ref[h, span, :]
                scores = dot_nt(k, q)
                if start == j * BLOCK:
                    scores = jnp.where(after, scores, NEGATIVE)
                probs = jnp.exp(scores)
                score_grad = (probs * dot_nt(v, do)).astype(jnp.bfloat16)
                dv += dot(probs.astype(jnp.bfloat16), do)
                dk += dot(score_grad, q)
                dq = dot_tn(score_grad, k)
                if j == 0:
                    dq_ref[h, span, :] = dq
                else:
                    dq_ref[h, span, :] += dq
        key_grads.append(dk)
        value_grads.append(dv)
    cosine, sine = cos_ref[...], -sin_ref[...]
    half = HEAD_SIZE
    parts = [turn(dq_ref[h] * SCALE, cosine, sine)[:, :half] for h in range(GROUP)]
    parts.append(turn(jnp.concatenate(key_grads, axis=0), cosine, sine)[:, :half])
    parts.append(jnp.concatenate(value_grads, axis=0)[:, :half])
    parts.append(jnp.zeros((rows, WIDE - SPAN), jnp.float32))
    out_ref[0] = jnp.concatenate(parts, axis=1).astype(jnp.bfloat16)


def attend_back(q, k, v, do, cosine, sine, first, begin, groups):
    rows = q.shape[1]
    one = pl.BlockSpec((1, rows, LANES), lambda g: (g + first, 0, 0))
    table = whole((rows, LANES))
    return call(
        attend_back_kernel,
        (groups,),
        [
            pl.BlockSpec((GROUP, rows, LANES), lambda g: (g + begin, 0, 0)),
            one,
            one,
            pl.BlockSpec((GROUP, rows, LANES), lambda g: (g + first, 0, 0)),
            table,
            table,
        ],
        pl.BlockSpec((1, rows, WIDE), lambda g: (g, 0, 0)),
        struct((groups, rows, WIDE), jnp.bfloat16),
        scratch=[pltpu.VMEM((GROUP, rows, LANES), jnp.float32)],
        flops=2 * 10 * rows * rows * LANES * GROUP * groups,
        move=3_000_000 * groups,
    )(q, k, v, do, cosine, sine)


def weight_kernel(flip_ref, *refs):
    flip = flip_ref[...]
    parts = []
    for ref in refs[:-1]:
        if len(ref.shape) == 2:
            parts.append(ref[...])
            continue
        for g in range(ref.shape[0]):
            parts.append(dot(flip, ref[g])[:, :SPAN].astype(jnp.bfloat16))
    refs[-1][...] = jnp.concatenate(parts, axis=1)


def weight_grads(flip, pieces):
    width, rows = flip.shape
    half = width // 2
    across = sum(p.shape[1] if p.ndim == 2 else p.shape[0] * SPAN for p in pieces)
    specs = [
        pl.BlockSpec((half, p.shape[1]), lambda i: (i, 0)) if p.ndim == 2 else whole(p.shape)
        for p in pieces
    ]
    return call(
        weight_kernel,
        (2,),
        [pl.BlockSpec((half, rows), lambda i: (i, 0))] + specs,
        pl.BlockSpec((half, across), lambda i: (i, 0)),
        struct((width, across), jnp.bfloat16),
        flops=2 * rows * width * across,
        move=10_000_000,
    )(flip, *pieces)


def finish_kernel(
    at_ref, x_ref, mid_ref, da_ref, db_ref, dc_ref, gain_ref, own_ref, p0, p1, p2, p3,
    out_ref, gain_out, w_ref,
):
    @pl.when(pl.program_id(0) == 0)
    def _():
        fill_rows(at_ref, w_ref, own_ref, (p0, p1, p2, p3))

    x = x_ref[...].astype(jnp.float32).T
    inverse = lax.rsqrt(jnp.mean(x * x, axis=-1, keepdims=True) + EPS)
    normed = x * inverse
    back = jnp.zeros_like(x)
    g = 0
    for ref in (da_ref, db_ref, dc_ref):
        for k in range(ref.shape[0]):
            back += dot_nt(ref[k], w_ref[:, pl.ds(g * WIDE, WIDE)])
            g += 1
    product = back * normed
    partial_gain = jnp.sum(product, axis=0, keepdims=True)

    @pl.when(pl.program_id(0) == 0)
    def _():
        gain_out[...] = partial_gain

    @pl.when(pl.program_id(0) > 0)
    def _():
        gain_out[...] += partial_gain

    mean = jnp.mean(product * gain_ref[...], axis=-1, keepdims=True)
    grad = mid_ref[...] + inverse * (back * gain_ref[...] - normed * mean)
    out_ref[...] = grad.T.astype(jnp.bfloat16)


def finish(at, x, middle_grad, backs, gain, own, parts):
    width, rows = x.shape
    side = pl.BlockSpec((width, BLOCK), lambda i, a: (0, i))
    return call(
        finish_kernel,
        (rows // BLOCK,),
        [side, pl.BlockSpec((BLOCK, width), lambda i, a: (i, 0))]
        + [pl.BlockSpec((b.shape[0], BLOCK, WIDE), lambda i, a: (0, i, 0)) for b in backs]
        + [whole((1, width)), whole(own.shape)]
        + [whole(parts[0].shape)] * 4,
        [side, whole((1, width))],
        [struct((width, rows), jnp.bfloat16), struct((1, width), jnp.float32)],
        scratch=[pltpu.VMEM((2 * own.shape[0], own.shape[1]), jnp.bfloat16)],
        flops=2 * rows * width * WIDE * KEY_VALUE_HEADS,
        prefetch=1,
        move=14_000_000,
    )(at, x, middle_grad, *backs, gain, own, *parts)


def widen_kernel(at_ref, mine_ref, other_ref, out_ref):
    core = at_ref[2]

    @pl.when(pl.program_id(0) == core)
    def _():
        out_ref[...] = mine_ref[0].astype(jnp.float32)

    @pl.when(pl.program_id(0) != core)
    def _():
        out_ref[...] = other_ref[0].astype(jnp.float32)


def widen(at, mine, other, order, spread):
    _, rows, columns = mine.shape

    def place(c, j, a):
        apart = {2: a[1] ^ (j // 2), 4: a[4] ^ (j % 2)}
        return (apart[order[0]] + 2 * apart[order[1]], 0, 0)

    if spread:
        shape = (2 * rows, 4 * columns)
        out = pl.BlockSpec((rows, columns), lambda c, j, a: (j % 2, 2 * (j // 2) + c))
    else:
        shape = (4 * rows, 2 * columns)
        out = pl.BlockSpec((rows, columns), lambda c, j, a: (j, c))
    return call(
        widen_kernel,
        (2, 4),
        [pl.BlockSpec((1, rows, columns), place)] * 2,
        out,
        struct(shape, jnp.float32),
        prefetch=1,
        move=10_000_000,
    )(at, mine, other)


def tie(value, *others):
    return lax.optimization_barrier((value, *others))[0]


def first_rows(w_query, w_key, w_value):
    rows = w_query.shape[0]
    pad = jnp.zeros((rows, WIDE - SPAN), w_query.dtype)
    deep = GROUP * HEAD_SIZE
    columns = []
    for g in range(KEY_VALUE_HEADS):
        columns.append(w_query[:, g * deep : (g + 1) * deep])
        columns.append(w_key[:, g * HEAD_SIZE : (g + 1) * HEAD_SIZE])
        columns.append(w_value[:, g * HEAD_SIZE : (g + 1) * HEAD_SIZE])
        columns.append(pad)
    return jnp.concatenate(columns, axis=1)


def spread_rows(received):
    beside = swap_rep(received, 2)
    return [received, beside, swap_rep(received, 1), swap_rep(beside, 1)]


def start_sum(send, keep):
    return add_up(keep, swap_rep(send, 1))


def one_step(value, step, axes):
    if step == 0:
        return halve_shard(value)
    return halve(value, rep_bit(step), axes[step], partial(swap_rep, bit=step))


def end_sum(value, order):
    bit = 8
    while bit < lax.axis_size("rep"):
        value = add_up(value, swap_rep(value, bit))
        bit *= 2
    return spread_sum(value, order)


def spread_sum(value, order):
    for step in order:
        value = jnp.concatenate([value, swap_rep(value, step)], axis=0)
    return value, swap_rep(value, 1)


def split_cores(grad):
    core = rep_bit(1)
    half = grad.shape[-1] // 2
    send = lax.dynamic_slice_in_dim(grad, (1 - core) * half, half, grad.ndim - 1)
    keep = lax.dynamic_slice_in_dim(grad, core * half, half, grad.ndim - 1)
    return send, keep


def per_device(
    tokens,
    segments,
    gain_attn,
    w_query,
    key_weight_matrix,
    value_weight_matrix,
    w_out,
    gain_mlp,
    w_gate,
    w_up,
    w_down,
    cotangent,
):
    shards = lax.axis_size("shard")
    fast = shards == 2
    rows, width = tokens.shape[1:]
    half = width // 2
    columns = QUERY_HEADS * HEAD_SIZE
    key_columns = KEY_VALUE_HEADS * HEAD_SIZE
    inner = w_gate.shape[1]
    cut = inner // 4
    x_t = tokens[0].T
    dy_t = cotangent[0].T
    tall = half * 4 // 15
    zero = jnp.int32(0)

    if fast:
        x, side, core, depth = lax.axis_index("shard"), rep_bit(2), rep_bit(1), rep_bit(4)
        x, side, core, depth = (v.astype(jnp.int32) for v in (x, side, core, depth))
        other = 1 - core
        start = window(None, core, side, half)
        narrow = partial(lax.dynamic_slice_in_dim, start_index=start, slice_size=tall, axis=0)
        part_first = first_rows(
            narrow(w_query), narrow(key_weight_matrix), narrow(value_weight_matrix)
        )
        came_first = swap_shard(part_first, 1)
        own_first = first_rows(w_query, key_weight_matrix, value_weight_matrix)
        gains = jnp.stack([gain_attn, gain_mlp]).astype(jnp.float32)
        gains = place_pair(gains, swap_shard(gains, 1), x, 1)
        column = (2 * side + other) * cut
        part_out = narrow(w_out)
        part_gate = lax.dynamic_slice_in_dim(w_gate, column, cut, 1)
        part_up = lax.dynamic_slice_in_dim(w_up, column, cut, 1)
        own_down = w_down.T
        part_down = lax.dynamic_slice(own_down, (side * half, other * cut), (half, cut))
        part_out, part_gate = tie(part_out, came_first), tie(part_gate, came_first)
        part_up, part_down = tie(part_up, came_first), tie(part_down, came_first)
        came_out, came_gate = swap_shard(part_out, 1), swap_shard(part_gate, 1)
        came_up, came_down = swap_shard(part_up, 1), swap_shard(part_down, 1)
        parts_first = spread_rows(came_first)
        parts_out = spread_rows(came_out)
        parts_gate, parts_up, parts_down = (
            spread_rows(came) for came in (came_gate, came_up, came_down)
        )
        own_out, own_gate, own_up = w_out, w_gate, w_up
    else:
        x = side = core = depth = zero
        other = 1 - core
        full = gather_rows(first_rows(w_query, key_weight_matrix, value_weight_matrix))
        full_out = gather_rows(w_out)
        starts = [half + window(None, c, y, half) for c in (0, 1) for y in (0, 1)]
        own_first, parts_first = full[:half], [full[s : s + tall] for s in starts]
        own_out, parts_out = full_out[:half], [full_out[s : s + tall] for s in starts]
        gains = gather_rows(jnp.pad(jnp.stack([gain_attn, gain_mlp], axis=1), ((0, 0), (0, 126))))
        gains = gains[:, :2].T.astype(jnp.float32)

        def cut_up(value):
            blocks = [value[half:, k * cut : (k + 1) * cut] for k in range(4)]
            return value[:half], [blocks[1], blocks[3], blocks[0], blocks[2]]

        own_gate, parts_gate = cut_up(gather_rows(w_gate))
        own_up, parts_up = cut_up(gather_rows(w_up))
        full_down = gather_rows(w_down).T
        own_down = full_down[:, : 2 * cut]
        parts_down = [
            full_down[r : r + half, (2 + c) * cut : (3 + c) * cut]
            for c in (1, 0)
            for r in (0, half)
        ]

    at = jnp.stack([x, side, core, core, depth])
    at_other = jnp.stack([x, side, core, other, depth])
    cosine, sine = angles(segments[0], HEAD_SIZE)
    cosine, sine = cosine[:, 0], sine[:, 0]
    cosine, sine = (
        jnp.concatenate([cosine] * 4, axis=1),
        jnp.concatenate([-sine, sine, -sine, sine], axis=1),
    )
    gain_one, gain_two = gains[:1], gains[1:]

    flip_one, q, k, v = project(
        at, x_t, segments[0][:, None], cosine, sine, gain_one.T, own_first, parts_first
    )
    if fast:
        q = tie(q, came_gate)
    heads0, back0 = attend(q, k, v, 0, 3)
    if fast:
        q = tie(q, heads0, came_up)
    heads1, back1 = attend(q, k, v, 3, 2)
    heads = (heads0, heads1)
    if fast:
        heads = (heads0, tie(heads1, came_down))
    middle, entry, flip, dy = blend(at, x_t, dy_t, heads, gain_two, own_out, parts_out)
    y0, d0, gate0, up0, down0 = mix(
        at_other, entry, flip, dy, dy_t,
        (own_gate, *parts_gate[:2]), (own_up, *parts_up[:2]), (own_down, *parts_down[:2]),
    )
    y1, d1, gate1, up1, down1 = mix(
        at, tie(entry, d0), flip, dy, dy_t,
        (own_gate, *parts_gate[2:]), (own_up, *parts_up[2:]), (own_down, *parts_down[2:]),
    )
    wide, tower = {2: 2, 4: 1}, {2: 1, 4: 1}
    if fast:
        cube = (2, half, 2 * cut)
        gate = start_sum(gate0.reshape(cube), gate1.reshape(cube))
        up = start_sum(up0.reshape(cube), up1.reshape(cube))
        down = start_sum(down0, down1)
        y1, gate, up, down = lax.optimization_barrier((y1, gate, up, down))
        gate, up, down = one_step(gate, 0, wide), one_step(up, 4, wide), one_step(down, 2, tower)
    mixed, middle_grad, do, grad_gain_two, grad_out = middle_back(
        at, middle, y0, y1, d0, d1, dy, heads, gain_two, own_out, parts_out
    )
    rope = (cosine, sine)
    backs0 = attend_back(back0, k, v, do, *rope, 0, 0, 1)
    near = weight_grads(flip_one, (grad_out, backs0))
    if fast:
        near = start_sum(*split_cores(near.reshape(2, half, -1)))
        do, gate, up, down = lax.optimization_barrier((do, gate, up, down))
        gate, up, down = one_step(gate, 2, wide), one_step(up, 2, wide), one_step(down, 0, tower)
    backs1 = attend_back(back0, k, v, do, *rope, 1, 1, 2)
    if fast:
        do, backs1, gate, up, down, near = lax.optimization_barrier(
            (do, backs1, gate, up, down, near)
        )
        gate, up, down = one_step(gate, 4, wide), one_step(up, 0, wide), one_step(down, 4, tower)
        near = one_step(near, 2, tower)
    backs2 = attend_back(back1, k, v, do, *rope, 3, 0, 2)
    if fast:
        backs1, gate, up, down, near = lax.optimization_barrier((backs1, gate, up, down, near))
        near = one_step(near, 4, tower)
    far = weight_grads(flip_one, (backs1, backs2))
    grad_tokens, grad_gain_one = finish(
        at, x_t, middle_grad, (backs0, backs1, backs2), gain_one, own_first, parts_first
    )
    gain_sums = reduce_gains(jnp.concatenate([grad_gain_one, grad_gain_two]))
    if fast:
        far = start_sum(*split_cores(far.reshape(2, half, -1)))
        near = one_step(near, 0, tower)
        far = one_step(one_step(one_step(far, 0, tower), 2, tower), 4, tower)
        sum_gate = widen(at, *end_sum(gate, (4, 2)), (4, 2), True)
        sum_up = widen(at, *end_sum(up, (2, 4)), (2, 4), True)
        sum_down = widen(at, *end_sum(down, (4, 2)), (4, 2), False).T
        sum_near = widen(at, *end_sum(near, (4, 2)), (4, 2), False)
        sum_far = widen(at, *end_sum(far, (4, 2)), (4, 2), False)
    else:
        def whole_grad(two, one):
            both = jnp.stack([one.reshape(width, 2, cut), two.reshape(width, 2, cut)], axis=2)
            return both.reshape(width, inner)

        across, upright = {1: 2, 2: 2, 4: 1}, {1: 1, 2: 1, 4: 1}
        sum_gate = reduce_rows(whole_grad(gate0, gate1), (0, 2, 4), across)
        sum_up = reduce_rows(whole_grad(up0, up1), (4, 2, 0), across)
        downs = [d.transpose(1, 0, 2) for d in (down0, down1)]
        sum_down = reduce_rows(whole_grad(*downs).T, (2, 0, 4), upright)
        sum_near = reduce_rows(near, (0, 2, 4), across)
        sum_far = reduce_rows(far, (0, 4, 2), across)
    tall_rows = sum_near.shape[0]
    groups = jnp.concatenate([sum_near[:, columns:], sum_far], axis=1)
    groups = groups.reshape(tall_rows, KEY_VALUE_HEADS, SPAN)
    deep = GROUP * HEAD_SIZE
    return (
        mixed.T[None],
        grad_tokens.T[None],
        gain_sums[0],
        groups[:, :, :deep].reshape(tall_rows, columns),
        groups[:, :, deep : deep + HEAD_SIZE].reshape(tall_rows, key_columns),
        groups[:, :, deep + HEAD_SIZE :].reshape(tall_rows, key_columns),
        sum_near[:, :columns],
        gain_sums[1],
        sum_gate,
        sum_up,
        sum_down,
    )


def solution(mesh):
    placed = (
        P(("rep", "shard"), None, None),
        P(("rep", "shard"), None),
        P("shard"),
        P("shard", None),
        P("shard", None),
        P("shard", None),
        P("shard", None),
        P("shard"),
        P("shard", None),
        P("shard", None),
        P("shard", None),
        P(("rep", "shard"), None, None),
    )
    return jax.shard_map(
        per_device,
        mesh=mesh,
        in_specs=placed,
        out_specs=(
            P(("rep", "shard"), None, None),
            P(("rep", "shard"), None, None),
            P("shard"),
            P("shard", None),
            P("shard", None),
            P("shard", None),
            P("shard", None),
            P("shard"),
            P("shard", None),
            P("shard", None),
            P("shard", None),
        ),
        check_vma=False,
    )
```

time: 839 us -> 541 us (0.64)
  matrix products: 298 us -> 0 us
  Pallas kernels: 0 us -> 276 us
  other arithmetic: 180 us -> 33.7 us
  waiting for transfers between devices: 192 us -> 108 us
  local copies, waits for them, and re-layouts: 114 us -> 59 us
  starting transfers between devices: 41.6 us -> 52.9 us
    dot_general x33 -> x0, matrix products: 298 us -> none  [the longest x21 130 us: product(): return jnp.dot(left, right, preferred_element_type=jnp.float32)]
    pallas_call x0 -> x18, Pallas kernels: none -> 276 us  [the longest x2 84.7 us: mix(): call(mix_kernel, (2,), [full, turned, full, turned, side, piece, piece, s...]
    convert_element_type x11 -> x1, other arithmetic: 70.8 us -> 0.01 us  [per_device(): gains = jnp.stack([gain_attn, gain_mlp]).astype(jnp.float32)]
    select_n x31 -> x1, other arithmetic: 53 us -> 0.08 us  [place_pair(): return jnp.where(bit == 0, low, high)]
    ppermute x10 -> x12, waiting for transfers between devices: 54.5 us -> 10.1 us  [swap_shard(): return lax.ppermute(value, 'shard', bit_swap(lax.axis_size('shard'), bit))]
    ppermute x42 -> x54, waiting for transfers between devices: 138 us -> 97.5 us  [swap_rep(): return lax.ppermute(value, 'rep', bit_swap(lax.axis_size('rep'), bit))]
    reduce_sum x3 -> x0, other arithmetic: 26.1 us -> none  [the longest x2 25.6 us: attend_forward(): summed = jnp.sum(exponents, axis=-1, keepdims=True)]
    unnamed x191 -> x67, local copies, waits for them, and re-layouts: 29.7 us -> 17 us
  transfers between devices with their start and end apart: 52 -> 66, of which waited for: 23 -> 21; matrix products, arithmetic and copies ran while one was open for 41% -> 13% of each run, Pallas kernels for 0% -> 49%
where the time goes in v2:
time: 541 us; the launch traced here: 531 us
  Pallas kernels  276 us (51%)
  waiting for transfers between devices  108 us (20%)
  local copies, waits for them, and re-layouts  59 us (11%)
  starting transfers between devices  52.9 us (10%)
  other arithmetic  33.7 us (6%)
    ppermute x54, waiting for transfers between devices, swap_rep(): return lax.ppermute(value, 'rep', bit_swap(lax.axis_size('rep'), bit))  97.5 us
    pallas_call x2, Pallas kernels, mix(): call(mix_kernel, (2,), [full, turned, full, turned, side, piece, piece, s...  84.7 us
    pallas_call x3, Pallas kernels, attend_back(): call(attend_back_kernel, (groups,), [pl.BlockSpec((GROUP, rows, LANES), l...  47.3 us
    ppermute x54, starting transfers between devices, swap_rep(): return lax.ppermute(value, 'rep', bit_swap(lax.axis_size('rep'), bit))  41.1 us
    pallas_call x5, Pallas kernels, widen(): call(widen_kernel, (2, 4), [pl.BlockSpec((1, rows, columns), place)] * 2,...  36.3 us
    pallas_call x1, Pallas kernels, middle_back(): call(middle_kernel, (rows // BLOCK,), [band] * 6 + head_specs(heads) + [w...  32.2 us
    pallas_call x2, Pallas kernels, attend(): call(attend_kernel, (groups,), [three, one, one], [pl.BlockSpec((1, rows,...  24.6 us
    convert_element_type x25, other arithmetic, add_up(): (left.astype(jnp.float32) + right.astype(jnp.float32)).astype(jnp.bfloat16)  20.2 us
  transfers between devices with their start and end apart: 66, of which 21 were waited for; matrix products, arithmetic and copies ran while one was open for 13% of the time, Pallas kernels for 49%

profile of v2, /device:TPU:0, one launch (start us, length us, event | category | flops | bytes accessed | tf_op | source)
XLA Modules:
  0.0 531.5 jit_solution(3568196209344104390)
XLA Ops:
  2.1 3.0 collective-permute-start
  11.2 2.4 constant_dynamic-slice_fusion.23
  14.5 8.1 %collective-permute-done.1.p0 = bf16[128,1920]{1,0:T(8,128)(2,1)} collective-permute-done((bf16[128,1920]{1,0:T(8,128)(2,1)}, bf16[128,1920]{1,0:T(8,128)(2,1)}, u32[]{:S(2)}, u32[]{:S(2)}) %collective-permute-start.1) | collective-permute-done | bytes 491552 | tf_op jit(solution)/shard_map/ppermute | solution.py:39
  24.2 1.9 fusion.2
  28.2 1.7 constant_dynamic-slice_fusion.22
  30.4 4.3 collective-permute-done.2.p1
  34.7 1.9 dynamic-slice_bitcast_fusion
  38.9 1.6 copy.72
  40.5 1.6 copy.73
  42.1 1.6 copy.74
  43.7 1.6 copy.75
  46.1 1.6 copy.77
  48.5 1.6 copy.79
  51.4 4.2 concatenate.70.own_ref
  55.6 1.9 pad_maximum_fusion.9
  57.5 1.8 collective-permute-done.8.p0
  62.2 4.1 collective-permute-done.9.p1
  68.8 15.9 %shard_map.203 = (bf16[960,1024]{1,0:T(8,128)(2,1)}, bf16[15,1024,128]{2,1,0:T(8,128)(2,1)}, bf16[5,1024,128]{2,1,0:T(8,128)(2,1)}, bf16[5,1024,128]{2,1,0:T(8,128)(2,1)}) custom-call(s32[5]{0:T(128)} %stack.39.at_ref, bf16[960,1024]{1,0:T(8,128)(2,1)} %bitcast.59, s32[1024,1]{1,0:T(8,128)} %copy.66.doc_ref, f32[1024,128]{1,0:T(8,128)} %get-tuple-element.185.cos_ref, ...), custom_call_target="tpu_custom_call" | custom-call | flops 3774873600 | bytes 20000000 | tf_op jit(solution)/shard_map/pallas_call | solution.py:259
  84.7 14.4 %shard_map.204 = (bf16[3,1024,192]{2,1,0:T(8,128)(2,1)}, bf16[9,1024,128]{2,1,0:T(8,128)(2,1)}) custom-call(bf16[15,1024,128]{2,1,0:T(8,128)(2,1)} %get-tuple-element.74.q_ref, bf16[5,1024,128]{2,1,0:T(8,128)(2,1)} %get-tuple-element.70.k_ref, bf16[5,1024,128]{2,1,0:T(8,128)(2,1)} %get-tuple-element.71.v_ref), custom_call_target="tpu_custom_call" | custom-call | flops 9663676416 | bytes 9000000 | tf_op jit(solution)/shard_map/pallas_call | solution.py:314
  100.8 10.2 %shard_map.205 = (bf16[2,1024,192]{2,1,0:T(8,128)(2,1)}, bf16[6,1024,128]{2,1,0:T(8,128)(2,1)}) custom-call(bf16[15,1024,128]{2,1,0:T(8,128)(2,1)} %get-tuple-element.74.q_ref, bf16[5,1024,128]{2,1,0:T(8,128)(2,1)} %get-tuple-element.70.k_ref, bf16[5,1024,128]{2,1,0:T(8,128)(2,1)} %get-tuple-element.71.v_ref), custom_call_target="tpu_custom_call" | custom-call | flops 6442450944 | bytes 6000000 | tf_op jit(solution)/shard_map/pallas_call | solution.py:314
  111.7 10.3 %shard_map.206 = (f32[1024,960]{1,0:T(8,128)}, bf16[1024,960]{1,0:T(8,128)(2,1)}, bf16[960,1024]{1,0:T(8,128)(2,1)}, bf16[1024,960]{1,0:T(8,128)(2,1)}) custom-call(s32[5]{0:T(128)} %stack.39.at_ref, bf16[960,1024]{1,0:T(8,128)(2,1)} %bitcast.60, bf16[960,1024]{1,0:T(8,128)(2,1)} %bitcast.56, bf16[3,1024,192]{2,1,0:T(8,128)(2,1)} %get-tuple-element.72.o0_ref, ...), custom_call_target="tpu_custom_call" | custom-call | flops 1887436800 | bytes 18000000 | tf_op jit(solution)/shard_map/pallas_call | solution.py:362
  123.1 42.3 %shard_map.207 = (f32[1024,960]{1,0:T(8,128)}, f32[1024,960]{1,0:T(8,128)}, bf16[960,1280]{1,0:T(8,128)(2,1)}, bf16[960,1280]{1,0:T(8,128)(2,1)}, bf16[2,960,640]{2,1,0:T(8,128)(2,1)}) custom-call(s32[5]{0:T(128)} %stack.44.at_ref, bf16[1024,960]{1,0:T(8,128)(2,1)} %get-tuple-element.85.in_ref, bf16[960,1024]{1,0:T(8,128)(2,1)} %get-tuple-element.81.flip_ref, ...), custom_call_target="tpu_custom_call" | custom-call | flops 22649241600 | bytes 30000000 | tf_op jit(solution)/shard_map/pallas_call | solution.py:448
  166.2 42.3 %shard_map.208 = (f32[1024,960]{1,0:T(8,128)}, f32[1024,960]{1,0:T(8,128)}, bf16[960,1280]{1,0:T(8,128)(2,1)}, bf16[960,1280]{1,0:T(8,128)(2,1)}, bf16[2,960,640]{2,1,0:T(8,128)(2,1)}) custom-call(s32[5]{0:T(128)} %stack.39.at_ref, bf16[1024,960]{1,0:T(8,128)(2,1)} %get-tuple-element.85.in_ref, bf16[960,1024]{1,0:T(8,128)(2,1)} %get-tuple-element.81.flip_ref, ...), custom_call_target="tpu_custom_call" | custom-call | flops 22649241600 | bytes 30000000 | tf_op jit(solution)/shard_map/pallas_call | solution.py:448
  208.6 2.4 fusion.1
  211.0 2.5 fusion
  213.5 2.3 add_convert_fusion
  221.9 32.2 %shard_map.209 = (bf16[960,1024]{1,0:T(8,128)(2,1)}, f32[1024,960]{1,0:T(8,128)}, bf16[15,1024,128]{2,1,0:T(8,128)(2,1)}, f32[1,960]{1,0:T(1,128)}, bf16[960,960]{1,0:T(8,128)(2,1)}) custom-call(s32[5]{0:T(128)} %stack.39.at_ref, f32[1024,960]{1,0:T(8,128)} %get-tuple-element.79.mid_ref, f32[1024,960]{1,0:T(8,128)} %get-tuple-element.83.y0_ref, ...), custom_call_target="tpu_custom_call" | custom-call | flops 3774873600 | bytes 40000000 | tf_op jit(solution)/shard_map/pallas_call | solution.py:532
  254.2 10.4 %shard_map.210.refs_1_.da_ref = bf16[1,1024,384]{2,1,0:T(8,128)(2,1)} custom-call(bf16[9,1024,128]{2,1,0:T(8,128)(2,1)} %get-tuple-element.97.q_ref, bf16[5,1024,128]{2,1,0:T(8,128)(2,1)} %get-tuple-element.70.k_ref, bf16[5,1024,128]{2,1,0:T(8,128)(2,1)} %get-tuple-element.71.v_ref, bf16[15,1024,128]{2,1,0:T(8,128)(2,1)} %get-tuple-element.115.do_ref, ...), custom_call_target="tpu_custom_call" | custom-call | flops 8053063680 | bytes 3000000 | tf_op jit(solution)/shard_map/pallas_call | solution.py:603
  264.6 4.3 shard_map.212
  268.9 2.4 constant_dynamic-slice_fusion.15
  271.3 2.6 add_convert_fusion.3
  279.5 18.4 %shard_map.211.db_ref.refs_0_ = bf16[2,1024,384]{2,1,0:T(8,128)(2,1)} custom-call(bf16[9,1024,128]{2,1,0:T(8,128)(2,1)} %get-tuple-element.97.q_ref, bf16[5,1024,128]{2,1,0:T(8,128)(2,1)} %get-tuple-element.70.k_ref, bf16[5,1024,128]{2,1,0:T(8,128)(2,1)} %get-tuple-element.71.v_ref, bf16[15,1024,128]{2,1,0:T(8,128)(2,1)} %get-tuple-element.115.do_ref, ...), custom_call_target="tpu_custom_call" | custom-call | flops 16106127360 | bytes 6000000 | tf_op jit(solution)/shard_map/pallas_call | solution.py:603
  301.9 12.1 %collective-permute-done.28 = bf16[2,240,640]{2,1,0:T(8,128)(2,1)S(1)} collective-permute-done((bf16[2,240,640]{2,1,0:T(8,128)(2,1)S(1)}, bf16[2,240,640]{2,1,0:T(8,128)(2,1)S(1)}, u32[]{:S(2)}, u32[]{:S(2)}) %collective-permute-start.28) | collective-permute-done | bytes 614432 | tf_op jit(solution)/shard_map/ppermute | solution.py:35
  316.7 1.6 collective-permute-start.33
  320.0 18.4 %shard_map.213.dc_ref.refs_1_ = bf16[2,1024,384]{2,1,0:T(8,128)(2,1)} custom-call(bf16[6,1024,128]{2,1,0:T(8,128)(2,1)} %get-tuple-element.114.q_ref, bf16[5,1024,128]{2,1,0:T(8,128)(2,1)} %get-tuple-element.70.k_ref, bf16[5,1024,128]{2,1,0:T(8,128)(2,1)} %get-tuple-element.71.v_ref, bf16[15,1024,128]{2,1,0:T(8,128)(2,1)} %get-tuple-element.115.do_ref, ...), custom_call_target="tpu_custom_call" | custom-call | flops 16106127360 | bytes 6000000 | tf_op jit(solution)/shard_map/pallas_call | solution.py:603
  340.3 7.8 %shard_map.216 = bf16[960,1280]{1,0:T(8,128)(2,1)} custom-call(bf16[960,1024]{1,0:T(8,128)(2,1)} %get-tuple-element.106.flip_ref, bf16[2,1024,384]{2,1,0:T(8,128)(2,1)} %shard_map.211.db_ref.refs_0_, bf16[2,1024,384]{2,1,0:T(8,128)(2,1)} %shard_map.213.dc_ref.refs_1_), custom_call_target="tpu_custom_call" | custom-call | flops 2516582400 | bytes 10000000 | tf_op jit(solution)/shard_map/pallas_call | solution.py:642
  348.1 2.4 constant_dynamic-slice_fusion.7
  350.6 13.1 %shard_map.214 = (bf16[960,1024]{1,0:T(8,128)(2,1)}, f32[1,960]{1,0:T(1,128)}) custom-call(s32[5]{0:T(128)} %stack.39.at_ref, bf16[960,1024]{1,0:T(8,128)(2,1)} %bitcast.61, f32[1024,960]{1,0:T(8,128)} %get-tuple-element.96.mid_ref, bf16[1,1024,384]{2,1,0:T(8,128)(2,1)} %shard_map.210.refs_1_.da_ref, bf16[2,1024,384]{2,1,0:T(8,128)(2,1)} %shard_map.211.db_ref.refs_0_, ...), custom_call_target="tpu_custom_call" | custom-call | flops 3774873600 | bytes 14000000 | tf_op jit(solution)/shard_map/pallas_call | solution.py:689
  367.5 2.6 collective-permute-start.54
  370.6 2.6 collective-permute-start.62
  373.9 7.7 %collective-permute-done.40 = bf16[2,120,640]{2,1,0:T(8,128)(2,1)} collective-permute-done((bf16[2,120,640]{2,1,0:T(8,128)(2,1)}, bf16[2,120,640]{2,1,0:T(8,128)(2,1)}, u32[]{:S(2)}, u32[]{:S(2)}) %collective-permute-start.40) | collective-permute-done | bytes 307232 | tf_op jit(solution)/shard_map/ppermute | solution.py:35
  385.0 13.5 %collective-permute-done.54 = bf16[1,240,640]{2,1,0:T(8,128)(2,1)S(1)} collective-permute-done((bf16[1,240,640]{2,1,0:T(8,128)(2,1)}, bf16[1,240,640]{2,1,0:T(8,128)(2,1)S(1)}, u32[]{:S(2)}, u32[]{:S(2)}) %collective-permute-start.54) | collective-permute-done | bytes 307232 | tf_op jit(solution)/shard_map/ppermute | solution.py:35
  399.3 5.8 %collective-permute-done.58 = bf16[1,240,640]{2,1,0:T(8,128)(2,1)S(1)} collective-permute-done((bf16[1,240,640]{2,1,0:T(8,128)(2,1)}, bf16[1,240,640]{2,1,0:T(8,128)(2,1)S(1)}, u32[]{:S(2)}, u32[]{:S(2)}) %collective-permute-start.58) | collective-permute-done | bytes 307232 | tf_op jit(solution)/shard_map/ppermute | solution.py:35
  406.1 4.4 collective-permute-done.62
  414.2 2.9 collective-permute-done.55
  418.6 2.1 collective-permute-done.59
  422.3 5.0 collective-permute-done.48
  427.4 2.1 collective-permute-start.49
  429.7 16.3 %collective-permute-done.49 = bf16[1,120,640]{2,1,0:T(8,128)(2,1)S(1)} collective-permute-done((bf16[1,120,640]{2,1,0:T(8,128)(2,1)S(1)}, bf16[1,120,640]{2,1,0:T(8,128)(2,1)S(1)}, u32[]{:S(2)}, u32[]{:S(2)}) %collective-permute-start.49) | collective-permute-done | bytes 153632 | tf_op jit(solution)/shard_map/ppermute | solution.py:35
  446.0 2.3 collective-permute-start.64
  450.1 6.1 %collective-permute-done.50 = bf16[1,120,640]{2,1,0:T(8,128)(2,1)S(1)} collective-permute-done((bf16[1,120,640]{2,1,0:T(8,128)(2,1)S(1)}, bf16[1,120,640]{2,1,0:T(8,128)(2,1)S(1)}, u32[]{:S(2)}, u32[]{:S(2)}) %collective-permute-start.50) | collective-permute-done | bytes 153632 | tf_op jit(solution)/shard_map/ppermute | solution.py:35
  458.1 1.7 collective-permute-start.44
  459.8 2.9 collective-permute-done.51
  463.8 3.5 collective-permute-done.38
  469.7 5.2 collective-permute-done.52
  477.3 6.6 %shard_map.215 = f32[480,1280]{1,0:T(8,128)} custom-call(s32[5]{0:T(128)} %stack.39.at_ref, bf16[4,120,640]{2,1,0:T(8,128)(2,1)} %pad_maximum_fusion.4.mine_ref, bf16[4,120,640]{2,1,0:T(8,128)(2,1)} %collective-permute-done.45.other_ref), custom_call_target="tpu_custom_call" | custom-call | bytes 10000000 | tf_op jit(solution)/shard_map/pallas_call | solution.py:730
  485.3 3.0 slice.183
  488.4 7.7 %shard_map.218 = f32[480,2560]{1,0:T(8,128)} custom-call(s32[5]{0:T(128)} %stack.39.at_ref, bf16[4,240,640]{2,1,0:T(8,128)(2,1)} %copy-done.1, bf16[4,240,640]{2,1,0:T(8,128)(2,1)} %collective-permute-done.57.other_ref), custom_call_target="tpu_custom_call" | custom-call | bytes 10000000 | tf_op jit(solution)/shard_map/pallas_call | solution.py:730
  496.0 7.7 %shard_map.219 = f32[480,2560]{1,0:T(8,128)} custom-call(s32[5]{0:T(128)} %stack.39.at_ref, bf16[4,240,640]{2,1,0:T(8,128)(2,1)} %copy-done.2, bf16[4,240,640]{2,1,0:T(8,128)(2,1)} %collective-permute-done.61.other_ref), custom_call_target="tpu_custom_call" | custom-call | bytes 10000000 | tf_op jit(solution)/shard_map/pallas_call | solution.py:730
  503.7 7.7 %shard_map.220 = f32[960,1280]{1,0:T(8,128)} custom-call(s32[5]{0:T(128)} %stack.39.at_ref, bf16[4,240,640]{2,1,0:T(8,128)(2,1)} %pad_maximum_fusion.3.mine_ref, bf16[4,240,640]{2,1,0:T(8,128)(2,1)} %collective-permute-done.65.other_ref), custom_call_target="tpu_custom_call" | custom-call | bytes 10000000 | tf_op jit(solution)/shard_map/pallas_call | solution.py:730
  511.4 6.7 %shard_map.217 = f32[480,1280]{1,0:T(8,128)} custom-call(s32[5]{0:T(128)} %stack.39.at_ref, bf16[4,120,640]{2,1,0:T(8,128)(2,1)} %copy-done.8, bf16[4,120,640]{2,1,0:T(8,128)(2,1)} %collective-permute-done.53.other_ref), custom_call_target="tpu_custom_call" | custom-call | bytes 10000000 | tf_op jit(solution)/shard_map/pallas_call | solution.py:730
  518.1 4.1 pad_maximum_fusion
  522.2 3.4 copy.68
  528.2 2.8 copy.69
  (249 shorter events, 79.7 us)
Async XLA Ops:
  2.1 28.3 %collective-permute-start = (f32[2,480]{1,0:T(2,128)S(1)}, f32[2,480]{1,0:T(2,128)S(1)}, u32[]{:S(2)}, u32[]{:S(2)}) collective-permute-start(f32[2,480]{1,0:T(2,128)S(1)} %maximum_convert_fusion), channel_id=1, source_target_pairs={{0,1},{1,0},{2,3},{3,2},{4,5},{5,4},{6,7},{7,6},{8,9},{9,8},{10,11... | collective-permute-start | bytes 11528 | tf_op jit(solution)/shard_map/ppermute | solution.py:39
  9.6 13.0 %collective-permute-start.1 = (bf16[128,1920]{1,0:T(8,128)(2,1)}, bf16[128,1920]{1,0:T(8,128)(2,1)}, u32[]{:S(2)}, u32[]{:S(2)}) collective-permute-start(bf16[128,1920]{1,0:T(8,128)(2,1)} %concatenate.71), channel_id=1, source_target_pairs={{0,1},{1,0},{2,3},{3,2},{4,5},{5,4},{6,7},{7,6},{8,9},{9,8},{10,11... | collective-permute-start | bytes 1474568 | tf_op jit(solution)/shard_map/ppermute | solution.py:39
  22.6 12.1 %collective-permute-start.2 = (bf16[128,1920]{1,0:T(8,128)(2,1)}, bf16[128,1920]{1,0:T(8,128)(2,1)}, u32[]{:S(2)}, u32[]{:S(2)}) collective-permute-start(bf16[128,1920]{1,0:T(8,128)(2,1)} %collective-permute-done.1.p0), channel_id=1, source_target_pairs={{0,4},{2,6},{4,0},{6,2},{8,12},{10,14},{12,8},{14,10},{16,20},{18,... | collective-permute-start | bytes 1474568 | tf_op jit(solution)/shard_map/ppermute | solution.py:35
  26.1 40.1 %collective-permute-start.5 = (bf16[480,640]{1,0:T(8,128)(2,1)}, bf16[480,640]{1,0:T(8,128)(2,1)}, u32[]{:S(2)}, u32[]{:S(2)}) collective-permute-start(bf16[480,640]{1,0:T(8,128)(2,1)} %get-tuple-element.68), channel_id=1, source_target_pairs={{0,1},{1,0},{2,3},{3,2},{4,5},{5,4},{6,7},{7,6},{8,9},{9,8},{10,11... | collective-permute-start | bytes 1843208 | tf_op jit(solution)/shard_map/ppermute | solution.py:39
  26.7 40.0 %collective-permute-start.6 = (bf16[480,640]{1,0:T(8,128)(2,1)}, bf16[480,640]{1,0:T(8,128)(2,1)}, u32[]{:S(2)}, u32[]{:S(2)}) collective-permute-start(bf16[480,640]{1,0:T(8,128)(2,1)} %get-tuple-element.73), channel_id=1, source_target_pairs={{0,1},{1,0},{2,3},{3,2},{4,5},{5,4},{6,7},{7,6},{8,9},{9,8},{10,11... | collective-permute-start | bytes 1843208 | tf_op jit(solution)/shard_map/ppermute | solution.py:39
  29.9 29.4 %collective-permute-start.8 = (bf16[128,960]{1,0:T(8,128)(2,1)}, bf16[128,960]{1,0:T(8,128)(2,1)S(1)}, u32[]{:S(2)}, u32[]{:S(2)}) collective-permute-start(bf16[128,960]{1,0:T(8,128)(2,1)} %constant_dynamic-slice_fusion.22), channel_id=1, source_target_pairs={{0,1},{1,0},{2,3},{3,2},{4,5},{5,4},{6,7},{7,6},{8,9},{9,8},{10,11... | collective-permute-start | bytes 737288 | tf_op jit(solution)/shard_map/ppermute | solution.py:39
  30.4 31.1 %collective-permute-start.3 = (bf16[128,1920]{1,0:T(8,128)(2,1)}, bf16[128,1920]{1,0:T(8,128)(2,1)}, u32[]{:S(2)}, u32[]{:S(2)}) collective-permute-start(bf16[128,1920]{1,0:T(8,128)(2,1)} %collective-permute-done.1.p0), channel_id=1, source_target_pairs={{0,2},{2,0},{4,6},{6,4},{8,10},{10,8},{12,14},{14,12},{16,18},{18,... | collective-permute-start | bytes 1474568 | tf_op jit(solution)/shard_map/ppermute | solution.py:35
  34.7 33.5 %collective-permute-start.4 = (bf16[128,1920]{1,0:T(8,128)(2,1)}, bf16[128,1920]{1,0:T(8,128)(2,1)}, u32[]{:S(2)}, u32[]{:S(2)}) collective-permute-start(bf16[128,1920]{1,0:T(8,128)(2,1)} %collective-permute-done.2.p1), channel_id=1, source_target_pairs={{0,2},{2,0},{4,6},{6,4},{8,10},{10,8},{12,14},{14,12},{16,18},{18,... | collective-permute-start | bytes 1474568 | tf_op jit(solution)/shard_map/ppermute | solution.py:35
  59.3 6.9 %collective-permute-start.9 = (bf16[128,960]{1,0:T(8,128)(2,1)S(1)}, bf16[128,960]{1,0:T(8,128)(2,1)S(1)}, u32[]{:S(2)}, u32[]{:S(2)}) collective-permute-start(bf16[128,960]{1,0:T(8,128)(2,1)S(1)} %collective-permute-done.8.p0), channel_id=1, source_target_pairs={{0,4},{2,6},{4,0},{6,2},{8,12},{10,14},{12,8},{14,10},{16,20},{18,... | collective-permute-start | bytes 737288 | tf_op jit(solution)/shard_map/ppermute | solution.py:35
  61.5 37.7 %collective-permute-start.7 = (bf16[480,640]{1,0:T(8,128)(2,1)S(1)}, bf16[480,640]{1,0:T(8,128)(2,1)}, u32[]{:S(2)}, u32[]{:S(2)}) collective-permute-start(bf16[480,640]{1,0:T(8,128)(2,1)S(1)} %copy-done.15), channel_id=1, source_target_pairs={{0,1},{1,0},{2,3},{3,2},{4,5},{5,4},{6,7},{7,6},{8,9},{9,8},{10,11... | collective-permute-start | bytes 1843208 | tf_op jit(solution)/shard_map/ppermute | solution.py:39
  66.2 32.9 %collective-permute-start.10 = (bf16[128,960]{1,0:T(8,128)(2,1)S(1)}, bf16[128,960]{1,0:T(8,128)(2,1)S(1)}, u32[]{:S(2)}, u32[]{:S(2)}) collective-permute-start(bf16[128,960]{1,0:T(8,128)(2,1)S(1)} %collective-permute-done.8.p0), channel_id=1, source_target_pairs={{0,2},{2,0},{4,6},{6,4},{8,10},{10,8},{12,14},{14,12},{16,18},{18,... | collective-permute-start | bytes 737288 | tf_op jit(solution)/shard_map/ppermute | solution.py:35
  66.2 44.8 %collective-permute-start.11 = (bf16[128,960]{1,0:T(8,128)(2,1)S(1)}, bf16[128,960]{1,0:T(8,128)(2,1)S(1)}, u32[]{:S(2)}, u32[]{:S(2)}) collective-permute-start(bf16[128,960]{1,0:T(8,128)(2,1)S(1)} %collective-permute-done.9.p1), channel_id=1, source_target_pairs={{0,2},{2,0},{4,6},{6,4},{8,10},{10,8},{12,14},{14,12},{16,18},{18,... | collective-permute-start | bytes 737288 | tf_op jit(solution)/shard_map/ppermute | solution.py:35
  66.7 55.2 %collective-permute-start.12 = (bf16[480,640]{1,0:T(8,128)(2,1)}, bf16[480,640]{1,0:T(8,128)(2,1)}, u32[]{:S(2)}, u32[]{:S(2)}) collective-permute-start(bf16[480,640]{1,0:T(8,128)(2,1)} %collective-permute-done.5.g0), channel_id=1, source_target_pairs={{0,4},{2,6},{4,0},{6,2},{8,12},{10,14},{12,8},{14,10},{16,20},{18,... | collective-permute-start | bytes 1843208 | tf_op jit(solution)/shard_map/ppermute | solution.py:35
  68.3 53.9 %collective-permute-start.13 = (bf16[480,640]{1,0:T(8,128)(2,1)}, bf16[480,640]{1,0:T(8,128)(2,1)}, u32[]{:S(2)}, u32[]{:S(2)}) collective-permute-start(bf16[480,640]{1,0:T(8,128)(2,1)} %collective-permute-done.6.u0), channel_id=1, source_target_pairs={{0,4},{2,6},{4,0},{6,2},{8,12},{10,14},{12,8},{14,10},{16,20},{18,... | collective-permute-start | bytes 1843208 | tf_op jit(solution)/shard_map/ppermute | solution.py:35
  99.1 23.6 %collective-permute-start.15 = (bf16[480,640]{1,0:T(8,128)(2,1)}, bf16[480,640]{1,0:T(8,128)(2,1)S(1)}, u32[]{:S(2)}, u32[]{:S(2)}) collective-permute-start(bf16[480,640]{1,0:T(8,128)(2,1)} %collective-permute-done.5.g0), channel_id=1, source_target_pairs={{0,2},{2,0},{4,6},{6,4},{8,10},{10,8},{12,14},{14,12},{16,18},{18,... | collective-permute-start | bytes 1843208 | tf_op jit(solution)/shard_map/ppermute | solution.py:35
  99.2 23.3 %collective-permute-start.14 = (bf16[480,640]{1,0:T(8,128)(2,1)}, bf16[480,640]{1,0:T(8,128)(2,1)}, u32[]{:S(2)}, u32[]{:S(2)}) collective-permute-start(bf16[480,640]{1,0:T(8,128)(2,1)} %collective-permute-done.7.d0), channel_id=1, source_target_pairs={{0,4},{2,6},{4,0},{6,2},{8,12},{10,14},{12,8},{14,10},{16,20},{18,... | collective-permute-start | bytes 1843208 | tf_op jit(solution)/shard_map/ppermute | solution.py:35
  111.0 54.4 %collective-permute-start.17 = (bf16[480,640]{1,0:T(8,128)(2,1)}, bf16[480,640]{1,0:T(8,128)(2,1)S(1)}, u32[]{:S(2)}, u32[]{:S(2)}) collective-permute-start(bf16[480,640]{1,0:T(8,128)(2,1)} %collective-permute-done.6.u0), channel_id=1, source_target_pairs={{0,2},{2,0},{4,6},{6,4},{8,10},{10,8},{12,14},{14,12},{16,18},{18,... | collective-permute-start | bytes 1843208 | tf_op jit(solution)/shard_map/ppermute | solution.py:35
  122.0 43.7 %collective-permute-start.19 = (bf16[480,640]{1,0:T(8,128)(2,1)}, bf16[480,640]{1,0:T(8,128)(2,1)}, u32[]{:S(2)}, u32[]{:S(2)}) collective-permute-start(bf16[480,640]{1,0:T(8,128)(2,1)} %collective-permute-done.7.d0), channel_id=1, source_target_pairs={{0,2},{2,0},{4,6},{6,4},{8,10},{10,8},{12,14},{14,12},{16,18},{18,... | collective-permute-start | bytes 1843208 | tf_op jit(solution)/shard_map/ppermute | solution.py:35
  122.2 43.8 %collective-permute-start.16 = (bf16[480,640]{1,0:T(8,128)(2,1)}, bf16[480,640]{1,0:T(8,128)(2,1)}, u32[]{:S(2)}, u32[]{:S(2)}) collective-permute-start(bf16[480,640]{1,0:T(8,128)(2,1)} %collective-permute-done.12.g1), channel_id=1, source_target_pairs={{0,2},{2,0},{4,6},{6,4},{8,10},{10,8},{12,14},{14,12},{16,18},{18,... | collective-permute-start | bytes 1843208 | tf_op jit(solution)/shard_map/ppermute | solution.py:35
  122.5 43.6 %collective-permute-start.18 = (bf16[480,640]{1,0:T(8,128)(2,1)}, bf16[480,640]{1,0:T(8,128)(2,1)}, u32[]{:S(2)}, u32[]{:S(2)}) collective-permute-start(bf16[480,640]{1,0:T(8,128)(2,1)} %collective-permute-done.13.u1), channel_id=1, source_target_pairs={{0,2},{2,0},{4,6},{6,4},{8,10},{10,8},{12,14},{14,12},{16,18},{18,... | collective-permute-start | bytes 1843208 | tf_op jit(solution)/shard_map/ppermute | solution.py:35
  122.7 43.4 %collective-permute-start.20 = (bf16[480,640]{1,0:T(8,128)(2,1)}, bf16[480,640]{1,0:T(8,128)(2,1)}, u32[]{:S(2)}, u32[]{:S(2)}) collective-permute-start(bf16[480,640]{1,0:T(8,128)(2,1)} %collective-permute-done.14.d1), channel_id=1, source_target_pairs={{0,2},{2,0},{4,6},{6,4},{8,10},{10,8},{12,14},{14,12},{16,18},{18,... | collective-permute-start | bytes 1843208 | tf_op jit(solution)/shard_map/ppermute | solution.py:35
  165.4 43.2 %collective-permute-start.21 = (bf16[2,480,1280]{2,1,0:T(8,128)(2,1)}, bf16[2,480,1280]{2,1,0:T(8,128)(2,1)S(1)}, u32[]{:S(2)}, u32[]{:S(2)}) collective-permute-start(bf16[2,480,1280]{2,1,0:T(8,128)(2,1)} %bitcast.70), channel_id=1, source_target_pairs={{0,2},{2,0},{4,6},{6,4},{8,10},{10,8},{12,14},{14,12},{16,18},{18,... | collective-permute-start | bytes 7372808 | tf_op jit(solution)/shard_map/ppermute | solution.py:35
  165.6 45.4 %collective-permute-start.22 = (bf16[2,480,1280]{2,1,0:T(8,128)(2,1)}, bf16[2,480,1280]{2,1,0:T(8,128)(2,1)}, u32[]{:S(2)}, u32[]{:S(2)}) collective-permute-start(bf16[2,480,1280]{2,1,0:T(8,128)(2,1)} %bitcast.69), channel_id=1, source_target_pairs={{0,2},{2,0},{4,6},{6,4},{8,10},{10,8},{12,14},{14,12},{16,18},{18,... | collective-permute-start | bytes 7372808 | tf_op jit(solution)/shard_map/ppermute | solution.py:35
  166.0 47.5 %collective-permute-start.23 = (bf16[2,960,640]{2,1,0:T(8,128)(2,1)}, bf16[2,960,640]{2,1,0:T(8,128)(2,1)}, u32[]{:S(2)}, u32[]{:S(2)}) collective-permute-start(bf16[2,960,640]{2,1,0:T(8,128)(2,1)} %get-tuple-element.92), channel_id=1, source_target_pairs={{0,2},{2,0},{4,6},{6,4},{8,10},{10,8},{12,14},{14,12},{16,18},{18,... | collective-permute-start | bytes 7372808 | tf_op jit(solution)/shard_map/ppermute | solution.py:35
  217.0 56.9 %collective-permute-start.24 = (bf16[1,480,1280]{2,1,0:T(8,128)(2,1)}, bf16[1,480,1280]{2,1,0:T(8,128)(2,1)}, u32[]{:S(2)}, u32[]{:S(2)}) collective-permute-start(bf16[1,480,1280]{2,1,0:T(8,128)(2,1)} %constant_dynamic-slice_fusion.21), channel_id=1, source_target_pairs={{0,1},{1,0},{2,3},{3,2},{4,5},{5,4},{6,7},{7,6},{8,9},{9,8},{10,11... | collective-permute-start | bytes 3686408 | tf_op jit(solution)/shard_map/ppermute | solution.py:39
  218.7 56.8 %collective-permute-start.25 = (bf16[2,240,1280]{2,1,0:T(8,128)(2,1)}, bf16[2,240,1280]{2,1,0:T(8,128)(2,1)}, u32[]{:S(2)}, u32[]{:S(2)}) collective-permute-start(bf16[2,240,1280]{2,1,0:T(8,128)(2,1)} %constant_dynamic-slice_fusion.20), channel_id=1, source_target_pairs={{0,8},{2,10},{4,12},{6,14},{8,0},{10,2},{12,4},{14,6},{16,24},{18,... | collective-permute-start | bytes 3686408 | tf_op jit(solution)/shard_map/ppermute | solution.py:35
  221.4 49.9 %collective-permute-start.26 = (bf16[2,480,640]{2,1,0:T(8,128)(2,1)}, bf16[2,480,640]{2,1,0:T(8,128)(2,1)}, u32[]{:S(2)}, u32[]{:S(2)}) collective-permute-start(bf16[2,480,640]{2,1,0:T(8,128)(2,1)} %constant_dynamic-slice_fusion.19), channel_id=1, source_target_pairs={{0,4},{2,6},{4,0},{6,2},{8,12},{10,14},{12,8},{14,10},{16,20},{18,... | collective-permute-start | bytes 3686408 | tf_op jit(solution)/shard_map/ppermute | solution.py:35
  271.3 28.9 %collective-permute-start.30 = (bf16[2,480,640]{2,1,0:T(8,128)(2,1)}, bf16[2,480,640]{2,1,0:T(8,128)(2,1)}, u32[]{:S(2)}, u32[]{:S(2)}) collective-permute-start(bf16[2,480,640]{2,1,0:T(8,128)(2,1)} %constant_dynamic-slice_fusion.15), channel_id=1, source_target_pairs={{0,2},{2,0},{4,6},{6,4},{8,10},{10,8},{12,14},{14,12},{16,18},{18,... | collective-permute-start | bytes 3686408 | tf_op jit(solution)/shard_map/ppermute | solution.py:35
  278.0 23.8 %collective-permute-start.27 = (bf16[1,480,640]{2,1,0:T(8,128)(2,1)}, bf16[1,480,640]{2,1,0:T(8,128)(2,1)S(1)}, u32[]{:S(2)}, u32[]{:S(2)}) collective-permute-start(bf16[1,480,640]{2,1,0:T(8,128)(2,1)} %constant_dynamic-slice_fusion.18), channel_id=1, source_target_pairs={{0,4},{2,6},{4,0},{6,2},{8,12},{10,14},{12,8},{14,10},{16,20},{18,... | collective-permute-start | bytes 1843208 | tf_op jit(solution)/shard_map/ppermute | solution.py:35
  298.0 16.1 %collective-permute-start.28 = (bf16[2,240,640]{2,1,0:T(8,128)(2,1)S(1)}, bf16[2,240,640]{2,1,0:T(8,128)(2,1)S(1)}, u32[]{:S(2)}, u32[]{:S(2)}) collective-permute-start(bf16[2,240,640]{2,1,0:T(8,128)(2,1)S(1)} %constant_dynamic-slice_fusion.17), channel_id=1, source_target_pairs={{0,4},{2,6},{4,0},{6,2},{8,12},{10,14},{12,8},{14,10},{16,20},{18,... | collective-permute-start | bytes 1843208 | tf_op jit(solution)/shard_map/ppermute | solution.py:35
  298.6 15.8 %collective-permute-start.29 = (bf16[1,480,640]{2,1,0:T(8,128)(2,1)S(1)}, bf16[1,480,640]{2,1,0:T(8,128)(2,1)S(1)}, u32[]{:S(2)}, u32[]{:S(2)}) collective-permute-start(bf16[1,480,640]{2,1,0:T(8,128)(2,1)S(1)} %constant_dynamic-slice_fusion.16), channel_id=1, source_target_pairs={{0,1},{1,0},{2,3},{3,2},{4,5},{5,4},{6,7},{7,6},{8,9},{9,8},{10,11... | collective-permute-start | bytes 1843208 | tf_op jit(solution)/shard_map/ppermute | solution.py:39
  314.6 23.9 %collective-permute-start.31 = (bf16[1,240,640]{2,1,0:T(8,128)(2,1)S(1)}, bf16[1,240,640]{2,1,0:T(8,128)(2,1)S(1)}, u32[]{:S(2)}, u32[]{:S(2)}) collective-permute-start(bf16[1,240,640]{2,1,0:T(8,128)(2,1)S(1)} %constant_dynamic-slice_fusion.14), channel_id=1, source_target_pairs={{0,8},{2,10},{4,12},{6,14},{8,0},{10,2},{12,4},{14,6},{16,24},{18,... | collective-permute-start | bytes 921608 | tf_op jit(solution)/shard_map/ppermute | solution.py:35
  315.3 24.0 %collective-permute-start.32 = (bf16[1,240,640]{2,1,0:T(8,128)(2,1)S(1)}, bf16[1,240,640]{2,1,0:T(8,128)(2,1)S(1)}, u32[]{:S(2)}, u32[]{:S(2)}) collective-permute-start(bf16[1,240,640]{2,1,0:T(8,128)(2,1)S(1)} %constant_dynamic-slice_fusion.13), channel_id=1, source_target_pairs={{0,1},{1,0},{2,3},{3,2},{4,5},{5,4},{6,7},{7,6},{8,9},{9,8},{10,11... | collective-permute-start | bytes 921608 | tf_op jit(solution)/shard_map/ppermute | solution.py:39
  316.7 23.3 %collective-permute-start.33 = (bf16[1,240,640]{2,1,0:T(8,128)(2,1)S(1)}, bf16[1,240,640]{2,1,0:T(8,128)(2,1)S(1)}, u32[]{:S(2)}, u32[]{:S(2)}) collective-permute-start(bf16[1,240,640]{2,1,0:T(8,128)(2,1)S(1)} %constant_dynamic-slice_fusion.12), channel_id=1, source_target_pairs={{0,8},{2,10},{4,12},{6,14},{8,0},{10,2},{12,4},{14,6},{16,24},{18,... | collective-permute-start | bytes 921608 | tf_op jit(solution)/shard_map/ppermute | solution.py:35
  318.4 21.7 %collective-permute-start.34 = (bf16[2,240,640]{2,1,0:T(8,128)(2,1)S(1)}, bf16[2,240,640]{2,1,0:T(8,128)(2,1)S(1)}, u32[]{:S(2)}, u32[]{:S(2)}) collective-permute-start(bf16[2,240,640]{2,1,0:T(8,128)(2,1)S(1)} %constant_dynamic-slice_fusion.11), channel_id=1, source_target_pairs={{0,4},{2,6},{4,0},{6,2},{8,12},{10,14},{12,8},{14,10},{16,20},{18,... | collective-permute-start | bytes 1843208 | tf_op jit(solution)/shard_map/ppermute | solution.py:35
  350.5 32.1 %collective-permute-start.46 = (bf16[2,480,640]{2,1,0:T(8,128)(2,1)}, bf16[2,480,640]{2,1,0:T(8,128)(2,1)}, u32[]{:S(2)}, u32[]{:S(2)}) collective-permute-start(bf16[2,480,640]{2,1,0:T(8,128)(2,1)} %constant_dynamic-slice_fusion.7), channel_id=1, source_target_pairs={{0,2},{2,0},{4,6},{6,4},{8,10},{10,8},{12,14},{14,12},{16,18},{18,... | collective-permute-start | bytes 3686408 | tf_op jit(solution)/shard_map/ppermute | solution.py:35
  365.7 15.9 %collective-permute-start.40 = (bf16[2,120,640]{2,1,0:T(8,128)(2,1)}, bf16[2,120,640]{2,1,0:T(8,128)(2,1)}, u32[]{:S(2)}, u32[]{:S(2)}) collective-permute-start(bf16[2,120,640]{2,1,0:T(8,128)(2,1)} %constant_dynamic-slice_fusion.9), channel_id=1, source_target_pairs={{0,8},{2,10},{4,12},{6,14},{8,0},{10,2},{12,4},{14,6},{16,24},{18,... | collective-permute-start | bytes 921608 | tf_op jit(solution)/shard_map/ppermute | solution.py:35
  366.9 3.7 collective-permute-start.36
  367.5 31.0 %collective-permute-start.54 = (bf16[1,240,640]{2,1,0:T(8,128)(2,1)}, bf16[1,240,640]{2,1,0:T(8,128)(2,1)S(1)}, u32[]{:S(2)}, u32[]{:S(2)}) collective-permute-start(bf16[1,240,640]{2,1,0:T(8,128)(2,1)} %add_convert_fusion.18), channel_id=1, source_target_pairs={{0,16},{2,18},{4,20},{6,22},{8,24},{10,26},{12,28},{14,30},{16,0},... | collective-permute-start | bytes 921608 | tf_op jit(solution)/shard_map/ppermute | solution.py:35
  370.0 35.0 %collective-permute-start.58 = (bf16[1,240,640]{2,1,0:T(8,128)(2,1)}, bf16[1,240,640]{2,1,0:T(8,128)(2,1)S(1)}, u32[]{:S(2)}, u32[]{:S(2)}) collective-permute-start(bf16[1,240,640]{2,1,0:T(8,128)(2,1)} %add_convert_fusion.17), channel_id=1, source_target_pairs={{0,16},{2,18},{4,20},{6,22},{8,24},{10,26},{12,28},{14,30},{16,0},... | collective-permute-start | bytes 921608 | tf_op jit(solution)/shard_map/ppermute | solution.py:35
  370.6 39.9 %collective-permute-start.62 = (bf16[1,240,640]{2,1,0:T(8,128)(2,1)S(1)}, bf16[1,240,640]{2,1,0:T(8,128)(2,1)S(1)}, u32[]{:S(2)}, u32[]{:S(2)}) collective-permute-start(bf16[1,240,640]{2,1,0:T(8,128)(2,1)S(1)} %add_convert_fusion.16), channel_id=1, source_target_pairs={{0,16},{2,18},{4,20},{6,22},{8,24},{10,26},{12,28},{14,30},{16,0},... | collective-permute-start | bytes 921608 | tf_op jit(solution)/shard_map/ppermute | solution.py:35
  381.6 76.5 %collective-permute-start.37 = (f32[2,960]{1,0:T(2,128)S(1)}, f32[2,960]{1,0:T(2,128)S(1)}, u32[]{:S(2)}, u32[]{:S(2)}) collective-permute-start(f32[2,960]{1,0:T(2,128)S(1)} %fusion.15), channel_id=1, source_target_pairs={{0,8},{2,10},{4,12},{6,14},{8,0},{10,2},{12,4},{14,6},{16,24},{18,... | collective-permute-start | bytes 23048 | tf_op jit(solution)/shard_map/ppermute | solution.py:35
  382.7 30.2 %collective-permute-start.41 = (bf16[1,120,640]{2,1,0:T(8,128)(2,1)S(1)}, bf16[1,120,640]{2,1,0:T(8,128)(2,1)S(1)}, u32[]{:S(2)}, u32[]{:S(2)}) collective-permute-start(bf16[1,120,640]{2,1,0:T(8,128)(2,1)S(1)} %constant_dynamic-slice_fusion.8), channel_id=1, source_target_pairs={{0,1},{1,0},{2,3},{3,2},{4,5},{5,4},{6,7},{7,6},{8,9},{9,8},{10,11... | collective-permute-start | bytes 460808 | tf_op jit(solution)/shard_map/ppermute | solution.py:39
  398.5 13.6 %collective-permute-start.47 = (bf16[1,480,640]{2,1,0:T(8,128)(2,1)S(1)}, bf16[1,480,640]{2,1,0:T(8,128)(2,1)S(1)}, u32[]{:S(2)}, u32[]{:S(2)}) collective-permute-start(bf16[1,480,640]{2,1,0:T(8,128)(2,1)S(1)} %constant_dynamic-slice_fusion.6), channel_id=1, source_target_pairs={{0,1},{1,0},{2,3},{3,2},{4,5},{5,4},{6,7},{7,6},{8,9},{9,8},{10,11... | collective-permute-start | bytes 1843208 | tf_op jit(solution)/shard_map/ppermute | solution.py:39
  405.1 12.0 %collective-permute-start.55 = (bf16[1,240,640]{2,1,0:T(8,128)(2,1)S(1)}, bf16[1,240,640]{2,1,0:T(8,128)(2,1)S(1)}, u32[]{:S(2)}, u32[]{:S(2)}) collective-permute-start(bf16[1,240,640]{2,1,0:T(8,128)(2,1)S(1)} %add_convert_fusion.13), channel_id=1, source_target_pairs={{0,8},{2,10},{4,12},{6,14},{8,0},{10,2},{12,4},{14,6},{16,24},{18,... | collective-permute-start | bytes 921608 | tf_op jit(solution)/shard_map/ppermute | solution.py:35
  410.5 10.2 %collective-permute-start.59 = (bf16[1,240,640]{2,1,0:T(8,128)(2,1)S(1)}, bf16[1,240,640]{2,1,0:T(8,128)(2,1)S(1)}, u32[]{:S(2)}, u32[]{:S(2)}) collective-permute-start(bf16[1,240,640]{2,1,0:T(8,128)(2,1)S(1)} %add_convert_fusion.12), channel_id=1, source_target_pairs={{0,4},{2,6},{4,0},{6,2},{8,12},{10,14},{12,8},{14,10},{16,20},{18,... | collective-permute-start | bytes 921608 | tf_op jit(solution)/shard_map/ppermute | solution.py:35
  412.1 17.5 %collective-permute-start.63 = (bf16[1,240,640]{2,1,0:T(8,128)(2,1)S(1)}, bf16[1,240,640]{2,1,0:T(8,128)(2,1)S(1)}, u32[]{:S(2)}, u32[]{:S(2)}) collective-permute-start(bf16[1,240,640]{2,1,0:T(8,128)(2,1)S(1)} %add_convert_fusion.11), channel_id=1, source_target_pairs={{0,8},{2,10},{4,12},{6,14},{8,0},{10,2},{12,4},{14,6},{16,24},{18,... | collective-permute-start | bytes 921608 | tf_op jit(solution)/shard_map/ppermute | solution.py:35
  412.9 14.4 %collective-permute-start.48 = (bf16[1,240,640]{2,1,0:T(8,128)(2,1)S(1)}, bf16[1,240,640]{2,1,0:T(8,128)(2,1)S(1)}, u32[]{:S(2)}, u32[]{:S(2)}) collective-permute-start(bf16[1,240,640]{2,1,0:T(8,128)(2,1)S(1)} %constant_dynamic-slice_fusion.5), channel_id=1, source_target_pairs={{0,4},{2,6},{4,0},{6,2},{8,12},{10,14},{12,8},{14,10},{16,20},{18,... | collective-permute-start | bytes 921608 | tf_op jit(solution)/shard_map/ppermute | solution.py:35
  417.1 10.3 %collective-permute-start.42 = (bf16[1,120,640]{2,1,0:T(8,128)(2,1)S(1)}, bf16[1,120,640]{2,1,0:T(8,128)(2,1)S(1)}, u32[]{:S(2)}, u32[]{:S(2)}) collective-permute-start(bf16[1,120,640]{2,1,0:T(8,128)(2,1)S(1)} %add_convert_fusion.22), channel_id=1, source_target_pairs={{0,16},{2,18},{4,20},{6,22},{8,24},{10,26},{12,28},{14,30},{16,0},... | collective-permute-start | bytes 460808 | tf_op jit(solution)/shard_map/ppermute | solution.py:35
  420.7 27.7 %collective-permute-start.56 = (bf16[2,240,640]{2,1,0:T(8,128)(2,1)S(1)}, bf16[2,240,640]{2,1,0:T(8,128)(2,1)S(1)}, u32[]{:S(2)}, u32[]{:S(2)}) collective-permute-start(bf16[2,240,640]{2,1,0:T(8,128)(2,1)S(1)} %pad_maximum_fusion.6), channel_id=1, source_target_pairs={{0,4},{2,6},{4,0},{6,2},{8,12},{10,14},{12,8},{14,10},{16,20},{18,... | collective-permute-start | bytes 1843208 | tf_op jit(solution)/shard_map/ppermute | solution.py:35
  427.3 22.6 %collective-permute-start.60 = (bf16[2,240,640]{2,1,0:T(8,128)(2,1)S(1)}, bf16[2,240,640]{2,1,0:T(8,128)(2,1)S(1)}, u32[]{:S(2)}, u32[]{:S(2)}) collective-permute-start(bf16[2,240,640]{2,1,0:T(8,128)(2,1)S(1)} %pad_maximum_fusion.7), channel_id=1, source_target_pairs={{0,8},{2,10},{4,12},{6,14},{8,0},{10,2},{12,4},{14,6},{16,24},{18,... | collective-permute-start | bytes 1843208 | tf_op jit(solution)/shard_map/ppermute | solution.py:35
  427.4 18.6 %collective-permute-start.49 = (bf16[1,120,640]{2,1,0:T(8,128)(2,1)S(1)}, bf16[1,120,640]{2,1,0:T(8,128)(2,1)S(1)}, u32[]{:S(2)}, u32[]{:S(2)}) collective-permute-start(bf16[1,120,640]{2,1,0:T(8,128)(2,1)S(1)} %constant_dynamic-slice_fusion.4), channel_id=1, source_target_pairs={{0,8},{2,10},{4,12},{6,14},{8,0},{10,2},{12,4},{14,6},{16,24},{18,... | collective-permute-start | bytes 460808 | tf_op jit(solution)/shard_map/ppermute | solution.py:35
  429.6 28.1 %collective-permute-start.43 = (bf16[1,120,640]{2,1,0:T(8,128)(2,1)S(1)}, bf16[1,120,640]{2,1,0:T(8,128)(2,1)S(1)}, u32[]{:S(2)}, u32[]{:S(2)}) collective-permute-start(bf16[1,120,640]{2,1,0:T(8,128)(2,1)S(1)} %add_convert_fusion.21), channel_id=1, source_target_pairs={{0,8},{2,10},{4,12},{6,14},{8,0},{10,2},{12,4},{14,6},{16,24},{18,... | collective-permute-start | bytes 460808 | tf_op jit(solution)/shard_map/ppermute | solution.py:35
  446.0 10.4 %collective-permute-start.64 = (bf16[2,240,640]{2,1,0:T(8,128)(2,1)S(1)}, bf16[2,240,640]{2,1,0:T(8,128)(2,1)S(1)}, u32[]{:S(2)}, u32[]{:S(2)}) collective-permute-start(bf16[2,240,640]{2,1,0:T(8,128)(2,1)S(1)} %pad_maximum_fusion.8), channel_id=1, source_target_pairs={{0,4},{2,6},{4,0},{6,2},{8,12},{10,14},{12,8},{14,10},{16,20},{18,... | collective-permute-start | bytes 1843208 | tf_op jit(solution)/shard_map/ppermute | solution.py:35
  448.4 7.8 %collective-permute-start.50 = (bf16[1,120,640]{2,1,0:T(8,128)(2,1)S(1)}, bf16[1,120,640]{2,1,0:T(8,128)(2,1)S(1)}, u32[]{:S(2)}, u32[]{:S(2)}) collective-permute-start(bf16[1,120,640]{2,1,0:T(8,128)(2,1)S(1)} %add_convert_fusion.20), channel_id=1, source_target_pairs={{0,16},{2,18},{4,20},{6,22},{8,24},{10,26},{12,28},{14,30},{16,0},... | collective-permute-start | bytes 460808 | tf_op jit(solution)/shard_map/ppermute | solution.py:35
  449.9 38.5 %collective-permute-start.57 = (bf16[4,240,640]{2,1,0:T(8,128)(2,1)S(1)}, bf16[4,240,640]{2,1,0:T(8,128)(2,1)}, u32[]{:S(2)}, u32[]{:S(2)}) collective-permute-start(bf16[4,240,640]{2,1,0:T(8,128)(2,1)S(1)} %pad_maximum_fusion.1.mine_ref), channel_id=1, source_target_pairs={{0,2},{2,0},{4,6},{6,4},{8,10},{10,8},{12,14},{14,12},{16,18},{18,... | collective-permute-start | bytes 3686408 | tf_op jit(solution)/shard_map/ppermute | solution.py:35
  456.2 39.8 %collective-permute-start.61 = (bf16[4,240,640]{2,1,0:T(8,128)(2,1)S(1)}, bf16[4,240,640]{2,1,0:T(8,128)(2,1)}, u32[]{:S(2)}, u32[]{:S(2)}) collective-permute-start(bf16[4,240,640]{2,1,0:T(8,128)(2,1)S(1)} %pad_maximum_fusion.2.mine_ref), channel_id=1, source_target_pairs={{0,2},{2,0},{4,6},{6,4},{8,10},{10,8},{12,14},{14,12},{16,18},{18,... | collective-permute-start | bytes 3686408 | tf_op jit(solution)/shard_map/ppermute | solution.py:35
  456.5 6.3 %collective-permute-start.51 = (bf16[1,120,640]{2,1,0:T(8,128)(2,1)S(1)}, bf16[1,120,640]{2,1,0:T(8,128)(2,1)S(1)}, u32[]{:S(2)}, u32[]{:S(2)}) collective-permute-start(bf16[1,120,640]{2,1,0:T(8,128)(2,1)S(1)} %add_convert_fusion.19), channel_id=1, source_target_pairs={{0,8},{2,10},{4,12},{6,14},{8,0},{10,2},{12,4},{14,6},{16,24},{18,... | collective-permute-start | bytes 460808 | tf_op jit(solution)/shard_map/ppermute | solution.py:35
  457.7 46.1 %collective-permute-start.65 = (bf16[4,240,640]{2,1,0:T(8,128)(2,1)}, bf16[4,240,640]{2,1,0:T(8,128)(2,1)}, u32[]{:S(2)}, u32[]{:S(2)}) collective-permute-start(bf16[4,240,640]{2,1,0:T(8,128)(2,1)} %pad_maximum_fusion.3.mine_ref), channel_id=1, source_target_pairs={{0,2},{2,0},{4,6},{6,4},{8,10},{10,8},{12,14},{14,12},{16,18},{18,... | collective-permute-start | bytes 3686408 | tf_op jit(solution)/shard_map/ppermute | solution.py:35
  458.1 10.1 %collective-permute-start.44 = (bf16[2,120,640]{2,1,0:T(8,128)(2,1)S(1)}, bf16[2,120,640]{2,1,0:T(8,128)(2,1)S(1)}, u32[]{:S(2)}, u32[]{:S(2)}) collective-permute-start(bf16[2,120,640]{2,1,0:T(8,128)(2,1)S(1)} %pad_maximum_fusion.11), channel_id=1, source_target_pairs={{0,4},{2,6},{4,0},{6,2},{8,12},{10,14},{12,8},{14,10},{16,20},{18,... | collective-permute-start | bytes 921608 | tf_op jit(solution)/shard_map/ppermute | solution.py:35
  462.7 4.5 collective-permute-start.38
  467.3 7.6 %collective-permute-start.52 = (bf16[2,120,640]{2,1,0:T(8,128)(2,1)S(1)}, bf16[2,120,640]{2,1,0:T(8,128)(2,1)S(1)}, u32[]{:S(2)}, u32[]{:S(2)}) collective-permute-start(bf16[2,120,640]{2,1,0:T(8,128)(2,1)S(1)} %pad_maximum_fusion.12), channel_id=1, source_target_pairs={{0,4},{2,6},{4,0},{6,2},{8,12},{10,14},{12,8},{14,10},{16,20},{18,... | collective-permute-start | bytes 921608 | tf_op jit(solution)/shard_map/ppermute | solution.py:35
  468.2 6.8 %collective-permute-start.39 = (f32[2,960]{1,0:T(2,128)S(1)}, f32[2,960]{1,0:T(2,128)S(1)}, u32[]{:S(2)}, u32[]{:S(2)}) collective-permute-start(f32[2,960]{1,0:T(2,128)S(1)} %add.245), channel_id=1, source_target_pairs={{0,1},{1,0},{2,3},{3,2},{4,5},{5,4},{6,7},{7,6},{8,9},{9,8},{10,11... | collective-permute-start | bytes 23048 | tf_op jit(solution)/shard_map/ppermute | solution.py:39
  475.0 36.4 %collective-permute-start.53 = (bf16[4,120,640]{2,1,0:T(8,128)(2,1)S(1)}, bf16[4,120,640]{2,1,0:T(8,128)(2,1)}, u32[]{:S(2)}, u32[]{:S(2)}) collective-permute-start(bf16[4,120,640]{2,1,0:T(8,128)(2,1)S(1)} %pad_maximum_fusion.5.mine_ref), channel_id=1, source_target_pairs={{0,2},{2,0},{4,6},{6,4},{8,10},{10,8},{12,14},{14,12},{16,18},{18,... | collective-permute-start | bytes 1843208 | tf_op jit(solution)/shard_map/ppermute | solution.py:35
  (25 other events, 300.7 us)

commit v3 on v2

--- a/solution.py
+++ b/solution.py
@@ -217,13 +217,21 @@
 
 
 def project_kernel(
-    at_ref, x_ref, doc_ref, cos_ref, sin_ref, gain_ref, own_ref, p0, p1, p2, p3,
-    flip_ref, q_ref, k_ref, v_ref, in_ref, w_ref,
+    at_ref, x_ref, doc_ref, cos_ref, sin_ref, gain_ref, wq_ref, wk_ref, wv_ref, p0, p1, p2, p3,
+    flip_ref, q_ref, k_ref, v_ref, w_ref, in_ref, own_ref,
 ):
     step = pl.program_id(0)
 
     @pl.when(step == 0)
     def _():
+        w_key, w_value = wk_ref[...].T, wv_ref[...].T
+        deep = GROUP * HEAD_SIZE
+        pad = jnp.zeros((own_ref.shape[0], WIDE - SPAN), jnp.bfloat16)
+        columns = []
+        for g in range(KEY_VALUE_HEADS):
+            span = slice(g * HEAD_SIZE, (g + 1) * HEAD_SIZE)
+            columns += [wq_ref[:, g * deep : (g + 1) * deep], w_key[:, span], w_value[:, span], pad]
+        own_ref[...] = jnp.concatenate(columns, axis=1)
         fill_rows(at_ref, w_ref, own_ref, (p0, p1, p2, p3))
         x = x_ref[...].astype(jnp.float32)
         inverse = lax.rsqrt(jnp.mean(x * x, axis=0, keepdims=True) + EPS)
@@ -255,29 +263,35 @@
 def project(at, x, documents, cosine, sine, gain, own, parts):
     width, rows = x.shape
     table = whole((rows, LANES))
-    across = own.shape[1]
+    across = parts[0].shape[1]
     return call(
         project_kernel,
         (KEY_VALUE_HEADS,),
-        [whole((width, rows)), whole((rows, 1)), table, table, whole((width, 1)), whole(own.shape)]
+        [whole((width, rows)), whole((rows, 1)), table, table, whole((width, 1))]
+        + [whole(w.shape) for w in own]
         + [whole(parts[0].shape)] * 4,
         [
             whole((width, rows)),
             pl.BlockSpec((GROUP, rows, LANES), lambda g, a: (g, 0, 0)),
             pl.BlockSpec((1, rows, LANES), lambda g, a: (g, 0, 0)),
             pl.BlockSpec((1, rows, LANES), lambda g, a: (g, 0, 0)),
+            whole((width, across)),
         ],
         [
             struct((width, rows), jnp.bfloat16),
             struct((QUERY_HEADS, rows, LANES), jnp.bfloat16),
             struct((KEY_VALUE_HEADS, rows, LANES), jnp.bfloat16),
             struct((KEY_VALUE_HEADS, rows, LANES), jnp.bfloat16),
+            struct((width, across), jnp.bfloat16),
         ],
-        scratch=[pltpu.VMEM((rows, width), jnp.bfloat16), pltpu.VMEM((width, across), jnp.bfloat16)],
+        scratch=[
+            pltpu.VMEM((rows, width), jnp.bfloat16),
+            pltpu.VMEM((width // 2, across), jnp.bfloat16),
+        ],
         flops=2 * rows * width * WIDE * KEY_VALUE_HEADS,
         prefetch=1,
         move=20_000_000,
-    )(at, x, documents, cosine, sine, gain, own, *parts)
+    )(at, x, documents, cosine, sine, gain, *own, *parts)
 
 
 def attend_kernel(q_ref, k_ref, v_ref, o_ref, qb_ref):
@@ -467,68 +481,56 @@
 
 def middle_kernel(
     at_ref, mid_ref, y0_ref, y1_ref, d0_ref, d1_ref, dy_ref, o0_ref, o1_ref, gain_ref,
-    own_ref, p0, p1, p2, p3, mixed_ref, grad_ref, do_ref, gain_out, w_out, w_total, w_ref,
+    own_ref, p0, p1, p2, p3, mixed_ref, grad_ref, branch_ref, do_ref, gain_out, w_ref,
 ):
     step = pl.program_id(0)
 
     @pl.when(step == 0)
     def _():
         fill_rows(at_ref, w_ref, own_ref, (p0, p1, p2, p3))
+        gain_out[...] = jnp.zeros_like(gain_out)
 
     middle = mid_ref[...]
-    mixed_ref[...] = (middle + y0_ref[...] + y1_ref[...]).T.astype(jnp.bfloat16)
+    mixed_ref[...] = (middle + y0_ref[...] + y1_ref[...]).astype(jnp.bfloat16).T
     inverse = lax.rsqrt(jnp.mean(middle * middle, axis=-1, keepdims=True) + EPS)
     normed = middle * inverse
     back = d0_ref[...] + d1_ref[...]
     product = back * normed
-    weighted = product * gain_ref[...]
-    mean = jnp.mean(weighted, axis=-1, keepdims=True)
+    mean = jnp.mean(product * gain_ref[...], axis=-1, keepdims=True)
     grad = dy_ref[...].astype(jnp.float32) + inverse * (back * gain_ref[...] - normed * mean)
     grad_ref[...] = grad
     branch = grad.astype(jnp.bfloat16)
+    branch_ref[...] = branch
+    gain_out[...] += jnp.sum(product, axis=0, keepdims=True)
     deep = GROUP * HEAD_SIZE
-    partial_gain = jnp.sum(product, axis=0, keepdims=True)
-
-    @pl.when(step == 0)
-    def _():
-        gain_out[...] = partial_gain
-
-    @pl.when(step > 0)
-    def _():
-        gain_out[...] += partial_gain
-
     lane = lanes_of((BLOCK, LANES))
+    inner = lane < HEAD_SIZE
     for g in range(KEY_VALUE_HEADS):
-        span = pl.ds(g * deep, deep)
         heads = o0_ref[g] if g < o0_ref.shape[0] else o1_ref[g - o0_ref.shape[0]]
-        part = dot_tn(heads, branch)
-
-        @pl.when(step == 0)
-        def _(part=part, span=span):
-            w_total[span, :] = part
-
-        @pl.when(step > 0)
-        def _(part=part, span=span):
-            w_total[span, :] += part
-
-        upstream = dot_nt(branch, w_ref[span, :]).astype(jnp.bfloat16).astype(jnp.float32)
-        inner = upstream * heads.astype(jnp.float32)
+        upstream = dot_nt(branch, w_ref[pl.ds(g * deep, deep), :]).astype(jnp.bfloat16)
+        upstream = upstream.astype(jnp.float32)
+        both = upstream * heads.astype(jnp.float32)
+        pair, pair_both = upstream[:, :LANES], both[:, :LANES]
+        wide = (pair, pltpu.roll(pair, HEAD_SIZE, 1), upstream[:, LANES:])
+        sums = (
+            jnp.sum(jnp.where(inner, pair_both, 0.0), axis=-1, keepdims=True),
+            jnp.sum(jnp.where(inner, 0.0, pair_both), axis=-1, keepdims=True),
+            jnp.sum(both[:, LANES:], axis=-1, keepdims=True),
+        )
         for h in range(GROUP):
-            at = h * HEAD_SIZE
-            delta = jnp.sum(inner[:, at : at + HEAD_SIZE], axis=-1, keepdims=True)
-            own = upstream[:, at : at + HEAD_SIZE]
-            wide = jnp.concatenate([own, jnp.zeros_like(own)], axis=1)
-            do_ref[g * GROUP + h] = put_parts(wide, -delta, HEAD_SIZE).astype(jnp.bfloat16)
-
-    @pl.when(step == pl.num_programs(0) - 1)
-    def _():
-        w_out[...] = w_total[...].astype(jnp.bfloat16)
+            delta = -sums[h]
+            high = delta.astype(jnp.bfloat16).astype(jnp.float32)
+            low = delta - high
+            own = wide[h]
+            if own.shape[1] < LANES:
+                own = jnp.concatenate([own, jnp.zeros_like(own)], axis=1)
+            rest = jnp.where(lane == HEAD_SIZE, high, jnp.where(lane == HEAD_SIZE + 1, low, 0.0))
+            do_ref[g * GROUP + h] = jnp.where(inner, own, rest).astype(jnp.bfloat16)
 
 
 def middle_back(at, middle, y0, y1, d0, d1, dy, heads, gain, own, parts):
     rows, width = middle.shape
     band = pl.BlockSpec((BLOCK, width), lambda i, a: (i, 0))
-    square = (2 * own.shape[0], width)
     return call(
         middle_kernel,
         (rows // BLOCK,),
@@ -539,21 +541,21 @@
         [
             pl.BlockSpec((width, BLOCK), lambda i, a: (0, i)),
             band,
+            band,
             pl.BlockSpec((QUERY_HEADS, BLOCK, LANES), lambda i, a: (0, i, 0)),
             whole((1, width)),
-            whole(square),
         ],
         [
             struct((width, rows), jnp.bfloat16),
             struct((rows, width), jnp.float32),
+            struct((rows, width), jnp.bfloat16),
             struct((QUERY_HEADS, rows, LANES), jnp.bfloat16),
             struct((1, width), jnp.float32),
-            struct(square, jnp.bfloat16),
         ],
-        scratch=[pltpu.VMEM(square, jnp.float32), pltpu.VMEM(square, jnp.bfloat16)],
-        flops=2 * 2 * rows * width * width,
+        scratch=[pltpu.VMEM((2 * own.shape[0], width), jnp.bfloat16)],
+        flops=2 * rows * width * width,
         prefetch=1,
-        move=40_000_000,
+        move=30_000_000,
     )(at, middle, y0, y1, d0, d1, dy, *heads, gain, own, *parts)
 
 
@@ -621,121 +623,178 @@
 
 def weight_kernel(flip_ref, *refs):
     flip = flip_ref[...]
-    parts = []
-    for ref in refs[:-1]:
-        if len(ref.shape) == 2:
-            parts.append(ref[...])
-            continue
-        for g in range(ref.shape[0]):
-            parts.append(dot(flip, ref[g])[:, :SPAN].astype(jnp.bfloat16))
+    parts = [dot(flip, ref[0])[:, :SPAN].astype(jnp.bfloat16) for ref in refs[:-1]]
     refs[-1][...] = jnp.concatenate(parts, axis=1)
 
 
-def weight_grads(flip, pieces):
+def weight_grads(flip, backs):
     width, rows = flip.shape
     half = width // 2
-    across = sum(p.shape[1] if p.ndim == 2 else p.shape[0] * SPAN for p in pieces)
-    specs = [
-        pl.BlockSpec((half, p.shape[1]), lambda i: (i, 0)) if p.ndim == 2 else whole(p.shape)
-        for p in pieces
-    ]
+    across = len(backs) * SPAN
     return call(
         weight_kernel,
         (2,),
-        [pl.BlockSpec((half, rows), lambda i: (i, 0))] + specs,
+        [pl.BlockSpec((half, rows), lambda i: (i, 0))] + [whole(b.shape) for b in backs],
         pl.BlockSpec((half, across), lambda i: (i, 0)),
         struct((width, across), jnp.bfloat16),
         flops=2 * rows * width * across,
         move=10_000_000,
-    )(flip, *pieces)
-
-
-def finish_kernel(
-    at_ref, x_ref, mid_ref, da_ref, db_ref, dc_ref, gain_ref, own_ref, p0, p1, p2, p3,
-    out_ref, gain_out, w_ref,
-):
-    @pl.when(pl.program_id(0) == 0)
-    def _():
-        fill_rows(at_ref, w_ref, own_ref, (p0, p1, p2, p3))
-
+    )(flip, *backs)
+
+
+def near_kernel(flip_ref, back_ref, branch_ref, o0_ref, o1_ref, out_ref):
+    deep = GROUP * HEAD_SIZE
+    branch = branch_ref[...]
+    for g in range(KEY_VALUE_HEADS):
+        heads = o0_ref[g] if g < o0_ref.shape[0] else o1_ref[g - o0_ref.shape[0]]
+        span = pl.ds(g * deep, deep)
+        left = dot_tn(heads, branch)
+        right = dot(flip_ref[span, :], back_ref[0])[:, :SPAN]
+        out_ref[span, :] = jnp.concatenate([left, right], axis=1).astype(jnp.bfloat16)
+
+
+def near_grads(flip, back, branch, heads):
+    width, rows = flip.shape
+    args = (flip, back, branch, *heads)
+    return call(
+        near_kernel,
+        (1,),
+        [whole(a.shape) for a in args],
+        whole((width, width + SPAN)),
+        struct((width, width + SPAN), jnp.bfloat16),
+        flops=2 * rows * width * (width + SPAN),
+        move=12_000_000,
+    )(*args)
+
+
+def finish_kernel(x_ref, mid_ref, *refs):
+    gain_ref, w_ref, out_ref, gain_out = refs[KEY_VALUE_HEADS:]
     x = x_ref[...].astype(jnp.float32).T
     inverse = lax.rsqrt(jnp.mean(x * x, axis=-1, keepdims=True) + EPS)
     normed = x * inverse
     back = jnp.zeros_like(x)
-    g = 0
-    for ref in (da_ref, db_ref, dc_ref):
-        for k in range(ref.shape[0]):
-            back += dot_nt(ref[k], w_ref[:, pl.ds(g * WIDE, WIDE)])
-            g += 1
+    for g in range(KEY_VALUE_HEADS):
+        back += dot_nt(refs[g][0], w_ref[:, pl.ds(g * WIDE, WIDE)])
     product = back * normed
-    partial_gain = jnp.sum(product, axis=0, keepdims=True)
 
     @pl.when(pl.program_id(0) == 0)
     def _():
-        gain_out[...] = partial_gain
-
-    @pl.when(pl.program_id(0) > 0)
-    def _():
-        gain_out[...] += partial_gain
-
+        gain_out[...] = jnp.zeros_like(gain_out)
+
+    gain_out[...] += jnp.sum(product, axis=0, keepdims=True)
     mean = jnp.mean(product * gain_ref[...], axis=-1, keepdims=True)
     grad = mid_ref[...] + inverse * (back * gain_ref[...] - normed * mean)
-    out_ref[...] = grad.T.astype(jnp.bfloat16)
-
-
-def finish(at, x, middle_grad, backs, gain, own, parts):
+    out_ref[...] = grad.astype(jnp.bfloat16).T
+
+
+def finish(x, middle_grad, backs, gain, w_first):
     width, rows = x.shape
-    side = pl.BlockSpec((width, BLOCK), lambda i, a: (0, i))
+    side = pl.BlockSpec((width, BLOCK), lambda i: (0, i))
     return call(
         finish_kernel,
         (rows // BLOCK,),
-        [side, pl.BlockSpec((BLOCK, width), lambda i, a: (i, 0))]
-        + [pl.BlockSpec((b.shape[0], BLOCK, WIDE), lambda i, a: (0, i, 0)) for b in backs]
-        + [whole((1, width)), whole(own.shape)]
-        + [whole(parts[0].shape)] * 4,
+        [side, pl.BlockSpec((BLOCK, width), lambda i: (i, 0))]
+        + [pl.BlockSpec((1, BLOCK, WIDE), lambda i: (0, i, 0)) for _ in backs]
+        + [whole((1, width)), whole(w_first.shape)],
         [side, whole((1, width))],
         [struct((width, rows), jnp.bfloat16), struct((1, width), jnp.float32)],
-        scratch=[pltpu.VMEM((2 * own.shape[0], own.shape[1]), jnp.bfloat16)],
         flops=2 * rows * width * WIDE * KEY_VALUE_HEADS,
-        prefetch=1,
         move=14_000_000,
-    )(at, x, middle_grad, *backs, gain, own, *parts)
+    )(x, middle_grad, *backs, gain, w_first)
 
 
 def widen_kernel(at_ref, mine_ref, other_ref, out_ref):
-    core = at_ref[2]
-
-    @pl.when(pl.program_id(0) == core)
+    cut = mine_ref.shape[2]
+    mine, other = mine_ref[0].astype(jnp.float32), other_ref[0].astype(jnp.float32)
+
+    @pl.when(at_ref[2] == 0)
     def _():
-        out_ref[...] = mine_ref[0].astype(jnp.float32)
-
-    @pl.when(pl.program_id(0) != core)
+        out_ref[:, :cut] = mine
+        out_ref[:, cut:] = other
+
+    @pl.when(at_ref[2] != 0)
     def _():
-        out_ref[...] = other_ref[0].astype(jnp.float32)
+        out_ref[:, :cut] = other
+        out_ref[:, cut:] = mine
+
+
+def came_at(at, j, order):
+    apart = {2: at[1] ^ (j // 2), 4: at[4] ^ (j % 2)}
+    return apart[order[0]] + 2 * apart[order[1]]
 
 
 def widen(at, mine, other, order, spread):
     _, rows, columns = mine.shape
-
-    def place(c, j, a):
-        apart = {2: a[1] ^ (j // 2), 4: a[4] ^ (j % 2)}
-        return (apart[order[0]] + 2 * apart[order[1]], 0, 0)
-
     if spread:
         shape = (2 * rows, 4 * columns)
-        out = pl.BlockSpec((rows, columns), lambda c, j, a: (j % 2, 2 * (j // 2) + c))
+        out = pl.BlockSpec((rows, 2 * columns), lambda j, a: (j % 2, j // 2))
     else:
         shape = (4 * rows, 2 * columns)
-        out = pl.BlockSpec((rows, columns), lambda c, j, a: (j, c))
+        out = pl.BlockSpec((rows, 2 * columns), lambda j, a: (j, 0))
     return call(
         widen_kernel,
-        (2, 4),
-        [pl.BlockSpec((1, rows, columns), place)] * 2,
+        (4,),
+        [pl.BlockSpec((1, rows, columns), lambda j, a: (came_at(a, j, order), 0, 0))] * 2,
         out,
         struct(shape, jnp.float32),
         prefetch=1,
         move=10_000_000,
     )(at, mine, other)
+
+
+def unpack_kernel(
+    at_ref, near0, near1, mid0, mid1, far0, far1, q_ref, k_ref, v_ref, out_ref,
+    near_ref, mid_ref, far_ref,
+):
+    core, side = at_ref[2], at_ref[1]
+    rows, columns = near0.shape[1:]
+    for j in range(4):
+        at = came_at(at_ref, j, (4, 2))
+        mine, other = near0[at].astype(jnp.float32), near1[at].astype(jnp.float32)
+        left, right = jnp.where(core == 0, mine, other), jnp.where(core == 0, other, mine)
+        near_ref[j * rows : (j + 1) * rows, :] = jnp.concatenate([left, right], axis=1)
+    for mine_ref, other_ref, into in ((mid0, mid1, mid_ref), (far0, far1, far_ref)):
+        for c in range(2):
+            for y in range(2):
+                at = y ^ side
+                mine, other = mine_ref[at].astype(jnp.float32), other_ref[at].astype(jnp.float32)
+                start = (2 * c + y) * mine.shape[0]
+                into[start : start + mine.shape[0], :] = jnp.where(core == c, mine, other)
+    near, mid, far = near_ref[...], mid_ref[...], far_ref[...]
+    deep = GROUP * HEAD_SIZE
+    split = near.shape[1] - SPAN
+    groups = [near[:, split:], mid[:, :SPAN], mid[:, SPAN:], far[:, :SPAN], far[:, SPAN:]]
+    out_ref[...] = near[:, :split]
+    q_ref[...] = jnp.concatenate([g[:, :deep] for g in groups], axis=1)
+    k_ref[...] = jnp.concatenate([g[:, deep : deep + HEAD_SIZE] for g in groups], axis=1).T
+    v_ref[...] = jnp.concatenate([g[:, deep + HEAD_SIZE :] for g in groups], axis=1).T
+
+
+def unpack(at, near, mid, far):
+    _, rows, columns = near[0].shape
+    args = (*near, *mid, *far)
+    tall = 4 * rows
+    key_columns = KEY_VALUE_HEADS * HEAD_SIZE
+    shapes = [
+        (tall, QUERY_HEADS * HEAD_SIZE),
+        (key_columns, tall),
+        (key_columns, tall),
+        (tall, 2 * columns - SPAN),
+    ]
+    return call(
+        unpack_kernel,
+        (1,),
+        [whole(a.shape) for a in args],
+        [whole(shape) for shape in shapes],
+        [struct(shape, jnp.float32) for shape in shapes],
+        scratch=[
+            pltpu.VMEM((tall, 2 * columns), jnp.float32),
+            pltpu.VMEM((tall, 2 * SPAN), jnp.float32),
+            pltpu.VMEM((tall, 2 * SPAN), jnp.float32),
+        ],
+        prefetch=1,
+        move=8_000_000,
+    )(at, *args)
 
 
 def tie(value, *others):
@@ -770,25 +829,23 @@
     return halve(value, rep_bit(step), axes[step], partial(swap_rep, bit=step))
 
 
-def end_sum(value, order):
+def over_z(value):
     bit = 8
     while bit < lax.axis_size("rep"):
         value = add_up(value, swap_rep(value, bit))
         bit *= 2
-    return spread_sum(value, order)
-
-
-def spread_sum(value, order):
-    for step in order:
-        value = jnp.concatenate([value, swap_rep(value, step)], axis=0)
-    return value, swap_rep(value, 1)
-
-
-def split_cores(grad):
+    return value
+
+
+def back_step(value, step):
+    return jnp.concatenate([value, swap_rep(value, step)], axis=0)
+
+
+def split_cores(grad, axis):
     core = rep_bit(1)
-    half = grad.shape[-1] // 2
-    send = lax.dynamic_slice_in_dim(grad, (1 - core) * half, half, grad.ndim - 1)
-    keep = lax.dynamic_slice_in_dim(grad, core * half, half, grad.ndim - 1)
+    half = grad.shape[axis] // 2
+    send = lax.dynamic_slice_in_dim(grad, (1 - core) * half, half, axis)
+    keep = lax.dynamic_slice_in_dim(grad, core * half, half, axis)
     return send, keep
 
 
@@ -829,8 +886,8 @@
             narrow(w_query), narrow(key_weight_matrix), narrow(value_weight_matrix)
         )
         came_first = swap_shard(part_first, 1)
-        own_first = first_rows(w_query, key_weight_matrix, value_weight_matrix)
-        gains = jnp.stack([gain_attn, gain_mlp]).astype(jnp.float32)
+        own_first = (w_query, key_weight_matrix.T, value_weight_matrix.T)
+        gains = tie(jnp.stack([gain_attn, gain_mlp]).astype(jnp.float32), part_first)
         gains = place_pair(gains, swap_shard(gains, 1), x, 1)
         column = (2 * side + other) * cut
         part_out = narrow(w_out)
@@ -851,10 +908,11 @@
     else:
         x = side = core = depth = zero
         other = 1 - core
-        full = gather_rows(first_rows(w_query, key_weight_matrix, value_weight_matrix))
+        full_first = [gather_rows(w) for w in (w_query, key_weight_matrix, value_weight_matrix)]
         full_out = gather_rows(w_out)
         starts = [half + window(None, c, y, half) for c in (0, 1) for y in (0, 1)]
-        own_first, parts_first = full[:half], [full[s : s + tall] for s in starts]
+        own_first = (full_first[0][:half], full_first[1][:half].T, full_first[2][:half].T)
+        parts_first = [first_rows(*(w[s : s + tall] for w in full_first)) for s in starts]
         own_out, parts_out = full_out[:half], [full_out[s : s + tall] for s in starts]
         gains = gather_rows(jnp.pad(jnp.stack([gain_attn, gain_mlp], axis=1), ((0, 0), (0, 126))))
         gains = gains[:, :2].T.astype(jnp.float32)
@@ -883,7 +941,7 @@
     )
     gain_one, gain_two = gains[:1], gains[1:]
 
-    flip_one, q, k, v = project(
+    flip_one, q, k, v, w_first = project(
         at, x_t, segments[0][:, None], cosine, sine, gain_one.T, own_first, parts_first
     )
     if fast:
@@ -904,49 +962,90 @@
         at, tie(entry, d0), flip, dy, dy_t,
         (own_gate, *parts_gate[2:]), (own_up, *parts_up[2:]), (own_down, *parts_down[2:]),
     )
-    wide, tower = {2: 2, 4: 1}, {2: 1, 4: 1}
+    wide, tower, low = {2: 2, 4: 1}, {2: 1, 4: 1}, {2: 1}
+    cube = (2, half, -1)
     if fast:
-        cube = (2, half, 2 * cut)
         gate = start_sum(gate0.reshape(cube), gate1.reshape(cube))
         up = start_sum(up0.reshape(cube), up1.reshape(cube))
         down = start_sum(down0, down1)
         y1, gate, up, down = lax.optimization_barrier((y1, gate, up, down))
         gate, up, down = one_step(gate, 0, wide), one_step(up, 4, wide), one_step(down, 2, tower)
-    mixed, middle_grad, do, grad_gain_two, grad_out = middle_back(
+    mixed, middle_grad, branch, do, grad_gain_two = middle_back(
         at, middle, y0, y1, d0, d1, dy, heads, gain_two, own_out, parts_out
     )
-    rope = (cosine, sine)
-    backs0 = attend_back(back0, k, v, do, *rope, 0, 0, 1)
-    near = weight_grads(flip_one, (grad_out, backs0))
+    backs = []
+
+    def group_back(do):
+        g = len(backs)
+        held, begin = (back0, g) if g < 3 else (back1, g - 3)
+        backs.append(attend_back(held, k, v, do, cosine, sine, g, begin, 1))
+
+    group_back(do)
     if fast:
-        near = start_sum(*split_cores(near.reshape(2, half, -1)))
-        do, gate, up, down = lax.optimization_barrier((do, gate, up, down))
+        gate, up, down, backs[0] = lax.optimization_barrier((gate, up, down, backs[0]))
         gate, up, down = one_step(gate, 2, wide), one_step(up, 2, wide), one_step(down, 0, tower)
-    backs1 = attend_back(back0, k, v, do, *rope, 1, 1, 2)
+    near = near_grads(flip_one, backs[0], branch, heads)
+    group_back(tie(do, near))
     if fast:
-        do, backs1, gate, up, down, near = lax.optimization_barrier(
-            (do, backs1, gate, up, down, near)
+        near = start_sum(*split_cores(near.reshape(cube), 2))
+        gate, up, down, near, backs[1] = lax.optimization_barrier(
+            (gate, up, down, near, backs[1])
         )
         gate, up, down = one_step(gate, 4, wide), one_step(up, 0, wide), one_step(down, 4, tower)
         near = one_step(near, 2, tower)
-    backs2 = attend_back(back1, k, v, do, *rope, 3, 0, 2)
+    group_back(tie(do, backs[1]))
     if fast:
-        backs1, gate, up, down, near = lax.optimization_barrier((backs1, gate, up, down, near))
+        gate, up, down, near, backs[2] = lax.optimization_barrier(
+            (gate, up, down, near, backs[2])
+        )
+        gate = over_z(gate)
         near = one_step(near, 4, tower)
-    far = weight_grads(flip_one, (backs1, backs2))
-    grad_tokens, grad_gain_one = finish(
-        at, x_t, middle_grad, (backs0, backs1, backs2), gain_one, own_first, parts_first
-    )
+    mid = weight_grads(flip_one, backs[1:3])
+    group_back(tie(do, mid))
+    if fast:
+        mid = start_sum(*split_cores(mid.reshape(cube), 1))
+        gate, mid, near, backs[3] = lax.optimization_barrier((gate, mid, near, backs[3]))
+        up = over_z(up)
+        gate = back_step(gate, 4)
+        near, mid = one_step(near, 0, tower), one_step(mid, 0, low)
+    group_back(tie(do, backs[3]))
+    if fast:
+        gate, up, near, mid, backs[4] = lax.optimization_barrier((gate, up, near, mid, backs[4]))
+        down = over_z(down)
+        gate, up = back_step(gate, 2), back_step(up, 2)
+        mid = one_step(mid, 2, low)
+    far = weight_grads(flip_one, backs[3:])
+    if fast:
+        far = start_sum(*split_cores(far.reshape(cube), 1))
+        far, mid, middle_grad = lax.optimization_barrier((far, mid, middle_grad))
+        far = one_step(far, 0, low)
+        near = over_z(near)
+        mid = add_up(mid, swap_rep(mid, 4))
+    grad_tokens, grad_gain_one = finish(x_t, middle_grad, backs, gain_one, w_first)
     gain_sums = reduce_gains(jnp.concatenate([grad_gain_one, grad_gain_two]))
     if fast:
-        far = start_sum(*split_cores(far.reshape(2, half, -1)))
-        near = one_step(near, 0, tower)
-        far = one_step(one_step(one_step(far, 0, tower), 2, tower), 4, tower)
-        sum_gate = widen(at, *end_sum(gate, (4, 2)), (4, 2), True)
-        sum_up = widen(at, *end_sum(up, (2, 4)), (2, 4), True)
-        sum_down = widen(at, *end_sum(down, (4, 2)), (4, 2), False).T
-        sum_near = widen(at, *end_sum(near, (4, 2)), (4, 2), False)
-        sum_far = widen(at, *end_sum(far, (4, 2)), (4, 2), False)
+        far, near, mid, up, gate, down, grad_tokens = lax.optimization_barrier(
+            (far, near, mid, up, gate, down, grad_tokens)
+        )
+        far = one_step(far, 2, low)
+        mid = over_z(mid)
+        down, up = back_step(down, 4), back_step(up, 4)
+        near = back_step(near, 4)
+        sum_gate = widen(at, gate, swap_rep(gate, 1), (4, 2), True)
+        far, near, down, sum_gate = lax.optimization_barrier((far, near, down, sum_gate))
+        far = add_up(far, swap_rep(far, 4))
+        near, down = back_step(near, 2), back_step(down, 2)
+        sum_up = widen(at, up, swap_rep(up, 1), (2, 4), True)
+        far, sum_up, mid = lax.optimization_barrier((far, sum_up, mid))
+        far = over_z(far)
+        mid = back_step(mid, 2)
+        sum_down = widen(at, down, swap_rep(down, 1), (4, 2), False).T
+        far, sum_down = lax.optimization_barrier((far, sum_down))
+        far = back_step(far, 2)
+        grad_query, grad_key, grad_value, grad_out = unpack(
+            at, (near, swap_rep(near, 1)), (mid, swap_rep(mid, 1)), (far, swap_rep(far, 1))
+        )
+        grad_key, grad_value = grad_key.T, grad_value.T
     else:
         def whole_grad(two, one):
             both = jnp.stack([one.reshape(width, 2, cut), two.reshape(width, 2, cut)], axis=2)
@@ -957,20 +1056,23 @@
         sum_up = reduce_rows(whole_grad(up0, up1), (4, 2, 0), across)
         downs = [d.transpose(1, 0, 2) for d in (down0, down1)]
         sum_down = reduce_rows(whole_grad(*downs).T, (2, 0, 4), upright)
-        sum_near = reduce_rows(near, (0, 2, 4), across)
-        sum_far = reduce_rows(far, (0, 4, 2), across)
-    tall_rows = sum_near.shape[0]
-    groups = jnp.concatenate([sum_near[:, columns:], sum_far], axis=1)
-    groups = groups.reshape(tall_rows, KEY_VALUE_HEADS, SPAN)
-    deep = GROUP * HEAD_SIZE
+        sums = [reduce_rows(part, (0, 2, 4), across) for part in (near, mid, far)]
+        tall_rows = sums[0].shape[0]
+        grad_out = sums[0][:, :columns]
+        groups = jnp.concatenate([sums[0][:, columns:], *sums[1:]], axis=1)
+        groups = groups.reshape(tall_rows, KEY_VALUE_HEADS, SPAN)
+        deep = GROUP * HEAD_SIZE
+        grad_query = groups[:, :, :deep].reshape(tall_rows, columns)
+        grad_key = groups[:, :, deep : deep + HEAD_SIZE].reshape(tall_rows, key_columns)
+        grad_value = groups[:, :, deep + HEAD_SIZE :].reshape(tall_rows, key_columns)
     return (
         mixed.T[None],
         grad_tokens.T[None],
         gain_sums[0],
-        groups[:, :, :deep].reshape(tall_rows, columns),
-        groups[:, :, deep : deep + HEAD_SIZE].reshape(tall_rows, key_columns),
-        groups[:, :, deep + HEAD_SIZE :].reshape(tall_rows, key_columns),
-        sum_near[:, :columns],
+        grad_query,
+        grad_key,
+        grad_value,
+        grad_out,
         gain_sums[1],
         sum_gate,
         sum_up,

time: 541 us -> 471 us (0.87)
  local copies, waits for them, and re-layouts: 59 us -> 24.9 us
  Pallas kernels: 276 us -> 257 us
  other arithmetic: 33.7 us -> 19.7 us
  waiting for transfers between devices: 108 us -> 94.5 us
  starting transfers between devices: 52.9 us -> 63.9 us
    ppermute x54 -> x59, waiting for transfers between devices: 97.5 us -> 67.9 us  [swap_rep(): return lax.ppermute(value, 'rep', bit_swap(lax.axis_size('rep'), bit))]
    ppermute x12 -> x13, waiting for transfers between devices: 10.1 us -> 26.6 us  [swap_shard(): return lax.ppermute(value, 'shard', bit_swap(lax.axis_size('shard'), bit))]
    pallas_call x1, Pallas kernels: 32.2 us -> 17 us  [middle_back(): call(middle_kernel, (rows // BLOCK,), [band] * 6 + head_specs(heads) + [w...]
    unnamed x67 -> x71, local copies, waits for them, and re-layouts: 17 us -> 3.77 us
    slice x6 -> x1, local copies, waits for them, and re-layouts: 7.8 us -> 0.07 us  [the longest x1 3.05 us: per_device(): sum_near[:, :columns]]
    ppermute x54 -> x59, starting transfers between devices: 41.1 us -> 48.8 us  [swap_rep(): return lax.ppermute(value, 'rep', bit_swap(lax.axis_size('rep'), bit))]
    pallas_call x5, Pallas kernels: 36.3 us -> 28.9 us  [the longest x3 15.6 us: widen(): call(widen_kernel, (4,), [pl.BlockSpec((1, rows, columns), lambda j, a: (...]
    concatenate x11 -> x5, other arithmetic: 6.86 us -> 0.37 us  [back_step(): return jnp.concatenate([value, swap_rep(value, step)], axis=0)]
  transfers between devices with their start and end apart: 66 -> 72, of which waited for: 21 -> 22; matrix products, arithmetic and copies ran while one was open for 13% -> 7% of each run, Pallas kernels for 49% -> 54%
where the time goes in v3:
time: 471 us; the launch traced here: 462 us
  Pallas kernels  257 us (55%)
  waiting for transfers between devices  94.5 us (20%)
  starting transfers between devices  63.9 us (14%)
  local copies, waits for them, and re-layouts  24.9 us (5%)
  other arithmetic  19.7 us (4%)
    pallas_call x2, Pallas kernels, mix(): call(mix_kernel, (2,), [full, turned, full, turned, side, piece, piece, s...  84.7 us
    ppermute x59, waiting for transfers between devices, swap_rep(): return lax.ppermute(value, 'rep', bit_swap(lax.axis_size('rep'), bit))  67.9 us
    pallas_call x5, Pallas kernels, attend_back(): call(attend_back_kernel, (groups,), [pl.BlockSpec((GROUP, rows, LANES), l...  53 us
    ppermute x59, starting transfers between devices, swap_rep(): return lax.ppermute(value, 'rep', bit_swap(lax.axis_size('rep'), bit))  48.8 us
    ppermute x13, waiting for transfers between devices, swap_shard(): return lax.ppermute(value, 'shard', bit_swap(lax.axis_size('shard'), bit))  26.6 us
    pallas_call x2, Pallas kernels, attend(): call(attend_kernel, (groups,), [three, one, one], [pl.BlockSpec((1, rows,...  24.6 us
    pallas_call x1, Pallas kernels, middle_back(): call(middle_kernel, (rows // BLOCK,), [band] * 6 + head_specs(heads) + [w...  17 us
    pallas_call x1, Pallas kernels, project(): call(project_kernel, (KEY_VALUE_HEADS,), [whole((width, rows)), whole((ro...  16.8 us
  transfers between devices with their start and end apart: 72, of which 22 were waited for; matrix products, arithmetic and copies ran while one was open for 7% of the time, Pallas kernels for 54%

profile of v3, /device:TPU:0, one launch (start us, length us, event | category | flops | bytes accessed | tf_op | source)
XLA Modules:
  0.0 462.5 jit_solution(1548457842243546833)
XLA Ops:
  4.6 3.0 collective-permute-start.1
  8.5 2.2 constant_dynamic-slice_fusion.25
  10.7 8.3 %collective-permute-done.1.p0 = bf16[128,1920]{1,0:T(8,128)(2,1)} collective-permute-done((bf16[128,1920]{1,0:T(8,128)(2,1)S(1)}, bf16[128,1920]{1,0:T(8,128)(2,1)}, u32[]{:S(2)}, u32[]{:S(2)}) %collective-permute-start.1) | collective-permute-done | bytes 491552 | tf_op jit(solution)/shard_map/ppermute | solution.py:39
  19.0 1.8 collective-permute-start.2
  20.8 1.9 fusion.2
  22.7 1.6 collective-permute-start.5
  27.3 4.4 collective-permute-done.2.p1
  31.7 1.9 dynamic-slice_bitcast_fusion
  36.0 1.9 pad_maximum_fusion.4
  37.9 18.3 %collective-permute-done.8.p0 = bf16[128,960]{1,0:T(8,128)(2,1)S(1)} collective-permute-done((bf16[128,960]{1,0:T(8,128)(2,1)S(1)}, bf16[128,960]{1,0:T(8,128)(2,1)S(1)}, u32[]{:S(2)}, u32[]{:S(2)}) %collective-permute-start.8) | collective-permute-done | bytes 245792 | tf_op jit(solution)/shard_map/ppermute | solution.py:39
  59.8 2.7 collective-permute-done.9.p1
  65.1 16.8 %shard_map.203 = (bf16[960,1024]{1,0:T(8,128)(2,1)}, bf16[15,1024,128]{2,1,0:T(8,128)(2,1)}, bf16[5,1024,128]{2,1,0:T(8,128)(2,1)}, bf16[5,1024,128]{2,1,0:T(8,128)(2,1)}, bf16[960,1920]{1,0:T(8,128)(2,1)}) custom-call(s32[5]{0:T(128)} %stack.39.at_ref, bf16[960,1024]{1,0:T(8,128)(2,1)} %bitcast.59, s32[1024,1]{1,0:T(8,128)} %copy.32.doc_ref, ...), custom_call_target="tpu_custom_call" | custom-call | flops 3774873600 | bytes 20000000 | tf_op jit(solution)/shard_map/pallas_call | solution.py:267
  81.9 14.4 %shard_map.204 = (bf16[3,1024,192]{2,1,0:T(8,128)(2,1)}, bf16[9,1024,128]{2,1,0:T(8,128)(2,1)}) custom-call(bf16[15,1024,128]{2,1,0:T(8,128)(2,1)} %get-tuple-element.112.q_ref, bf16[5,1024,128]{2,1,0:T(8,128)(2,1)} %get-tuple-element.108.k_ref, bf16[5,1024,128]{2,1,0:T(8,128)(2,1)} %get-tuple-element.109.v_ref), custom_call_target="tpu_custom_call" | custom-call | flops 9663676416 | bytes 9000000 | tf_op jit(solution)/shard_map/pallas_call | solution.py:328
  97.1 10.2 %shard_map.205 = (bf16[2,1024,192]{2,1,0:T(8,128)(2,1)}, bf16[6,1024,128]{2,1,0:T(8,128)(2,1)}) custom-call(bf16[15,1024,128]{2,1,0:T(8,128)(2,1)} %get-tuple-element.112.q_ref, bf16[5,1024,128]{2,1,0:T(8,128)(2,1)} %get-tuple-element.108.k_ref, bf16[5,1024,128]{2,1,0:T(8,128)(2,1)} %get-tuple-element.109.v_ref), custom_call_target="tpu_custom_call" | custom-call | flops 6442450944 | bytes 6000000 | tf_op jit(solution)/shard_map/pallas_call | solution.py:328
  108.0 10.3 %shard_map.206 = (f32[1024,960]{1,0:T(8,128)}, bf16[1024,960]{1,0:T(8,128)(2,1)}, bf16[960,1024]{1,0:T(8,128)(2,1)}, bf16[1024,960]{1,0:T(8,128)(2,1)}) custom-call(s32[5]{0:T(128)} %stack.39.at_ref, bf16[960,1024]{1,0:T(8,128)(2,1)} %bitcast.60, bf16[960,1024]{1,0:T(8,128)(2,1)} %bitcast.56, bf16[3,1024,192]{2,1,0:T(8,128)(2,1)} %get-tuple-element.110.o0_ref, ...), custom_call_target="tpu_custom_call" | custom-call | flops 1887436800 | bytes 18000000 | tf_op jit(solution)/shard_map/pallas_call | solution.py:376
  119.3 42.3 %shard_map.207 = (f32[1024,960]{1,0:T(8,128)}, f32[1024,960]{1,0:T(8,128)}, bf16[960,1280]{1,0:T(8,128)(2,1)}, bf16[960,1280]{1,0:T(8,128)(2,1)}, bf16[2,960,640]{2,1,0:T(8,128)(2,1)}) custom-call(s32[5]{0:T(128)} %stack.44.at_ref, bf16[1024,960]{1,0:T(8,128)(2,1)} %get-tuple-element.123.in_ref, bf16[960,1024]{1,0:T(8,128)(2,1)} %get-tuple-element.119.flip_ref, ...), custom_call_target="tpu_custom_call" | custom-call | flops 22649241600 | bytes 30000000 | tf_op jit(solution)/shard_map/pallas_call | solution.py:462
  162.5 42.4 %shard_map.208 = (f32[1024,960]{1,0:T(8,128)}, f32[1024,960]{1,0:T(8,128)}, bf16[960,1280]{1,0:T(8,128)(2,1)}, bf16[960,1280]{1,0:T(8,128)(2,1)}, bf16[2,960,640]{2,1,0:T(8,128)(2,1)}) custom-call(s32[5]{0:T(128)} %stack.39.at_ref, bf16[1024,960]{1,0:T(8,128)(2,1)} %get-tuple-element.123.in_ref, bf16[960,1024]{1,0:T(8,128)(2,1)} %get-tuple-element.119.flip_ref, ...), custom_call_target="tpu_custom_call" | custom-call | flops 22649241600 | bytes 30000000 | tf_op jit(solution)/shard_map/pallas_call | solution.py:462
  204.9 2.4 fusion.1
  207.4 2.5 fusion
  209.9 2.3 add_convert_fusion
  218.6 1.6 collective-permute-start.25
  220.2 17.0 %shard_map.209 = (bf16[960,1024]{1,0:T(8,128)(2,1)}, f32[1024,960]{1,0:T(8,128)}, bf16[1024,960]{1,0:T(8,128)(2,1)}, bf16[15,1024,128]{2,1,0:T(8,128)(2,1)}, f32[1,960]{1,0:T(1,128)}) custom-call(s32[5]{0:T(128)} %stack.39.at_ref, f32[1024,960]{1,0:T(8,128)} %get-tuple-element.117.mid_ref, f32[1024,960]{1,0:T(8,128)} %get-tuple-element.121.y0_ref, ...), custom_call_target="tpu_custom_call" | custom-call | flops 1887436800 | bytes 30000000 | tf_op jit(solution)/shard_map/pallas_call | solution.py:534
  237.2 10.4 %shard_map.210.back_ref.refs_0_ = bf16[1,1024,384]{2,1,0:T(8,128)(2,1)} custom-call(bf16[9,1024,128]{2,1,0:T(8,128)(2,1)} %get-tuple-element.138.q_ref, bf16[5,1024,128]{2,1,0:T(8,128)(2,1)} %get-tuple-element.108.k_ref, bf16[5,1024,128]{2,1,0:T(8,128)(2,1)} %get-tuple-element.109.v_ref, bf16[15,1024,128]{2,1,0:T(8,128)(2,1)} %get-tuple-element.162.do_ref, ...), custom_call_target="tpu_custom_call" | custom-call | flops 8053063680 | bytes 3000000 | tf_op jit(solution)/shard_map/pallas_call | solution.py:605
  247.6 1.6 add_convert_fusion.2
  249.2 2.0 add_convert_fusion.4
  251.2 1.6 add_convert_fusion.3
  256.5 7.9 %shard_map.211 = bf16[960,1280]{1,0:T(8,128)(2,1)} custom-call(bf16[960,1024]{1,0:T(8,128)(2,1)} %get-tuple-element.134.flip_ref, bf16[1,1024,384]{2,1,0:T(8,128)(2,1)} %shard_map.210.back_ref.refs_0_, bf16[1024,960]{1,0:T(8,128)(2,1)} %get-tuple-element.144.branch_ref, bf16[3,1024,192]{2,1,0:T(8,128)(2,1)} %get-tuple-element.110.o0_ref, ...), custom_call_target="tpu_custom_call" | custom-call | flops 2516582400 | bytes 12000000 | tf_op jit(solution)/shard_map/pallas_call | solution.py:659
  265.9 10.7 %shard_map.212.refs_0_.refs_1_ = bf16[1,1024,384]{2,1,0:T(8,128)(2,1)} custom-call(bf16[9,1024,128]{2,1,0:T(8,128)(2,1)} %get-tuple-element.138.q_ref, bf16[5,1024,128]{2,1,0:T(8,128)(2,1)} %get-tuple-element.108.k_ref, bf16[5,1024,128]{2,1,0:T(8,128)(2,1)} %get-tuple-element.109.v_ref, bf16[15,1024,128]{2,1,0:T(8,128)(2,1)} %get-tuple-element.162.do_ref, ...), custom_call_target="tpu_custom_call" | custom-call | flops 8053063680 | bytes 3000000 | tf_op jit(solution)/shard_map/pallas_call | solution.py:605
  276.7 4.6 collective-permute-done.28
  283.3 1.6 collective-permute-start.33
  285.5 10.8 %shard_map.213.refs_1_.refs_2_ = bf16[1,1024,384]{2,1,0:T(8,128)(2,1)} custom-call(bf16[9,1024,128]{2,1,0:T(8,128)(2,1)} %get-tuple-element.138.q_ref, bf16[5,1024,128]{2,1,0:T(8,128)(2,1)} %get-tuple-element.108.k_ref, bf16[5,1024,128]{2,1,0:T(8,128)(2,1)} %get-tuple-element.109.v_ref, bf16[15,1024,128]{2,1,0:T(8,128)(2,1)} %get-tuple-element.162.do_ref, ...), custom_call_target="tpu_custom_call" | custom-call | flops 8053063680 | bytes 3000000 | tf_op jit(solution)/shard_map/pallas_call | solution.py:605
  296.7 1.8 collective-permute-done.34
  298.6 2.6 collective-permute-start.35
  301.3 5.0 %shard_map.214 = bf16[960,640]{1,0:T(8,128)(2,1)} custom-call(bf16[960,1024]{1,0:T(8,128)(2,1)} %get-tuple-element.134.flip_ref, bf16[1,1024,384]{2,1,0:T(8,128)(2,1)} %shard_map.212.refs_0_.refs_1_, bf16[1,1024,384]{2,1,0:T(8,128)(2,1)} %shard_map.213.refs_1_.refs_2_), custom_call_target="tpu_custom_call" | custom-call | flops 1258291200 | bytes 10000000 | tf_op jit(solution)/shard_map/pallas_call | solution.py:634
  308.4 2.6 collective-permute-start.49
  311.0 10.4 %shard_map.215.refs_0_.refs_3_ = bf16[1,1024,384]{2,1,0:T(8,128)(2,1)} custom-call(bf16[6,1024,128]{2,1,0:T(8,128)(2,1)} %get-tuple-element.155.q_ref, bf16[5,1024,128]{2,1,0:T(8,128)(2,1)} %get-tuple-element.108.k_ref, bf16[5,1024,128]{2,1,0:T(8,128)(2,1)} %get-tuple-element.109.v_ref, bf16[15,1024,128]{2,1,0:T(8,128)(2,1)} %get-tuple-element.162.do_ref, ...), custom_call_target="tpu_custom_call" | custom-call | flops 8053063680 | bytes 3000000 | tf_op jit(solution)/shard_map/pallas_call | solution.py:605
  321.4 2.3 collective-permute-done.37
  323.9 8.4 %collective-permute-done.39 = bf16[1,240,640]{2,1,0:T(8,128)(2,1)S(1)} collective-permute-done((bf16[1,240,640]{2,1,0:T(8,128)(2,1)S(1)}, bf16[1,240,640]{2,1,0:T(8,128)(2,1)S(1)}, u32[]{:S(2)}, u32[]{:S(2)}) %collective-permute-start.39) | collective-permute-done | bytes 307232 | tf_op jit(solution)/shard_map/ppermute | solution.py:35
  333.1 1.6 collective-permute-start.40
  335.3 10.6 %shard_map.216.refs_1_.refs_4_ = bf16[1,1024,384]{2,1,0:T(8,128)(2,1)} custom-call(bf16[6,1024,128]{2,1,0:T(8,128)(2,1)} %get-tuple-element.155.q_ref, bf16[5,1024,128]{2,1,0:T(8,128)(2,1)} %get-tuple-element.108.k_ref, bf16[5,1024,128]{2,1,0:T(8,128)(2,1)} %get-tuple-element.109.v_ref, bf16[15,1024,128]{2,1,0:T(8,128)(2,1)} %get-tuple-element.162.do_ref, ...), custom_call_target="tpu_custom_call" | custom-call | flops 8053063680 | bytes 3000000 | tf_op jit(solution)/shard_map/pallas_call | solution.py:605
  346.1 5.0 %shard_map.217 = bf16[960,640]{1,0:T(8,128)(2,1)} custom-call(bf16[960,1024]{1,0:T(8,128)(2,1)} %get-tuple-element.134.flip_ref, bf16[1,1024,384]{2,1,0:T(8,128)(2,1)} %shard_map.215.refs_0_.refs_3_, bf16[1,1024,384]{2,1,0:T(8,128)(2,1)} %shard_map.216.refs_1_.refs_4_), custom_call_target="tpu_custom_call" | custom-call | flops 1258291200 | bytes 10000000 | tf_op jit(solution)/shard_map/pallas_call | solution.py:634
  353.1 3.4 collective-permute-start.45
  358.9 5.3 %collective-permute-done.45 = bf16[1,120,640]{2,1,0:T(8,128)(2,1)S(1)} collective-permute-done((bf16[1,120,640]{2,1,0:T(8,128)(2,1)S(1)}, bf16[1,120,640]{2,1,0:T(8,128)(2,1)S(1)}, u32[]{:S(2)}, u32[]{:S(2)}) %collective-permute-start.45) | collective-permute-done | bytes 153632 | tf_op jit(solution)/shard_map/ppermute | solution.py:35
  364.3 2.5 collective-permute-done.47
  367.0 1.6 collective-permute-start.44
  369.3 12.1 %shard_map.218 = (bf16[960,1024]{1,0:T(8,128)(2,1)}, f32[1,960]{1,0:T(1,128)}) custom-call(bf16[960,1024]{1,0:T(8,128)(2,1)} %bitcast.61, f32[1024,960]{1,0:T(8,128)} %get-tuple-element.172.mid_ref, bf16[1,1024,384]{2,1,0:T(8,128)(2,1)} %shard_map.210.back_ref.refs_0_, bf16[1,1024,384]{2,1,0:T(8,128)(2,1)} %shard_map.212.refs_0_.refs_1_, ...), custom_call_target="tpu_custom_call" | custom-call | flops 3774873600 | bytes 14000000 | tf_op jit(solution)/shard_map/pallas_call | solution.py:693
  383.3 1.6 collective-permute-start.55
  384.8 2.0 collective-permute-start.62
  386.8 1.8 collective-permute-done.56
  389.4 5.8 %collective-permute-done.57 = bf16[1,240,640]{2,1,0:T(8,128)(2,1)S(1)} collective-permute-done((bf16[1,240,640]{2,1,0:T(8,128)(2,1)S(1)}, bf16[1,240,640]{2,1,0:T(8,128)(2,1)S(1)}, u32[]{:S(2)}, u32[]{:S(2)}) %collective-permute-start.57) | collective-permute-done | bytes 307232 | tf_op jit(solution)/shard_map/ppermute | solution.py:35
  396.4 5.2 %shard_map.219 = f32[480,2560]{1,0:T(8,128)} custom-call(s32[5]{0:T(128)} %stack.39.at_ref, bf16[4,240,640]{2,1,0:T(8,128)(2,1)} %copy-done.5, bf16[4,240,640]{2,1,0:T(8,128)(2,1)} %copy-done.11), custom_call_target="tpu_custom_call" | custom-call | bytes 10000000 | tf_op jit(solution)/shard_map/pallas_call | solution.py:734
  402.7 5.3 %collective-permute-done.62 = bf16[2,240,640]{2,1,0:T(8,128)(2,1)S(1)} collective-permute-done((bf16[2,240,640]{2,1,0:T(8,128)(2,1)S(1)}, bf16[2,240,640]{2,1,0:T(8,128)(2,1)S(1)}, u32[]{:S(2)}, u32[]{:S(2)}) %collective-permute-start.62) | collective-permute-done | bytes 614432 | tf_op jit(solution)/shard_map/ppermute | solution.py:35
  409.3 1.6 collective-permute-start.64
  410.9 5.7 %collective-permute-done.68 = bf16[2,240,640]{2,1,0:T(8,128)(2,1)S(1)} collective-permute-done((bf16[2,240,640]{2,1,0:T(8,128)(2,1)S(1)}, bf16[2,240,640]{2,1,0:T(8,128)(2,1)S(1)}, u32[]{:S(2)}, u32[]{:S(2)}) %collective-permute-start.68) | collective-permute-done | bytes 614432 | tf_op jit(solution)/shard_map/ppermute | solution.py:35
  418.3 2.3 collective-permute-done.52
  420.6 2.3 collective-permute-start.53
  422.9 2.2 collective-permute-done.53
  428.6 2.2 collective-permute-done.61
  430.9 5.2 %shard_map.220 = f32[480,2560]{1,0:T(8,128)} custom-call(s32[5]{0:T(128)} %stack.39.at_ref, bf16[4,240,640]{2,1,0:T(8,128)(2,1)} %copy-done.6, bf16[4,240,640]{2,1,0:T(8,128)(2,1)} %collective-permute-done.63.other_ref), custom_call_target="tpu_custom_call" | custom-call | bytes 10000000 | tf_op jit(solution)/shard_map/pallas_call | solution.py:734
  436.1 2.3 collective-permute-start.67
  438.9 5.0 %collective-permute-done.67 = bf16[1,120,640]{2,1,0:T(8,128)(2,1)S(1)} collective-permute-done((bf16[1,120,640]{2,1,0:T(8,128)(2,1)S(1)}, bf16[1,120,640]{2,1,0:T(8,128)(2,1)S(1)}, u32[]{:S(2)}, u32[]{:S(2)}) %collective-permute-start.67) | collective-permute-done | bytes 153632 | tf_op jit(solution)/shard_map/ppermute | solution.py:35
  443.9 5.2 %shard_map.221 = f32[960,1280]{1,0:T(8,128)} custom-call(s32[5]{0:T(128)} %stack.39.at_ref, bf16[4,240,640]{2,1,0:T(8,128)(2,1)} %copy-done.7, bf16[4,240,640]{2,1,0:T(8,128)(2,1)} %collective-permute-done.69.other_ref), custom_call_target="tpu_custom_call" | custom-call | bytes 10000000 | tf_op jit(solution)/shard_map/pallas_call | solution.py:734
  450.5 3.9 collective-permute-done.70
  456.8 5.4 %shard_map.222 = (f32[480,960]{1,0:T(8,128)}, f32[320,480]{1,0:T(8,128)}, f32[320,480]{1,0:T(8,128)}, f32[480,960]{1,0:T(8,128)}) custom-call(s32[5]{0:T(128)} %stack.39.at_ref, bf16[4,120,640]{2,1,0:T(8,128)(2,1)} %copy-done.10, bf16[4,120,640]{2,1,0:T(8,128)(2,1)} %copy-done.18, bf16[2,120,640]{2,1,0:T(8,128)(2,1)} %copy-done.16, ...), custom_call_target="tpu_custom_call" | custom-call | bytes 8000000 | tf_op jit(solution)/shard_map/pallas_call | solution.py:784
  (263 shorter events, 59.1 us)
Async XLA Ops:
  4.6 14.4 %collective-permute-start.1 = (bf16[128,1920]{1,0:T(8,128)(2,1)S(1)}, bf16[128,1920]{1,0:T(8,128)(2,1)}, u32[]{:S(2)}, u32[]{:S(2)}) collective-permute-start(bf16[128,1920]{1,0:T(8,128)(2,1)S(1)} %concatenate.57), channel_id=1, source_target_pairs={{0,1},{1,0},{2,3},{3,2},{4,5},{5,4},{6,7},{7,6},{8,9},{9,8},{10,11... | collective-permute-start | bytes 1474568 | tf_op jit(solution)/shard_map/ppermute | solution.py:39
  7.7 19.7 %collective-permute-start = (f32[2,480]{1,0:T(2,128)S(1)}, f32[2,480]{1,0:T(2,128)S(1)}, u32[]{:S(2)}, u32[]{:S(2)}) collective-permute-start(f32[2,480]{1,0:T(2,128)S(1)} %maximum_convert_fusion), channel_id=1, source_target_pairs={{0,1},{1,0},{2,3},{3,2},{4,5},{5,4},{6,7},{7,6},{8,9},{9,8},{10,11... | collective-permute-start | bytes 11528 | tf_op jit(solution)/shard_map/ppermute | solution.py:39
  19.0 12.7 %collective-permute-start.2 = (bf16[128,1920]{1,0:T(8,128)(2,1)}, bf16[128,1920]{1,0:T(8,128)(2,1)}, u32[]{:S(2)}, u32[]{:S(2)}) collective-permute-start(bf16[128,1920]{1,0:T(8,128)(2,1)} %collective-permute-done.1.p0), channel_id=1, source_target_pairs={{0,4},{2,6},{4,0},{6,2},{8,12},{10,14},{12,8},{14,10},{16,20},{18,... | collective-permute-start | bytes 1474568 | tf_op jit(solution)/shard_map/ppermute | solution.py:35
  22.7 39.8 %collective-permute-start.5 = (bf16[480,640]{1,0:T(8,128)(2,1)}, bf16[480,640]{1,0:T(8,128)(2,1)}, u32[]{:S(2)}, u32[]{:S(2)}) collective-permute-start(bf16[480,640]{1,0:T(8,128)(2,1)} %get-tuple-element.106), channel_id=1, source_target_pairs={{0,1},{1,0},{2,3},{3,2},{4,5},{5,4},{6,7},{7,6},{8,9},{9,8},{10,11... | collective-permute-start | bytes 1843208 | tf_op jit(solution)/shard_map/ppermute | solution.py:39
  24.2 38.8 %collective-permute-start.6 = (bf16[480,640]{1,0:T(8,128)(2,1)S(1)}, bf16[480,640]{1,0:T(8,128)(2,1)}, u32[]{:S(2)}, u32[]{:S(2)}) collective-permute-start(bf16[480,640]{1,0:T(8,128)(2,1)S(1)} %get-tuple-element.111), channel_id=1, source_target_pairs={{0,1},{1,0},{2,3},{3,2},{4,5},{5,4},{6,7},{7,6},{8,9},{9,8},{10,11... | collective-permute-start | bytes 1843208 | tf_op jit(solution)/shard_map/ppermute | solution.py:39
  25.8 30.4 %collective-permute-start.8 = (bf16[128,960]{1,0:T(8,128)(2,1)S(1)}, bf16[128,960]{1,0:T(8,128)(2,1)S(1)}, u32[]{:S(2)}, u32[]{:S(2)}) collective-permute-start(bf16[128,960]{1,0:T(8,128)(2,1)S(1)} %constant_dynamic-slice_fusion.24), channel_id=1, source_target_pairs={{0,1},{1,0},{2,3},{3,2},{4,5},{5,4},{6,7},{7,6},{8,9},{9,8},{10,11... | collective-permute-start | bytes 737288 | tf_op jit(solution)/shard_map/ppermute | solution.py:39
  27.3 31.1 %collective-permute-start.3 = (bf16[128,1920]{1,0:T(8,128)(2,1)}, bf16[128,1920]{1,0:T(8,128)(2,1)}, u32[]{:S(2)}, u32[]{:S(2)}) collective-permute-start(bf16[128,1920]{1,0:T(8,128)(2,1)} %collective-permute-done.1.p0), channel_id=1, source_target_pairs={{0,2},{2,0},{4,6},{6,4},{8,10},{10,8},{12,14},{14,12},{16,18},{18,... | collective-permute-start | bytes 1474568 | tf_op jit(solution)/shard_map/ppermute | solution.py:35
  31.7 31.9 %collective-permute-start.4 = (bf16[128,1920]{1,0:T(8,128)(2,1)}, bf16[128,1920]{1,0:T(8,128)(2,1)}, u32[]{:S(2)}, u32[]{:S(2)}) collective-permute-start(bf16[128,1920]{1,0:T(8,128)(2,1)} %collective-permute-done.2.p1), channel_id=1, source_target_pairs={{0,2},{2,0},{4,6},{6,4},{8,10},{10,8},{12,14},{14,12},{16,18},{18,... | collective-permute-start | bytes 1474568 | tf_op jit(solution)/shard_map/ppermute | solution.py:35
  56.2 6.4 %collective-permute-start.9 = (bf16[128,960]{1,0:T(8,128)(2,1)S(1)}, bf16[128,960]{1,0:T(8,128)(2,1)S(1)}, u32[]{:S(2)}, u32[]{:S(2)}) collective-permute-start(bf16[128,960]{1,0:T(8,128)(2,1)S(1)} %collective-permute-done.8.p0), channel_id=1, source_target_pairs={{0,4},{2,6},{4,0},{6,2},{8,12},{10,14},{12,8},{14,10},{16,20},{18,... | collective-permute-start | bytes 737288 | tf_op jit(solution)/shard_map/ppermute | solution.py:35
  58.4 38.0 %collective-permute-start.7 = (bf16[480,640]{1,0:T(8,128)(2,1)}, bf16[480,640]{1,0:T(8,128)(2,1)}, u32[]{:S(2)}, u32[]{:S(2)}) collective-permute-start(bf16[480,640]{1,0:T(8,128)(2,1)} %dynamic-slice_bitcast_fusion), channel_id=1, source_target_pairs={{0,1},{1,0},{2,3},{3,2},{4,5},{5,4},{6,7},{7,6},{8,9},{9,8},{10,11... | collective-permute-start | bytes 1843208 | tf_op jit(solution)/shard_map/ppermute | solution.py:39
  62.5 33.8 %collective-permute-start.10 = (bf16[128,960]{1,0:T(8,128)(2,1)S(1)}, bf16[128,960]{1,0:T(8,128)(2,1)S(1)}, u32[]{:S(2)}, u32[]{:S(2)}) collective-permute-start(bf16[128,960]{1,0:T(8,128)(2,1)S(1)} %collective-permute-done.8.p0), channel_id=1, source_target_pairs={{0,2},{2,0},{4,6},{6,4},{8,10},{10,8},{12,14},{14,12},{16,18},{18,... | collective-permute-start | bytes 737288 | tf_op jit(solution)/shard_map/ppermute | solution.py:35
  62.5 44.7 %collective-permute-start.11 = (bf16[128,960]{1,0:T(8,128)(2,1)S(1)}, bf16[128,960]{1,0:T(8,128)(2,1)S(1)}, u32[]{:S(2)}, u32[]{:S(2)}) collective-permute-start(bf16[128,960]{1,0:T(8,128)(2,1)S(1)} %collective-permute-done.9.p1), channel_id=1, source_target_pairs={{0,2},{2,0},{4,6},{6,4},{8,10},{10,8},{12,14},{14,12},{16,18},{18,... | collective-permute-start | bytes 737288 | tf_op jit(solution)/shard_map/ppermute | solution.py:35
  63.0 55.2 %collective-permute-start.12 = (bf16[480,640]{1,0:T(8,128)(2,1)}, bf16[480,640]{1,0:T(8,128)(2,1)}, u32[]{:S(2)}, u32[]{:S(2)}) collective-permute-start(bf16[480,640]{1,0:T(8,128)(2,1)} %collective-permute-done.5.g0), channel_id=1, source_target_pairs={{0,4},{2,6},{4,0},{6,2},{8,12},{10,14},{12,8},{14,10},{16,20},{18,... | collective-permute-start | bytes 1843208 | tf_op jit(solution)/shard_map/ppermute | solution.py:35
  63.6 54.8 %collective-permute-start.13 = (bf16[480,640]{1,0:T(8,128)(2,1)}, bf16[480,640]{1,0:T(8,128)(2,1)}, u32[]{:S(2)}, u32[]{:S(2)}) collective-permute-start(bf16[480,640]{1,0:T(8,128)(2,1)} %collective-permute-done.6.u0), channel_id=1, source_target_pairs={{0,4},{2,6},{4,0},{6,2},{8,12},{10,14},{12,8},{14,10},{16,20},{18,... | collective-permute-start | bytes 1843208 | tf_op jit(solution)/shard_map/ppermute | solution.py:35
  96.3 22.6 %collective-permute-start.15 = (bf16[480,640]{1,0:T(8,128)(2,1)}, bf16[480,640]{1,0:T(8,128)(2,1)S(1)}, u32[]{:S(2)}, u32[]{:S(2)}) collective-permute-start(bf16[480,640]{1,0:T(8,128)(2,1)} %collective-permute-done.5.g0), channel_id=1, source_target_pairs={{0,2},{2,0},{4,6},{6,4},{8,10},{10,8},{12,14},{14,12},{16,18},{18,... | collective-permute-start | bytes 1843208 | tf_op jit(solution)/shard_map/ppermute | solution.py:35
  96.4 22.4 %collective-permute-start.14 = (bf16[480,640]{1,0:T(8,128)(2,1)}, bf16[480,640]{1,0:T(8,128)(2,1)}, u32[]{:S(2)}, u32[]{:S(2)}) collective-permute-start(bf16[480,640]{1,0:T(8,128)(2,1)} %collective-permute-done.7.d0), channel_id=1, source_target_pairs={{0,4},{2,6},{4,0},{6,2},{8,12},{10,14},{12,8},{14,10},{16,20},{18,... | collective-permute-start | bytes 1843208 | tf_op jit(solution)/shard_map/ppermute | solution.py:35
  107.3 54.4 %collective-permute-start.17 = (bf16[480,640]{1,0:T(8,128)(2,1)}, bf16[480,640]{1,0:T(8,128)(2,1)S(1)}, u32[]{:S(2)}, u32[]{:S(2)}) collective-permute-start(bf16[480,640]{1,0:T(8,128)(2,1)} %collective-permute-done.6.u0), channel_id=1, source_target_pairs={{0,2},{2,0},{4,6},{6,4},{8,10},{10,8},{12,14},{14,12},{16,18},{18,... | collective-permute-start | bytes 1843208 | tf_op jit(solution)/shard_map/ppermute | solution.py:35
  118.2 43.7 %collective-permute-start.19 = (bf16[480,640]{1,0:T(8,128)(2,1)}, bf16[480,640]{1,0:T(8,128)(2,1)}, u32[]{:S(2)}, u32[]{:S(2)}) collective-permute-start(bf16[480,640]{1,0:T(8,128)(2,1)} %collective-permute-done.7.d0), channel_id=1, source_target_pairs={{0,2},{2,0},{4,6},{6,4},{8,10},{10,8},{12,14},{14,12},{16,18},{18,... | collective-permute-start | bytes 1843208 | tf_op jit(solution)/shard_map/ppermute | solution.py:35
  118.5 43.8 %collective-permute-start.16 = (bf16[480,640]{1,0:T(8,128)(2,1)}, bf16[480,640]{1,0:T(8,128)(2,1)}, u32[]{:S(2)}, u32[]{:S(2)}) collective-permute-start(bf16[480,640]{1,0:T(8,128)(2,1)} %collective-permute-done.12.g1), channel_id=1, source_target_pairs={{0,2},{2,0},{4,6},{6,4},{8,10},{10,8},{12,14},{14,12},{16,18},{18,... | collective-permute-start | bytes 1843208 | tf_op jit(solution)/shard_map/ppermute | solution.py:35
  118.8 43.6 %collective-permute-start.18 = (bf16[480,640]{1,0:T(8,128)(2,1)}, bf16[480,640]{1,0:T(8,128)(2,1)}, u32[]{:S(2)}, u32[]{:S(2)}) collective-permute-start(bf16[480,640]{1,0:T(8,128)(2,1)} %collective-permute-done.13.u1), channel_id=1, source_target_pairs={{0,2},{2,0},{4,6},{6,4},{8,10},{10,8},{12,14},{14,12},{16,18},{18,... | collective-permute-start | bytes 1843208 | tf_op jit(solution)/shard_map/ppermute | solution.py:35
  119.0 43.5 %collective-permute-start.20 = (bf16[480,640]{1,0:T(8,128)(2,1)}, bf16[480,640]{1,0:T(8,128)(2,1)}, u32[]{:S(2)}, u32[]{:S(2)}) collective-permute-start(bf16[480,640]{1,0:T(8,128)(2,1)} %collective-permute-done.14.d1), channel_id=1, source_target_pairs={{0,2},{2,0},{4,6},{6,4},{8,10},{10,8},{12,14},{14,12},{16,18},{18,... | collective-permute-start | bytes 1843208 | tf_op jit(solution)/shard_map/ppermute | solution.py:35
  161.7 43.3 %collective-permute-start.21 = (bf16[2,480,1280]{2,1,0:T(8,128)(2,1)}, bf16[2,480,1280]{2,1,0:T(8,128)(2,1)S(1)}, u32[]{:S(2)}, u32[]{:S(2)}) collective-permute-start(bf16[2,480,1280]{2,1,0:T(8,128)(2,1)} %bitcast.70), channel_id=1, source_target_pairs={{0,2},{2,0},{4,6},{6,4},{8,10},{10,8},{12,14},{14,12},{16,18},{18,... | collective-permute-start | bytes 7372808 | tf_op jit(solution)/shard_map/ppermute | solution.py:35
  161.9 45.5 %collective-permute-start.22 = (bf16[2,480,1280]{2,1,0:T(8,128)(2,1)}, bf16[2,480,1280]{2,1,0:T(8,128)(2,1)}, u32[]{:S(2)}, u32[]{:S(2)}) collective-permute-start(bf16[2,480,1280]{2,1,0:T(8,128)(2,1)} %bitcast.69), channel_id=1, source_target_pairs={{0,2},{2,0},{4,6},{6,4},{8,10},{10,8},{12,14},{14,12},{16,18},{18,... | collective-permute-start | bytes 7372808 | tf_op jit(solution)/shard_map/ppermute | solution.py:35
  162.3 47.6 %collective-permute-start.23 = (bf16[2,960,640]{2,1,0:T(8,128)(2,1)}, bf16[2,960,640]{2,1,0:T(8,128)(2,1)}, u32[]{:S(2)}, u32[]{:S(2)}) collective-permute-start(bf16[2,960,640]{2,1,0:T(8,128)(2,1)} %get-tuple-element.130), channel_id=1, source_target_pairs={{0,2},{2,0},{4,6},{6,4},{8,10},{10,8},{12,14},{14,12},{16,18},{18,... | collective-permute-start | bytes 7372808 | tf_op jit(solution)/shard_map/ppermute | solution.py:35
  213.4 34.2 %collective-permute-start.26 = (bf16[2,480,640]{2,1,0:T(8,128)(2,1)}, bf16[2,480,640]{2,1,0:T(8,128)(2,1)}, u32[]{:S(2)}, u32[]{:S(2)}) collective-permute-start(bf16[2,480,640]{2,1,0:T(8,128)(2,1)} %constant_dynamic-slice_fusion.21), channel_id=1, source_target_pairs={{0,4},{2,6},{4,0},{6,2},{8,12},{10,14},{12,8},{14,10},{16,20},{18,... | collective-permute-start | bytes 3686408 | tf_op jit(solution)/shard_map/ppermute | solution.py:35
  216.0 33.2 %collective-permute-start.24 = (bf16[1,480,1280]{2,1,0:T(8,128)(2,1)}, bf16[1,480,1280]{2,1,0:T(8,128)(2,1)}, u32[]{:S(2)}, u32[]{:S(2)}) collective-permute-start(bf16[1,480,1280]{2,1,0:T(8,128)(2,1)} %constant_dynamic-slice_fusion.23), channel_id=1, source_target_pairs={{0,1},{1,0},{2,3},{3,2},{4,5},{5,4},{6,7},{7,6},{8,9},{9,8},{10,11... | collective-permute-start | bytes 3686408 | tf_op jit(solution)/shard_map/ppermute | solution.py:39
  218.6 32.6 %collective-permute-start.25 = (bf16[2,240,1280]{2,1,0:T(8,128)(2,1)}, bf16[2,240,1280]{2,1,0:T(8,128)(2,1)}, u32[]{:S(2)}, u32[]{:S(2)}) collective-permute-start(bf16[2,240,1280]{2,1,0:T(8,128)(2,1)} %constant_dynamic-slice_fusion.22), channel_id=1, source_target_pairs={{0,8},{2,10},{4,12},{6,14},{8,0},{10,2},{12,4},{14,6},{16,24},{18,... | collective-permute-start | bytes 3686408 | tf_op jit(solution)/shard_map/ppermute | solution.py:35
  252.9 23.7 %collective-permute-start.27 = (bf16[1,480,640]{2,1,0:T(8,128)(2,1)S(1)}, bf16[1,480,640]{2,1,0:T(8,128)(2,1)S(1)}, u32[]{:S(2)}, u32[]{:S(2)}) collective-permute-start(bf16[1,480,640]{2,1,0:T(8,128)(2,1)S(1)} %constant_dynamic-slice_fusion.20), channel_id=1, source_target_pairs={{0,4},{2,6},{4,0},{6,2},{8,12},{10,14},{12,8},{14,10},{16,20},{18,... | collective-permute-start | bytes 1843208 | tf_op jit(solution)/shard_map/ppermute | solution.py:35
  254.4 27.0 %collective-permute-start.28 = (bf16[2,240,640]{2,1,0:T(8,128)(2,1)}, bf16[2,240,640]{2,1,0:T(8,128)(2,1)S(1)}, u32[]{:S(2)}, u32[]{:S(2)}) collective-permute-start(bf16[2,240,640]{2,1,0:T(8,128)(2,1)} %constant_dynamic-slice_fusion.19), channel_id=1, source_target_pairs={{0,4},{2,6},{4,0},{6,2},{8,12},{10,14},{12,8},{14,10},{16,20},{18,... | collective-permute-start | bytes 1843208 | tf_op jit(solution)/shard_map/ppermute | solution.py:35
  255.9 25.6 %collective-permute-start.29 = (bf16[1,480,640]{2,1,0:T(8,128)(2,1)S(1)}, bf16[1,480,640]{2,1,0:T(8,128)(2,1)S(1)}, u32[]{:S(2)}, u32[]{:S(2)}) collective-permute-start(bf16[1,480,640]{2,1,0:T(8,128)(2,1)S(1)} %constant_dynamic-slice_fusion.18), channel_id=1, source_target_pairs={{0,1},{1,0},{2,3},{3,2},{4,5},{5,4},{6,7},{7,6},{8,9},{9,8},{10,11... | collective-permute-start | bytes 1843208 | tf_op jit(solution)/shard_map/ppermute | solution.py:39
  265.8 15.8 %collective-permute-start.30 = (bf16[2,480,640]{2,1,0:T(8,128)(2,1)S(1)}, bf16[2,480,640]{2,1,0:T(8,128)(2,1)S(1)}, u32[]{:S(2)}, u32[]{:S(2)}) collective-permute-start(bf16[2,480,640]{2,1,0:T(8,128)(2,1)S(1)} %constant_dynamic-slice_fusion.17), channel_id=1, source_target_pairs={{0,2},{2,0},{4,6},{6,4},{8,10},{10,8},{12,14},{14,12},{16,18},{18,... | collective-permute-start | bytes 3686408 | tf_op jit(solution)/shard_map/ppermute | solution.py:35
  282.1 14.3 %collective-permute-start.31 = (bf16[1,240,640]{2,1,0:T(8,128)(2,1)S(1)}, bf16[1,240,640]{2,1,0:T(8,128)(2,1)S(1)}, u32[]{:S(2)}, u32[]{:S(2)}) collective-permute-start(bf16[1,240,640]{2,1,0:T(8,128)(2,1)S(1)} %constant_dynamic-slice_fusion.16), channel_id=1, source_target_pairs={{0,8},{2,10},{4,12},{6,14},{8,0},{10,2},{12,4},{14,6},{16,24},{18,... | collective-permute-start | bytes 921608 | tf_op jit(solution)/shard_map/ppermute | solution.py:35
  282.6 13.9 %collective-permute-start.32 = (bf16[1,240,640]{2,1,0:T(8,128)(2,1)S(1)}, bf16[1,240,640]{2,1,0:T(8,128)(2,1)S(1)}, u32[]{:S(2)}, u32[]{:S(2)}) collective-permute-start(bf16[1,240,640]{2,1,0:T(8,128)(2,1)S(1)} %constant_dynamic-slice_fusion.15), channel_id=1, source_target_pairs={{0,1},{1,0},{2,3},{3,2},{4,5},{5,4},{6,7},{7,6},{8,9},{9,8},{10,11... | collective-permute-start | bytes 921608 | tf_op jit(solution)/shard_map/ppermute | solution.py:39
  283.3 13.3 %collective-permute-start.33 = (bf16[1,240,640]{2,1,0:T(8,128)(2,1)S(1)}, bf16[1,240,640]{2,1,0:T(8,128)(2,1)S(1)}, u32[]{:S(2)}, u32[]{:S(2)}) collective-permute-start(bf16[1,240,640]{2,1,0:T(8,128)(2,1)S(1)} %constant_dynamic-slice_fusion.14), channel_id=1, source_target_pairs={{0,8},{2,10},{4,12},{6,14},{8,0},{10,2},{12,4},{14,6},{16,24},{18,... | collective-permute-start | bytes 921608 | tf_op jit(solution)/shard_map/ppermute | solution.py:35
  284.9 13.5 %collective-permute-start.34 = (bf16[2,240,640]{2,1,0:T(8,128)(2,1)S(1)}, bf16[2,240,640]{2,1,0:T(8,128)(2,1)S(1)}, u32[]{:S(2)}, u32[]{:S(2)}) collective-permute-start(bf16[2,240,640]{2,1,0:T(8,128)(2,1)S(1)} %constant_dynamic-slice_fusion.13), channel_id=1, source_target_pairs={{0,4},{2,6},{4,0},{6,2},{8,12},{10,14},{12,8},{14,10},{16,20},{18,... | collective-permute-start | bytes 1843208 | tf_op jit(solution)/shard_map/ppermute | solution.py:35
  298.6 25.2 %collective-permute-start.35 = (bf16[1,240,640]{2,1,0:T(8,128)(2,1)S(1)}, bf16[1,240,640]{2,1,0:T(8,128)(2,1)S(1)}, u32[]{:S(2)}, u32[]{:S(2)}) collective-permute-start(bf16[1,240,640]{2,1,0:T(8,128)(2,1)S(1)} %add_convert_fusion.19), channel_id=1, source_target_pairs={{0,16},{2,18},{4,20},{6,22},{8,24},{10,26},{12,28},{14,30},{16,0},... | collective-permute-start | bytes 921608 | tf_op jit(solution)/shard_map/ppermute | solution.py:35
  307.4 24.9 %collective-permute-start.36 = (bf16[2,240,640]{2,1,0:T(8,128)(2,1)S(1)}, bf16[2,240,640]{2,1,0:T(8,128)(2,1)S(1)}, u32[]{:S(2)}, u32[]{:S(2)}) collective-permute-start(bf16[2,240,640]{2,1,0:T(8,128)(2,1)S(1)} %constant_dynamic-slice_fusion.12), channel_id=1, source_target_pairs={{0,2},{2,0},{4,6},{6,4},{8,10},{10,8},{12,14},{14,12},{16,18},{18,... | collective-permute-start | bytes 1843208 | tf_op jit(solution)/shard_map/ppermute | solution.py:35
  307.5 16.1 %collective-permute-start.37 = (bf16[2,120,640]{2,1,0:T(8,128)(2,1)S(1)}, bf16[2,120,640]{2,1,0:T(8,128)(2,1)S(1)}, u32[]{:S(2)}, u32[]{:S(2)}) collective-permute-start(bf16[2,120,640]{2,1,0:T(8,128)(2,1)S(1)} %constant_dynamic-slice_fusion.11), channel_id=1, source_target_pairs={{0,8},{2,10},{4,12},{6,14},{8,0},{10,2},{12,4},{14,6},{16,24},{18,... | collective-permute-start | bytes 921608 | tf_op jit(solution)/shard_map/ppermute | solution.py:35
  308.1 24.2 %collective-permute-start.39 = (bf16[1,240,640]{2,1,0:T(8,128)(2,1)S(1)}, bf16[1,240,640]{2,1,0:T(8,128)(2,1)S(1)}, u32[]{:S(2)}, u32[]{:S(2)}) collective-permute-start(bf16[1,240,640]{2,1,0:T(8,128)(2,1)S(1)} %add_convert_fusion.18), channel_id=1, source_target_pairs={{0,16},{2,18},{4,20},{6,22},{8,24},{10,26},{12,28},{14,30},{16,0},... | collective-permute-start | bytes 921608 | tf_op jit(solution)/shard_map/ppermute | solution.py:35
  308.4 44.6 %collective-permute-start.49 = (bf16[1,240,640]{2,1,0:T(8,128)(2,1)S(1)}, bf16[1,240,640]{2,1,0:T(8,128)(2,1)S(1)}, u32[]{:S(2)}, u32[]{:S(2)}) collective-permute-start(bf16[1,240,640]{2,1,0:T(8,128)(2,1)S(1)} %add_convert_fusion.17), channel_id=1, source_target_pairs={{0,16},{2,18},{4,20},{6,22},{8,24},{10,26},{12,28},{14,30},{16,0},... | collective-permute-start | bytes 921608 | tf_op jit(solution)/shard_map/ppermute | solution.py:35
  332.5 13.4 %collective-permute-start.38 = (bf16[1,240,640]{2,1,0:T(8,128)(2,1)S(1)}, bf16[1,240,640]{2,1,0:T(8,128)(2,1)S(1)}, u32[]{:S(2)}, u32[]{:S(2)}) collective-permute-start(bf16[1,240,640]{2,1,0:T(8,128)(2,1)S(1)} %add_convert_fusion.16), channel_id=1, source_target_pairs={{0,8},{2,10},{4,12},{6,14},{8,0},{10,2},{12,4},{14,6},{16,24},{18,... | collective-permute-start | bytes 921608 | tf_op jit(solution)/shard_map/ppermute | solution.py:35
  333.1 12.8 %collective-permute-start.40 = (bf16[1,120,640]{2,1,0:T(8,128)(2,1)S(1)}, bf16[1,120,640]{2,1,0:T(8,128)(2,1)S(1)}, u32[]{:S(2)}, u32[]{:S(2)}) collective-permute-start(bf16[1,120,640]{2,1,0:T(8,128)(2,1)S(1)} %constant_dynamic-slice_fusion.10), channel_id=1, source_target_pairs={{0,1},{1,0},{2,3},{3,2},{4,5},{5,4},{6,7},{7,6},{8,9},{9,8},{10,11... | collective-permute-start | bytes 460808 | tf_op jit(solution)/shard_map/ppermute | solution.py:39
  334.7 11.4 %collective-permute-start.41 = (bf16[1,240,640]{2,1,0:T(8,128)(2,1)S(1)}, bf16[1,240,640]{2,1,0:T(8,128)(2,1)S(1)}, u32[]{:S(2)}, u32[]{:S(2)}) collective-permute-start(bf16[1,240,640]{2,1,0:T(8,128)(2,1)S(1)} %constant_dynamic-slice_fusion.9), channel_id=1, source_target_pairs={{0,1},{1,0},{2,3},{3,2},{4,5},{5,4},{6,7},{7,6},{8,9},{9,8},{10,11... | collective-permute-start | bytes 921608 | tf_op jit(solution)/shard_map/ppermute | solution.py:39
  352.3 14.5 %collective-permute-start.42 = (bf16[2,240,640]{2,1,0:T(8,128)(2,1)S(1)}, bf16[2,240,640]{2,1,0:T(8,128)(2,1)S(1)}, u32[]{:S(2)}, u32[]{:S(2)}) collective-permute-start(bf16[2,240,640]{2,1,0:T(8,128)(2,1)S(1)} %constant_dynamic-slice_fusion.8), channel_id=1, source_target_pairs={{0,2},{2,0},{4,6},{6,4},{8,10},{10,8},{12,14},{14,12},{16,18},{18,... | collective-permute-start | bytes 1843208 | tf_op jit(solution)/shard_map/ppermute | solution.py:35
  352.4 6.4 %collective-permute-start.43 = (bf16[1,120,640]{2,1,0:T(8,128)(2,1)S(1)}, bf16[1,120,640]{2,1,0:T(8,128)(2,1)S(1)}, u32[]{:S(2)}, u32[]{:S(2)}) collective-permute-start(bf16[1,120,640]{2,1,0:T(8,128)(2,1)S(1)} %constant_dynamic-slice_fusion.7), channel_id=1, source_target_pairs={{0,4},{2,6},{4,0},{6,2},{8,12},{10,14},{12,8},{14,10},{16,20},{18,... | collective-permute-start | bytes 460808 | tf_op jit(solution)/shard_map/ppermute | solution.py:35
  353.1 11.1 %collective-permute-start.45 = (bf16[1,120,640]{2,1,0:T(8,128)(2,1)S(1)}, bf16[1,120,640]{2,1,0:T(8,128)(2,1)S(1)}, u32[]{:S(2)}, u32[]{:S(2)}) collective-permute-start(bf16[1,120,640]{2,1,0:T(8,128)(2,1)S(1)} %add_convert_fusion.27), channel_id=1, source_target_pairs={{0,16},{2,18},{4,20},{6,22},{8,24},{10,26},{12,28},{14,30},{16,0},... | collective-permute-start | bytes 460808 | tf_op jit(solution)/shard_map/ppermute | solution.py:35
  356.6 10.1 %collective-permute-start.47 = (bf16[1,240,640]{2,1,0:T(8,128)(2,1)S(1)}, bf16[1,240,640]{2,1,0:T(8,128)(2,1)S(1)}, u32[]{:S(2)}, u32[]{:S(2)}) collective-permute-start(bf16[1,240,640]{2,1,0:T(8,128)(2,1)S(1)} %add_convert_fusion.14), channel_id=1, source_target_pairs={{0,4},{2,6},{4,0},{6,2},{8,12},{10,14},{12,8},{14,10},{16,20},{18,... | collective-permute-start | bytes 921608 | tf_op jit(solution)/shard_map/ppermute | solution.py:35
  358.1 23.3 %collective-permute-start.48 = (bf16[2,240,640]{2,1,0:T(8,128)(2,1)S(1)}, bf16[2,240,640]{2,1,0:T(8,128)(2,1)S(1)}, u32[]{:S(2)}, u32[]{:S(2)}) collective-permute-start(bf16[2,240,640]{2,1,0:T(8,128)(2,1)S(1)} %pad_maximum_fusion.1), channel_id=1, source_target_pairs={{0,4},{2,6},{4,0},{6,2},{8,12},{10,14},{12,8},{14,10},{16,20},{18,... | collective-permute-start | bytes 1843208 | tf_op jit(solution)/shard_map/ppermute | solution.py:35
  367.0 14.6 %collective-permute-start.44 = (bf16[1,240,640]{2,1,0:T(8,128)(2,1)S(1)}, bf16[1,240,640]{2,1,0:T(8,128)(2,1)S(1)}, u32[]{:S(2)}, u32[]{:S(2)}) collective-permute-start(bf16[1,240,640]{2,1,0:T(8,128)(2,1)S(1)} %constant_dynamic-slice_fusion.6), channel_id=1, source_target_pairs={{0,1},{1,0},{2,3},{3,2},{4,5},{5,4},{6,7},{7,6},{8,9},{9,8},{10,11... | collective-permute-start | bytes 921608 | tf_op jit(solution)/shard_map/ppermute | solution.py:39
  368.6 13.0 %collective-permute-start.46 = (bf16[1,120,640]{2,1,0:T(8,128)(2,1)S(1)}, bf16[1,120,640]{2,1,0:T(8,128)(2,1)S(1)}, u32[]{:S(2)}, u32[]{:S(2)}) collective-permute-start(bf16[1,120,640]{2,1,0:T(8,128)(2,1)S(1)} %add_convert_fusion.26), channel_id=1, source_target_pairs={{0,8},{2,10},{4,12},{6,14},{8,0},{10,2},{12,4},{14,6},{16,24},{18,... | collective-permute-start | bytes 460808 | tf_op jit(solution)/shard_map/ppermute | solution.py:35
  381.7 13.6 %collective-permute-start.58 = (bf16[4,240,640]{2,1,0:T(8,128)(2,1)S(1)}, bf16[4,240,640]{2,1,0:T(8,128)(2,1)S(1)}, u32[]{:S(2)}, u32[]{:S(2)}) collective-permute-start(bf16[4,240,640]{2,1,0:T(8,128)(2,1)S(1)} %pad_maximum_fusion.mine_ref), channel_id=1, source_target_pairs={{0,2},{2,0},{4,6},{6,4},{8,10},{10,8},{12,14},{14,12},{16,18},{18,... | collective-permute-start | bytes 3686408 | tf_op jit(solution)/shard_map/ppermute | solution.py:35
  381.8 6.8 %collective-permute-start.56 = (bf16[1,120,640]{2,1,0:T(8,128)(2,1)S(1)}, bf16[1,120,640]{2,1,0:T(8,128)(2,1)S(1)}, u32[]{:S(2)}, u32[]{:S(2)}) collective-permute-start(bf16[1,120,640]{2,1,0:T(8,128)(2,1)S(1)} %add_convert_fusion.25), channel_id=1, source_target_pairs={{0,8},{2,10},{4,12},{6,14},{8,0},{10,2},{12,4},{14,6},{16,24},{18,... | collective-permute-start | bytes 460808 | tf_op jit(solution)/shard_map/ppermute | solution.py:35
  384.8 10.4 %collective-permute-start.57 = (bf16[1,240,640]{2,1,0:T(8,128)(2,1)S(1)}, bf16[1,240,640]{2,1,0:T(8,128)(2,1)S(1)}, u32[]{:S(2)}, u32[]{:S(2)}) collective-permute-start(bf16[1,240,640]{2,1,0:T(8,128)(2,1)S(1)} %add_convert_fusion.11), channel_id=1, source_target_pairs={{0,8},{2,10},{4,12},{6,14},{8,0},{10,2},{12,4},{14,6},{16,24},{18,... | collective-permute-start | bytes 921608 | tf_op jit(solution)/shard_map/ppermute | solution.py:35
  384.8 23.1 %collective-permute-start.62 = (bf16[2,240,640]{2,1,0:T(8,128)(2,1)S(1)}, bf16[2,240,640]{2,1,0:T(8,128)(2,1)S(1)}, u32[]{:S(2)}, u32[]{:S(2)}) collective-permute-start(bf16[2,240,640]{2,1,0:T(8,128)(2,1)S(1)} %pad_maximum_fusion.2), channel_id=1, source_target_pairs={{0,8},{2,10},{4,12},{6,14},{8,0},{10,2},{12,4},{14,6},{16,24},{18,... | collective-permute-start | bytes 1843208 | tf_op jit(solution)/shard_map/ppermute | solution.py:35
  401.6 15.1 %collective-permute-start.68 = (bf16[2,240,640]{2,1,0:T(8,128)(2,1)S(1)}, bf16[2,240,640]{2,1,0:T(8,128)(2,1)S(1)}, u32[]{:S(2)}, u32[]{:S(2)}) collective-permute-start(bf16[2,240,640]{2,1,0:T(8,128)(2,1)S(1)} %pad_maximum_fusion.3), channel_id=1, source_target_pairs={{0,4},{2,6},{4,0},{6,2},{8,12},{10,14},{12,8},{14,10},{16,20},{18,... | collective-permute-start | bytes 1843208 | tf_op jit(solution)/shard_map/ppermute | solution.py:35
  408.0 22.9 %collective-permute-start.63 = (bf16[4,240,640]{2,1,0:T(8,128)(2,1)S(1)}, bf16[4,240,640]{2,1,0:T(8,128)(2,1)}, u32[]{:S(2)}, u32[]{:S(2)}) collective-permute-start(bf16[4,240,640]{2,1,0:T(8,128)(2,1)S(1)} %constant_dynamic-update-slice_fusion.2.mine_ref), channel_id=1, source_target_pairs={{0,2},{2,0},{4,6},{6,4},{8,10},{10,8},{12,14},{14,12},{16,18},{18,... | collective-permute-start | bytes 3686408 | tf_op jit(solution)/shard_map/ppermute | solution.py:35
  408.2 8.6 %collective-permute-start.51 = (f32[2,960]{1,0:T(2,128)S(1)}, f32[2,960]{1,0:T(2,128)S(1)}, u32[]{:S(2)}, u32[]{:S(2)}) collective-permute-start(f32[2,960]{1,0:T(2,128)S(1)} %fusion.5), channel_id=1, source_target_pairs={{0,4},{2,6},{4,0},{6,2},{8,12},{10,14},{12,8},{14,10},{16,20},{18,... | collective-permute-start | bytes 23048 | tf_op jit(solution)/shard_map/ppermute | solution.py:35
  409.3 17.7 %collective-permute-start.64 = (bf16[1,120,640]{2,1,0:T(8,128)(2,1)S(1)}, bf16[1,120,640]{2,1,0:T(8,128)(2,1)S(1)}, u32[]{:S(2)}, u32[]{:S(2)}) collective-permute-start(bf16[1,120,640]{2,1,0:T(8,128)(2,1)S(1)} %add_convert_fusion.24), channel_id=1, source_target_pairs={{0,16},{2,18},{4,20},{6,22},{8,24},{10,26},{12,28},{14,30},{16,0},... | collective-permute-start | bytes 460808 | tf_op jit(solution)/shard_map/ppermute | solution.py:35
  416.7 27.2 %collective-permute-start.69 = (bf16[4,240,640]{2,1,0:T(8,128)(2,1)S(1)}, bf16[4,240,640]{2,1,0:T(8,128)(2,1)}, u32[]{:S(2)}, u32[]{:S(2)}) collective-permute-start(bf16[4,240,640]{2,1,0:T(8,128)(2,1)S(1)} %constant_dynamic-update-slice_fusion.6.mine_ref), channel_id=1, source_target_pairs={{0,2},{2,0},{4,6},{6,4},{8,10},{10,8},{12,14},{14,12},{16,18},{18,... | collective-permute-start | bytes 3686408 | tf_op jit(solution)/shard_map/ppermute | solution.py:35
  425.1 29.3 %collective-permute-start.54 = (f32[2,960]{1,0:T(2,128)S(1)}, f32[2,960]{1,0:T(2,128)S(1)}, u32[]{:S(2)}, u32[]{:S(2)}) collective-permute-start(f32[2,960]{1,0:T(2,128)S(1)} %add.292), channel_id=1, source_target_pairs={{0,1},{1,0},{2,3},{3,2},{4,5},{5,4},{6,7},{7,6},{8,9},{9,8},{10,11... | collective-permute-start | bytes 23048 | tf_op jit(solution)/shard_map/ppermute | solution.py:39
  427.1 11.3 %collective-permute-start.59 = (bf16[2,120,640]{2,1,0:T(8,128)(2,1)S(1)}, bf16[2,120,640]{2,1,0:T(8,128)(2,1)S(1)}, u32[]{:S(2)}, u32[]{:S(2)}) collective-permute-start(bf16[2,120,640]{2,1,0:T(8,128)(2,1)S(1)} %pad_maximum_fusion.6), channel_id=1, source_target_pairs={{0,4},{2,6},{4,0},{6,2},{8,12},{10,14},{12,8},{14,10},{16,20},{18,... | collective-permute-start | bytes 921608 | tf_op jit(solution)/shard_map/ppermute | solution.py:35
  436.1 7.8 %collective-permute-start.67 = (bf16[1,120,640]{2,1,0:T(8,128)(2,1)S(1)}, bf16[1,120,640]{2,1,0:T(8,128)(2,1)S(1)}, u32[]{:S(2)}, u32[]{:S(2)}) collective-permute-start(bf16[1,120,640]{2,1,0:T(8,128)(2,1)S(1)} %add_convert_fusion.22), channel_id=1, source_target_pairs={{0,16},{2,18},{4,20},{6,22},{8,24},{10,26},{12,28},{14,30},{16,0},... | collective-permute-start | bytes 460808 | tf_op jit(solution)/shard_map/ppermute | solution.py:35
  438.4 16.7 %collective-permute-start.60 = (bf16[4,120,640]{2,1,0:T(8,128)(2,1)S(1)}, bf16[4,120,640]{2,1,0:T(8,128)(2,1)S(1)}, u32[]{:S(2)}, u32[]{:S(2)}) collective-permute-start(bf16[4,120,640]{2,1,0:T(8,128)(2,1)S(1)} %constant_dynamic-update-slice_fusion.near0), channel_id=1, source_target_pairs={{0,2},{2,0},{4,6},{6,4},{8,10},{10,8},{12,14},{14,12},{16,18},{18,... | collective-permute-start | bytes 1843208 | tf_op jit(solution)/shard_map/ppermute | solution.py:35
  438.5 11.8 %collective-permute-start.65 = (bf16[1,120,640]{2,1,0:T(8,128)(2,1)S(1)}, bf16[1,120,640]{2,1,0:T(8,128)(2,1)S(1)}, u32[]{:S(2)}, u32[]{:S(2)}) collective-permute-start(bf16[1,120,640]{2,1,0:T(8,128)(2,1)S(1)} %add_convert_fusion.21), channel_id=1, source_target_pairs={{0,4},{2,6},{4,0},{6,2},{8,12},{10,14},{12,8},{14,10},{16,20},{18,... | collective-permute-start | bytes 460808 | tf_op jit(solution)/shard_map/ppermute | solution.py:35
  (36 other events, 294.8 us)
